TPU v7x, 32 devices: a whole 2x2x4 slice. The times are simulated.
32 devices in a mesh: groups: 2 (over x), dp: 16 (over z, y, core).
Axes of the slice: x: 2, y: 2, z: 4, core: 2. Of those that a mesh axis runs over, the one named last changes fastest.
Arguments:
- acts: bfloat16 [1792, 8192], P(('groups', 'dp')), parts along dimension 0, may hold values from -6 to 6
- out_grad: bfloat16 [1792, 8192], P(('groups', 'dp')), parts along dimension 0, may hold values from -6 to 6
- gate_factor: bfloat16 [1792, 28672], P(('groups', 'dp')), parts along dimension 0, may hold values from -4 to 4
- down_weight: bfloat16 [28672, 8192], P('dp'), may hold values from -0.03125 to 0.03125
- proj_in: bfloat16 [64, 8192], replicated, may hold values from -0.0625 to 0.0625
- proj_out: bfloat16 [64, 28672], P(None, 'dp'), may hold values from -0.03125 to 0.03125
- lengths: int32 [32, 4], P(('groups', 'dp')), parts along dimension 0, may hold values from 1 to 28, 56 in all within a row
- queries: float32 [2048, 4096], P('dp'), may hold values from -4 to 4
Outputs:
- scores: float32 [128, 2048], P('groups', 'dp'), parts along dimension 0
There are 2 independent parts, one for each index of `groups`. A program takes and returns all parts, laid end to end along the dimension named above; an argument that names none is the same for every part. Nothing has to cross between parts.
Inputs may be any that keep to these rules, and one draw needn't show every extreme that they name: `lengths`: each row lists the token counts of the 4 examples of one block of 56 tokens, in order; each row sums to 56.
All inputs are finite; a program needn't handle non-finite values.
Results may differ from a plain program's by a relative error of at most 0.003.
Values may be sent and summed in bfloat16 or wider, within the bound.
No kernel may reach another device: no remote copies, remote signals or barrier semaphores. Data moves between devices by JAX's collectives and lax.ppermute only.
A program may use at most 128 MiB of HBM per device.

v0:
```python
import jax
import jax.numpy as jnp
from jax import lax
from jax.sharding import PartitionSpec as P


def contract_last(left, right):
    return lax.dot_general(
        left, right, (((1,), (1,)), ((), ())), preferred_element_type=jnp.float32
    )


def outer_sum(member, out_rows, in_rows):
    count = out_rows.shape[0]
    width = out_rows.shape[1]
    outer_rows = (out_rows[:, :, None] * in_rows[:, None, :]).reshape(count, width * width)
    return jnp.dot(member, outer_rows, precision=lax.Precision.HIGHEST)


def per_device(acts, out_grad, gate_factor, down_weight, proj_in, proj_out, lengths, queries):
    tok_rows = acts.shape[0]
    factor_local = lax.all_to_all(gate_factor, "dp", split_axis=1, concat_axis=0, tiled=True)
    hidden = contract_last(lax.all_gather(out_grad, "dp", axis=0, tiled=True), down_weight)
    hidden_grad = (hidden * factor_local.astype(jnp.float32)).astype(jnp.bfloat16)
    partial_proj = contract_last(hidden_grad, proj_out)
    in_proj = contract_last(acts, proj_in)
    own_proj = lax.psum_scatter(partial_proj, "dp", scatter_dimension=0, tiled=True)
    stop_at = jnp.cumsum(lengths[0])
    starts = stop_at - lengths[0]
    position = jnp.arange(tok_rows, dtype=jnp.int32)
    member = (
        (position[None, :] >= starts[:, None]) & (position[None, :] < stop_at[:, None])
    ).astype(jnp.float32)
    local_grads = outer_sum(member, own_proj, in_proj)
    grads = lax.all_gather(local_grads, "dp", axis=0, tiled=True)
    examples = grads.shape[0]
    gram = jnp.dot(grads, grads.T, precision=lax.Precision.HIGHEST)
    damping = 0.1 * jnp.trace(gram) / (examples * examples)
    system = gram / examples + damping * jnp.eye(examples, dtype=jnp.float32)
    against = lax.dot_general(
        grads,
        queries,
        (((1,), (1,)), ((), ())),
        precision=lax.Precision.HIGHEST,
        preferred_element_type=jnp.float32,
    )
    factor = jnp.linalg.cholesky(system)
    return jax.scipy.linalg.cho_solve((factor, True), against)


def solution(mesh):
    return jax.shard_map(
        per_device,
        mesh=mesh,
        in_specs=(
            P(("groups", "dp"), None),
            P(("groups", "dp"), None),
            P(("groups", "dp"), None),
            P("dp", None),
            P(),
            P(None, "dp"),
            P(("groups", "dp"), None),
            P("dp", None),
        ),
        out_specs=P("groups", "dp"),
        check_vma=False,
    )
```

profile of v0, /device:TPU:0, one launch (start us, length us, event | category | flops | bytes accessed | tf_op | source)
XLA Modules:
  0.0 341.1 jit_solution(2648880203408486094)
XLA Ops:
  6.5 0.7 all-gather.4.cloned.1.call-update
  7.3 3.8 %copy.21 = bf16[7,16,8,1792]{3,2,0,1:T(8,128)(2,1)} copy(bf16[7,16,8,1792]{3,2,1,0:T(8,128)(2,1)} %bitcast.45) | data formatting | bytes 6422528 | tf_op jit(solution)/shard_map/all_to_all | solution.py:22
  11.0 7.6 %all-to-all-start = ((bf16[56,16,1792]{2,0,1:T(8,128)(2,1)}), bf16[56,16,1792]{2,0,1:T(8,128)(2,1)}, u32[]{:S(2)}, u32[]{:S(2)}) async-start(bf16[56,16,1792]{2,0,1:T(8,128)(2,1)} %bitcast.44), calls=%async_computation | async-start | bytes 6422528 | tf_op jit(solution)/shard_map/all_to_all | solution.py:22
  18.6 0.0 reduce-scatter.4.cloned.1.call-start
  18.7 0.2 reduce-window.7
  18.8 89.8 %all-to-all-done = bf16[56,16,1792]{2,0,1:T(8,128)(2,1)} async-done(((bf16[56,16,1792]{2,0,1:T(8,128)(2,1)}), bf16[56,16,1792]{2,0,1:T(8,128)(2,1)}, u32[]{:S(2)}, u32[]{:S(2)}) %all-to-all-start) | async-done | bytes 3211296 | tf_op jit(solution)/shard_map/all_to_all | solution.py:22
  108.6 74.8 %all-gather.4.cloned.1.call-done = bf16[896,8192]{1,0:T(8,128)(2,1)} async-done(((bf16[56,8192]{1,0:T(8,128)(2,1)}), bf16[896,8192]{1,0:T(8,128)(2,1)}) %all-gather.4.cloned.1.call-update) | async-done | bytes 14680080 | tf_op jit(solution)/shard_map/all_gather | solution.py:23
  183.4 34.6 %fusion = bf16[896,1792]{1,0:T(8,128)(2,1)S(1)} fusion(bf16[896,8192]{1,0:T(8,128)(2,1)} %all-gather.4.cloned.1.call-done, bf16[1792,8192]{1,0:T(8,128)(2,1)} %param.11, bf16[56,16,1792]{2,0,1:T(8,128)(2,1)} %all-to-all-done), kind=kOutput, calls=%fused_computation.1 | convolution fusion | flops 26311491584 | bytes 50462720 | tf_op jit(solution)/shard_map/dot_general | solution.py:8
  218.0 0.0 copy-done.2
  218.0 0.0 copy-start.1
  218.0 1.7 fusion.12
  219.8 0.0 reduce-scatter.4.cloned.1.call-update
  219.8 0.2 all-gather.6.cloned.1.call-start
  220.1 1.6 fusion.13
  221.7 50.7 %reduce-scatter.4.cloned.1.call-done = f32[56,64]{1,0:T(8,128)} async-done(((f32[896,64]{1,0:T(8,128)}), f32[56,64]{1,0:T(8,128)}) %reduce-scatter.4.cloned.1.call-update) | async-done | bytes 14352
  272.4 2.5 broadcast_multiply_fusion
  274.9 2.1 mul.32
  277.0 1.0 convolution_bitcast_fusion
  278.0 0.0 all-gather.6.cloned.1.call-update
  278.0 37.1 %all-gather.6.cloned.1.call-done = f32[16,4,4096]{2,1,0:T(4,128)} async-done(((f32[1,4,4096]{2,1,0:T(4,128)}), f32[16,4,4096]{2,1,0:T(4,128)}) %all-gather.6.cloned.1.call-update) | async-done | bytes 1048592 | tf_op jit(solution)/shard_map/all_gather | solution.py:35
  315.2 1.6 reshape.56
  316.8 1.6 select_reduce_fusion.1
  318.3 0.1 copy.17
  318.4 0.1 copy.18
  319.2 5.8 %cholesky.17 = f32[64,64]{1,0:T(8,128)S(1)} custom-call(f32[64,64]{1,0:T(8,128)S(1)} %fusion.7), custom_call_target="Cholesky" | custom-call | tf_op jit(solution)/shard_map/jit(cholesky)/cholesky | solution.py:47
  325.1 0.6 compare_reduce_fusion
  325.7 0.7 fusion.1
  326.4 4.9 %custom-call.10 = f32[1,64,64]{1,2,0:T(8,128)S(1)} custom-call(f32[1,64,64]{2,1,0:T(8,128)S(1)} %fusion.1), custom_call_target="InvertDiagBlocksLowerTriangular" | custom-call | tf_op jit(solution)/shard_map/jit(_cho_solve)/triangular_solve | solution.py:48
  331.3 0.0 copy-done
  331.3 2.3 fusion.14
  333.6 0.2 fusion.4
  333.8 0.8 fusion.2
  (10 shorter events, 0.1 us)
Async XLA Ops:
  6.5 324.7 %copy-start = (f32[128,4096]{1,0:T(8,128)S(1)}, f32[128,4096]{1,0:T(8,128)}, u32[]{:S(2)}) copy-start(f32[128,4096]{1,0:T(8,128)} %param.15) | copy-start | bytes 6291460
  6.5 176.9 %all-gather.4.cloned.1.call-start = ((), (), s32[]{:S(2)}) async-start(), calls=%async_computation.2 | async-start | bytes 15597568 | tf_op jit(solution)/shard_map/all_gather | solution.py:23
  11.0 7.6 %copy-start.3 = (s32[1,4]{1,0:T(1,128)S(1)}, s32[1,4]{1,0:T(1,128)}, u32[]{:S(2)}) copy-start(s32[1,4]{1,0:T(1,128)} %param.14) | copy-start | bytes 52
  11.0 97.6 %all-to-all-start = ((bf16[56,16,1792]{2,0,1:T(8,128)(2,1)}), bf16[56,16,1792]{2,0,1:T(8,128)(2,1)}, u32[]{:S(2)}, u32[]{:S(2)}) async-start(bf16[56,16,1792]{2,0,1:T(8,128)(2,1)} %bitcast.44), calls=%async_computation | async-start | bytes 6422528 | tf_op jit(solution)/shard_map/all_to_all | solution.py:22
  18.6 253.8 %reduce-scatter.4.cloned.1.call-start = ((), (), s32[]{:S(2)}) async-start(), calls=%async_computation.4 | async-start | bytes 487424
  18.8 199.2 %copy-start.2 = (bf16[64,1792]{1,0:T(8,128)(2,1)S(1)}, bf16[64,1792]{1,0:T(8,128)(2,1)}, u32[]{:S(2)}) copy-start(bf16[64,1792]{1,0:T(8,128)(2,1)} %param.13) | copy-start | bytes 688132
  218.0 2.0 copy-start.1
  219.8 95.4 %all-gather.6.cloned.1.call-start = ((), (), s32[]{:S(2)}) async-start(), calls=%async_computation.3 | async-start | bytes 1114112 | tf_op jit(solution)/shard_map/all_gather | solution.py:35
Sparse Core Ops, SparseCore 0:
  9.7 173.6 all-gather.3
  219.9 52.3 reduce-scatter.3
  278.2 36.9 all-gather.5
where the time goes:
time: 341 us
  waiting for transfers between devices  253 us (74%)
  matrix products  43.9 us (13%)
  other arithmetic  14.8 us (4%)
  between operations  13.9 us (4%)
  starting transfers between devices  7.83 us (2%)
  local copies, waits for them, and re-layouts  7.58 us (2%)
    all_to_all x1, waiting for transfers between devices, per_device(): lax.all_to_all(gate_factor, 'dp', split_axis=1, concat_axis=0, tiled=True)  89.8 us
    all_gather x1, waiting for transfers between devices, per_device(): lax.all_gather(out_grad, 'dp', axis=0, tiled=True)  74.8 us
    unnamed x4, waiting for transfers between devices  51.4 us
    dot_general x3, matrix products, contract_last(): lax.dot_general(left, right, (((1,), (1,)), ((), ())), preferred_element_...  38 us
    all_gather x1, waiting for transfers between devices, per_device(): grads = lax.all_gather(local_grads, 'dp', axis=0, tiled=True)  37.1 us
    all_to_all x1, starting transfers between devices, per_device(): lax.all_to_all(gate_factor, 'dp', split_axis=1, concat_axis=0, tiled=True)  7.56 us
  transfers between devices with their start and end apart: 4, of which 4 were waited for; matrix products, arithmetic and copies ran while one was open for 2% of the time, Pallas kernels for 0%

commit v1 on v0

v1 whole, which is shorter than its diff:
```python
import functools

import jax
import jax.numpy as jnp
from jax import lax
from jax.experimental import pallas as pl
from jax.experimental.pallas import tpu as pltpu
from jax.sharding import PartitionSpec as P

AXIS = "dp"
HBM = pl.BlockSpec(memory_space=pl.ANY)
VMEM_LIMIT = 56 * 1024 * 1024


def contract_last(left, right):
    return lax.dot_general(
        left, right, (((1,), (1,)), ((), ())), preferred_element_type=jnp.float32
    )


def swap(block, bit, count):
    return lax.ppermute(block, AXIS, [(i, i ^ bit) for i in range(count)])


def line(block, pairs):
    return lax.ppermute(block, AXIS, [(4 * a + i, 4 * b + i) for a, b in pairs for i in range(4)])


def copies(pieces, shapes, *arrays):
    count = len(arrays)

    def body(*refs):
        ins, outs, sem = refs[:count], refs[count:-1], refs[-1]
        moves = pieces(lax.axis_index(AXIS), ins, outs)

        def each(act):
            for i, (when, src, dst) in enumerate(moves):
                move = pltpu.make_async_copy(src, dst, sem.at[i])
                if when is None:
                    act(move)
                else:
                    pl.when(when)(functools.partial(act, move))

        each(lambda move: move.start())
        each(lambda move: move.wait())

    total = sum(functools.reduce(lambda a, b: a * b, s) for s in shapes)
    return pl.pallas_call(
        body,
        out_shape=[jax.ShapeDtypeStruct(s, arrays[0].dtype) for s in shapes],
        in_specs=[HBM] * count,
        out_specs=[pl.BlockSpec(memory_space=pltpu.VMEM)] * len(shapes),
        scratch_shapes=[pltpu.SemaphoreType.DMA((32,))],
        cost_estimate=pl.CostEstimate(flops=0, bytes_accessed=total, transcendentals=0),
        name="copies",
    )(*arrays)


def either(first, second):
    def pieces(me, ins, outs):
        edge = (me < 4) | (me >= 12)
        lanes = first.shape[1] // 128
        number = next(n for n in (5, 4, 3, 2, 1) if lanes % n == 0)
        part = 128 * (lanes // number)
        cuts = [pl.ds(part * i, part) for i in range(number)]
        return [(edge, ins[0].at[:, cut], outs[0].at[:, cut]) for cut in cuts] + [
            (jnp.logical_not(edge), ins[1].at[:, cut], outs[0].at[:, cut]) for cut in cuts
        ]

    return copies(pieces, [first.shape], first, second)[0]


def fence(*arrays):
    def body(*refs):
        pass

    return pl.pallas_call(
        body,
        out_shape=[jax.ShapeDtypeStruct(a.shape, a.dtype) for a in arrays],
        in_specs=[HBM] * len(arrays),
        out_specs=[HBM] * len(arrays),
        input_output_aliases={i: i for i in range(len(arrays))},
        name="fence",
    )(*arrays)


def by_device(gate, count):
    rows, width = gate.shape[0], gate.shape[1] // count

    def pieces(me, ins, outs):
        return [(None, ins[0].at[:, pl.ds(i * width, width)], outs[0].at[i]) for i in range(count)]

    return copies(pieces, [(count, rows, width)], gate)[0]


def hidden_chunk(blocks, weight, tile=256):
    rows, wide = blocks[0].shape
    width, depth = weight.shape
    count = len(blocks)

    def body(*refs):
        ins, w, out, beside, stacked = refs[:count], *refs[count:]

        @pl.when(pl.program_id(0) == 0)
        def _():
            for i in range(count):
                stacked[64 * i : 64 * i + rows, :] = ins[i][:, :depth]
                beside[i, :rows] = ins[i][:, depth:].astype(jnp.float32)
                if rows < 64:
                    stacked[64 * i + rows : 64 * i + 64, :] = jnp.zeros((64 - rows, depth), stacked.dtype)
                    beside[i, rows:] = jnp.zeros((64 - rows, wide - depth), jnp.float32)

        out[...] = contract_last(stacked[...], w[...])

    return pl.pallas_call(
        body,
        grid=(width // tile,),
        out_shape=[
            jax.ShapeDtypeStruct((64 * count, width), jnp.float32),
            jax.ShapeDtypeStruct((count, 64, wide - depth), jnp.float32),
        ],
        in_specs=[pl.BlockSpec((rows, wide), lambda j: (0, 0), pipeline_mode=pl.Buffered(1))] * count
        + [pl.BlockSpec((tile, depth), lambda j: (j, 0))],
        out_specs=[
            pl.BlockSpec((64 * count, tile), lambda j: (0, j)),
            pl.BlockSpec((count, 64, wide - depth), lambda j: (0, 0, 0)),
        ],
        scratch_shapes=[pltpu.VMEM((64 * count, depth), jnp.bfloat16)],
        compiler_params=pltpu.CompilerParams(vmem_limit_bytes=VMEM_LIMIT),
        cost_estimate=pl.CostEstimate(flops=1, bytes_accessed=1, transcendentals=0),
        name="hidden_chunk",
    )(*blocks, weight)


def project(hiddens, gates, proj, lengths, tile=256):
    count, rows, width = gates.shape
    heads = proj.shape[0]
    slots = len(hiddens)

    def body(*refs):
        hs, g, p, spans, out, grads, total = refs[:slots], *refs[slots:]
        step = pl.program_id(0)
        me = lax.axis_index(AXIS)

        @pl.when(step == 0)
        def _():
            grads[...] = jnp.zeros_like(grads)
            total[...] = jnp.zeros_like(total)

        for m in range(slots):
            for r in range(4):
                gate = g[me ^ (4 * m + r)].astype(jnp.float32)
                at = 256 * m + 64 * r
                grads[at : at + rows, :] = (hs[m][64 * r : 64 * r + rows, :] * gate).astype(jnp.bfloat16)
        total[...] += contract_last(grads[...], p[...])

        @pl.when(step == pl.num_programs(0) - 1)
        def _():
            for r in range(4 * slots):
                block = total[64 * r : 64 * r + 64]
                if r == 0:
                    at = lax.broadcasted_iota(jnp.int32, block.shape, 0)
                    block = jnp.where(at == rows, spans[...], block)
                out[me ^ r] = jnp.concatenate([block[:32], block[32:]], axis=1)

    return pl.pallas_call(
        body,
        grid=(width // tile,),
        out_shape=jax.ShapeDtypeStruct((count, 32, 2 * heads), jnp.float32),
        in_specs=[pl.BlockSpec((256, tile), lambda j: (0, j))] * slots
        + [
            pl.BlockSpec((count, rows, tile), lambda j: (0, 0, j)),
            pl.BlockSpec((heads, tile), lambda j: (0, j)),
            pl.BlockSpec((1, heads), lambda j: (0, 0)),
        ],
        out_specs=pl.BlockSpec((count, 32, 2 * heads), lambda j: (0, 0, 0)),
        scratch_shapes=[pltpu.VMEM((256 * slots, tile), jnp.bfloat16), pltpu.VMEM((256 * slots, heads), jnp.float32)],
        compiler_params=pltpu.CompilerParams(vmem_limit_bytes=VMEM_LIMIT),
        cost_estimate=pl.CostEstimate(flops=1, bytes_accessed=1, transcendentals=0),
        name="project",
    )(*hiddens, gates, proj, lengths)


def partial_projection(rows, gate, weight, proj, lengths):
    pairs = [(0, 1), (1, 0), (2, 3), (3, 2)]
    middle = [(1, 2), (2, 1)]
    ends = [(1, 0), (2, 3)]

    def across(block):
        return swap(block, 2, 16)

    def core(block):
        return swap(block, 1, 16)

    near, mid, y0, c0 = line(rows, pairs), line(rows, middle), across(rows), core(rows)
    gates = by_device(gate, 16)
    near, mid, y0, c0, gates = fence(near, mid, y0, c0, gates)

    mid_far, out_mid, y1 = line(near, middle), line(mid, ends), across(near)
    c1, cy0 = core(near), core(y0)
    mid_far, out_mid, near, mid, y0, y1, c1, cy0, gates = fence(mid_far, out_mid, near, mid, y0, y1, c1, cy0, gates)

    gates = lax.all_to_all(gates, AXIS, split_axis=0, concat_axis=0, tiled=True)
    slot2 = either(out_mid, mid_far)
    out_far, y2 = line(mid_far, ends), across(slot2)
    c2, cy1 = core(slot2), core(y1)
    h0, i0 = hidden_chunk((rows, c0, y0, cy0), weight)
    out_far, mid, slot2, near, y1, c1, cy1, y2, c2, h0 = fence(out_far, mid, slot2, near, y1, c1, cy1, y2, c2, h0)

    slot3 = either(out_far, mid)
    y3 = across(slot3)
    c3, cy2 = core(slot3), core(y2)
    h1, i1 = hidden_chunk((near, c1, y1, cy1), weight)
    h2, i2 = hidden_chunk((slot2, c2, y2, cy2), weight)
    slot3, y3, c3, h1, h2 = fence(slot3, y3, c3, h1, h2)

    cy3 = core(y3)
    h3, i3 = hidden_chunk((slot3, c3, y3, cy3), weight)
    return project((h0, h1, h2, h3), gates, proj, lengths), jnp.concatenate([i0, i1, i2, i3], axis=0)


def eliminate(system, right):
    size = system.shape[0]
    at = lax.broadcasted_iota(jnp.int32, (size, 1), 0)
    for j in range(size):
        inverse = 1.0 / system[j : j + 1, j : j + 1]
        factor = jnp.where(at == j, 1.0 - inverse, system[:, j : j + 1] * inverse)
        system, right = system - factor * system[j : j + 1, :], right - factor * right[j : j + 1, :]
    return right


def finish(out_blocks, in_blocks, member, queries):
    count, _, heads = in_blocks.shape
    groups = count // 4
    examples = 4 * count
    wanted = queries.shape[0]
    exact = dict(precision=lax.Precision.HIGHEST, preferred_element_type=jnp.float32)

    def body(o, i, m, q, scores, left, double, both):
        both[:wanted, :] = q[...]
        double[...] = jnp.zeros_like(double)
        for g in range(groups):
            halves = [o[4 * g + r, :, part] for r in range(4) for part in (slice(heads), slice(heads, 2 * heads))]
            turned = jnp.concatenate(halves, axis=0).T
            inner = i[4 * g : 4 * g + 4].reshape(256, heads)
            double[:256, :heads] = inner
            double[256:, heads:] = inner
            mask = m[g]
            for p in range(heads // 2):
                left[16 * p : 16 * p + 16, :256] = mask * turned[2 * p : 2 * p + 1, :]
                left[16 * p : 16 * p + 16, 256:] = mask * turned[2 * p + 1 : 2 * p + 2, :]
            made = jnp.dot(left[...], double[...], **exact)
            for p in range(heads // 2):
                both[wanted + 16 * g : wanted + 16 * g + 16, 128 * p : 128 * p + 128] = made[16 * p : 16 * p + 16, :]
        grads = both[wanted:, :]
        products = lax.dot_general(grads, both[...], (((1,), (1,)), ((), ())), **exact)
        against, gram = products[:, :wanted], products[:, wanted:]
        row = lax.broadcasted_iota(jnp.int32, (examples, examples), 0)
        eye = (row == lax.broadcasted_iota(jnp.int32, (examples, examples), 1)).astype(jnp.float32)
        trace = jnp.sum(gram * eye, axis=(0, 1), keepdims=True)
        damping = 0.1 * trace / (examples * examples)
        scores[...] = eliminate(gram / examples + damping * eye, against)

    return pl.pallas_call(
        body,
        out_shape=jax.ShapeDtypeStruct((examples, wanted), jnp.float32),
        scratch_shapes=[
            pltpu.VMEM((8 * heads, 512), jnp.float32),
            pltpu.VMEM((512, 2 * heads), jnp.float32),
            pltpu.VMEM((wanted + examples, heads * heads), jnp.float32),
        ],
        compiler_params=pltpu.CompilerParams(vmem_limit_bytes=VMEM_LIMIT),
        name="finish",
    )(out_blocks, in_blocks, member, queries)


def reorder(blocks):
    return blocks[lax.axis_index(AXIS) ^ jnp.arange(blocks.shape[0])]


def in_place_order(beside, spans, rows):
    count = spans.shape[0]
    heads = beside.shape[2] // 2
    in_blocks = reorder(beside[:, :, :heads] + beside[:, :, heads:])
    stop_at = jnp.cumsum(spans, axis=1)
    position = jnp.arange(64, dtype=jnp.int32)
    inside = (position >= (stop_at - spans)[:, :, None]) & (position < stop_at[:, :, None])
    apart = jnp.eye(4, dtype=bool)[None, :, None, :, None] & inside.reshape(count // 4, 4, 4, 1, 64)
    return in_blocks, apart.astype(jnp.float32).reshape(count // 4, 16, 256)


def per_device(acts, out_grad, gate_factor, down_weight, proj_in, proj_out, lengths, queries):
    rows = acts.shape[0]
    count = gate_factor.shape[1] // down_weight.shape[0]
    heads = proj_in.shape[0]
    own = contract_last(acts, proj_in)
    high = lax.reduce_precision(own, 8, 7)
    low = (own - high).astype(jnp.bfloat16)
    sent = jnp.concatenate([out_grad, high.astype(jnp.bfloat16), low], axis=1)
    spans = jnp.pad(lengths.astype(jnp.float32), ((0, 0), (0, heads - 4)))
    if count == 16:
        partial, beside = partial_projection(sent, gate_factor, down_weight, proj_out, spans)
    else:
        sent = lax.all_gather(sent, AXIS, axis=0, tiled=True)
        factor = lax.all_to_all(gate_factor, AXIS, split_axis=1, concat_axis=0, tiled=True)
        hidden = contract_last(sent[:, : out_grad.shape[1]], down_weight)
        hidden_grad = (hidden * factor.astype(jnp.float32)).astype(jnp.bfloat16)
        partial = contract_last(hidden_grad, proj_out).reshape(count, rows, heads)
        partial = jnp.pad(partial, ((0, 0), (0, 64 - rows), (0, 0)))
        me = lax.axis_index(AXIS)
        partial = lax.dynamic_update_slice(partial, spans[None], (me, rows, 0))
        partial = jnp.concatenate([partial[:, :32], partial[:, 32:]], axis=2)
        beside = sent[:, out_grad.shape[1] :].astype(jnp.float32).reshape(count, rows, 2 * heads)
        beside = reorder(jnp.pad(beside, ((0, 0), (0, 64 - rows), (0, 0))))
    bit = 1
    while bit < count:
        partial = partial + swap(partial, bit, count)
        bit *= 2
    spans = partial[:, rows - 32, heads : heads + 4].astype(jnp.int32)
    in_blocks, member = in_place_order(beside, spans, rows)
    return finish(partial, in_blocks, member, queries)


def solution(mesh):
    return jax.shard_map(
        per_device,
        mesh=mesh,
        in_specs=(
            P(("groups", "dp"), None),
            P(("groups", "dp"), None),
            P(("groups", "dp"), None),
            P("dp", None),
            P(),
            P(None, "dp"),
            P(("groups", "dp"), None),
            P("dp", None),
        ),
        out_specs=P("groups", "dp"),
        check_vma=False,
    )
```

time: 341 us -> 266 us (0.78)
  waiting for transfers between devices: 253 us -> 124 us
  Pallas kernels: 0 us -> 102 us
  matrix products: 43.9 us -> 1.6 us
  starting transfers between devices: 7.83 us -> 21.9 us
  between operations: 13.9 us -> 0.33 us
  other arithmetic: 14.8 us -> 2.14 us
  local copies, waits for them, and re-layouts: 7.58 us -> 13.9 us
    ppermute x0 -> x21, waiting for transfers between devices: none -> 124 us  [the longest x16 77.6 us: swap(): return lax.ppermute(block, AXIS, [(i, i ^ bit) for i in range(count)])]
    all_gather x2 -> x0, waiting for transfers between devices: 112 us -> none  [the longest x1 74.8 us: per_device(): lax.all_gather(out_grad, 'dp', axis=0, tiled=True)]
    pallas_call x0 -> x13, Pallas kernels: none -> 102 us  [the longest x4 66.2 us: hidden_chunk(): pl.pallas_call(body, grid=(width // tile,), out_shape=[jax.ShapeDtypeStru...]
    all_to_all x1, waiting for transfers between devices: 89.8 us -> 0.01 us  [partial_projection(): gates = lax.all_to_all(gates, AXIS, split_axis=0, concat_axis=0, tiled=True)]
    unnamed x4 -> x0, waiting for transfers between devices: 51.4 us -> none
    dot_general x3 -> x1, matrix products: 38 us -> 1.6 us  [contract_last(): lax.dot_general(left, right, (((1,), (1,)), ((), ())), preferred_element_...]
    ppermute x0 -> x21, starting transfers between devices: none -> 17.4 us  [the longest x16 10.4 us: swap(): return lax.ppermute(block, AXIS, [(i, i ^ bit) for i in range(count)])]
    another operation x6 -> x1, other arithmetic: 12.2 us -> 0.01 us  [in_place_order(): stop_at = jnp.cumsum(spans, axis=1)]
  transfers between devices with their start and end apart: 4 -> 22, of which waited for: 4 -> 11; matrix products, arithmetic and copies ran while one was open for 2% -> 1% of each run, Pallas kernels for 0% -> 28%
where the time goes in v1:
time: 266 us; the launch traced here: 265 us
  waiting for transfers between devices  124 us (47%)
  Pallas kernels  102 us (38%)
  starting transfers between devices  21.9 us (8%)
  local copies, waits for them, and re-layouts  13.9 us (5%)
    ppermute x16, waiting for transfers between devices, swap(): return lax.ppermute(block, AXIS, [(i, i ^ bit) for i in range(count)])  77.6 us
    pallas_call x4, Pallas kernels, hidden_chunk(): pl.pallas_call(body, grid=(width // tile,), out_shape=[jax.ShapeDtypeStru...  66.2 us
    ppermute x5, waiting for transfers between devices, line(): lax.ppermute(block, AXIS, [(4 * a + i, 4 * b + i) for a, b in pairs for i...  46 us
    pallas_call x1, Pallas kernels, finish(): pl.pallas_call(body, out_shape=jax.ShapeDtypeStruct((examples, wanted), j...  18.9 us
    ppermute x16, starting transfers between devices, swap(): return lax.ppermute(block, AXIS, [(i, i ^ bit) for i in range(count)])  10.4 us
    unnamed x55, local copies, waits for them, and re-layouts  9.59 us
    pallas_call x3, Pallas kernels, copies(): pl.pallas_call(body, out_shape=[jax.ShapeDtypeStruct(s, arrays[0].dtype)...  8.97 us
    pallas_call x1, Pallas kernels, project(): pl.pallas_call(body, grid=(width // tile,), out_shape=jax.ShapeDtypeStruc...  7.77 us
  transfers between devices with their start and end apart: 22, of which 11 were waited for; matrix products, arithmetic and copies ran while one was open for 1% of the time, Pallas kernels for 28%

profile of v1, /device:TPU:0, one launch (start us, length us, event | category | flops | bytes accessed | tf_op | source)
XLA Modules:
  0.0 265.3 jit_solution(11753221300899894006)
XLA Ops:
  0.0 1.2 copy-done
  1.2 1.6 fusion.1
  2.8 1.8 concatenate.6.refs_0_
  4.6 3.0 %collective-permute-start = (bf16[56,8320]{1,0:T(8,128)(2,1)}, bf16[56,8320]{1,0:T(8,128)(2,1)S(1)}, u32[]{:S(2)}, u32[]{:S(2)}) collective-permute-start(bf16[56,8320]{1,0:T(8,128)(2,1)} %concatenate.6.refs_0_), channel_id=1, source_target_pairs={{0,4},{1,5},{2,6},{3,7},{4,0},{5,1},{6,2},{7,3},{8,12},{9,13},{10,... | collective-permute-start | bytes 2795528 | tf_op jit(solution)/shard_map/ppermute | solution.py:26
  8.3 1.6 collective-permute-start.2
  9.9 3.9 %copies.3.refs_4_ = bf16[16,56,1792]{2,1,0:T(8,128)(2,1)} custom-call(bf16[56,28672]{1,0:T(8,128)(2,1)} %refs_0_.1), custom_call_target="tpu_custom_call" | custom-call | bytes 1605632 | tf_op jit(solution)/shard_map/copies/pallas_call | solution.py:48
  13.8 14.7 %collective-permute-done.refs_0_ = bf16[56,8320]{1,0:T(8,128)(2,1)S(1)} collective-permute-done((bf16[56,8320]{1,0:T(8,128)(2,1)}, bf16[56,8320]{1,0:T(8,128)(2,1)S(1)}, u32[]{:S(2)}, u32[]{:S(2)}) %collective-permute-start) | collective-permute-done | bytes 931872 | tf_op jit(solution)/shard_map/ppermute | solution.py:26
  28.5 2.2 collective-permute-done.2.refs_2_
  32.4 1.6 collective-permute-start.6
  34.0 1.3 collective-permute-start.5
  35.9 18.0 %collective-permute-done.6.refs_5_ = bf16[56,8320]{1,0:T(8,128)(2,1)S(1)} collective-permute-done((bf16[56,8320]{1,0:T(8,128)(2,1)}, bf16[56,8320]{1,0:T(8,128)(2,1)S(1)}, u32[]{:S(2)}, u32[]{:S(2)}) %collective-permute-start.6) | collective-permute-done | bytes 931872 | tf_op jit(solution)/shard_map/ppermute | solution.py:22
  53.9 8.8 %collective-permute-done.5.refs_1_ = bf16[56,8320]{1,0:T(8,128)(2,1)S(1)} collective-permute-done((bf16[56,8320]{1,0:T(8,128)(2,1)}, bf16[56,8320]{1,0:T(8,128)(2,1)S(1)}, u32[]{:S(2)}, u32[]{:S(2)}) %collective-permute-start.5) | collective-permute-done | bytes 931872 | tf_op jit(solution)/shard_map/ppermute | solution.py:26
  64.6 4.5 %all-to-all-start = ((bf16[16,56,1792]{2,1,0:T(8,128)(2,1)}), bf16[16,56,1792]{2,1,0:T(8,128)(2,1)}, u32[]{:S(2)}, u32[]{:S(2)}) async-start(bf16[16,56,1792]{2,1,0:T(8,128)(2,1)} %get-tuple-element.74), calls=%async_computation | async-start | bytes 6422528 | tf_op jit(solution)/shard_map/all_to_all | solution.py:203
  69.1 2.6 copies.4.refs_2_
  71.7 1.8 collective-permute-start.11
  74.0 1.3 collective-permute-start.9
  75.3 16.5 %hidden_chunk.4 = (f32[256,1792]{1,0:T(8,128)}, f32[4,64,128]{2,1,0:T(8,128)}) custom-call(bf16[56,8320]{1,0:T(8,128)(2,1)} %concatenate.6.refs_0_, bf16[56,8320]{1,0:T(8,128)(2,1)} %get-tuple-element.52.refs_1_, bf16[56,8320]{1,0:T(8,128)(2,1)} %get-tuple-element.53.refs_2_, bf16[56,8320]{1,0:T(8,128)(2,1)} %get-tuple-element.54.refs_3_, ...), custom_call_target="tpu_custom_call" | custom-call | flops 1 | bytes 1 | tf_op jit(solution)/shard_map/hidden_chunk/pallas_call | solution.py:115
  91.8 28.3 %collective-permute-done.11.refs_7_ = bf16[56,8320]{1,0:T(8,128)(2,1)S(1)} collective-permute-done((bf16[56,8320]{1,0:T(8,128)(2,1)}, bf16[56,8320]{1,0:T(8,128)(2,1)S(1)}, u32[]{:S(2)}, u32[]{:S(2)}) %collective-permute-start.11) | collective-permute-done | bytes 931872 | tf_op jit(solution)/shard_map/ppermute | solution.py:22
  121.1 22.6 %collective-permute-done.9.refs_0_ = bf16[56,8320]{1,0:T(8,128)(2,1)S(1)} collective-permute-done((bf16[56,8320]{1,0:T(8,128)(2,1)}, bf16[56,8320]{1,0:T(8,128)(2,1)S(1)}, u32[]{:S(2)}, u32[]{:S(2)}) %collective-permute-start.9) | collective-permute-done | bytes 931872 | tf_op jit(solution)/shard_map/ppermute | solution.py:26
  144.7 2.5 copies.5.refs_0_
  147.2 1.7 collective-permute-start.13
  149.1 16.6 %hidden_chunk.5 = (f32[256,1792]{1,0:T(8,128)}, f32[4,64,128]{2,1,0:T(8,128)}) custom-call(bf16[56,8320]{1,0:T(8,128)(2,1)} %get-tuple-element.59.refs_0_, bf16[56,8320]{1,0:T(8,128)(2,1)} %get-tuple-element.60.refs_1_, bf16[56,8320]{1,0:T(8,128)(2,1)} %get-tuple-element.61.refs_2_, bf16[56,8320]{1,0:T(8,128)(2,1)} %get-tuple-element.62.refs_3_, ...), custom_call_target="tpu_custom_call" | custom-call | flops 1 | bytes 1 | tf_op jit(solution)/shard_map/hidden_chunk/pallas_call | solution.py:115
  166.5 16.5 %hidden_chunk.6 = (f32[256,1792]{1,0:T(8,128)}, f32[4,64,128]{2,1,0:T(8,128)}) custom-call(bf16[56,8320]{1,0:T(8,128)(2,1)} %get-tuple-element.64.refs_0_, bf16[56,8320]{1,0:T(8,128)(2,1)} %get-tuple-element.65.refs_1_, bf16[56,8320]{1,0:T(8,128)(2,1)} %get-tuple-element.66.refs_2_, bf16[56,8320]{1,0:T(8,128)(2,1)} %copy-done.18, bf16[1792,8192]{1,0:T(8,128)(2,1)} %refs_4_.7), custom_call_target="tpu_custom_call" | custom-call | flops 1 | bytes 1 | tf_op jit(solution)/shard_map/hidden_chunk/pallas_call | solution.py:115
  185.6 1.5 collective-permute-done.16.refs_3_
  188.0 16.6 %hidden_chunk.7 = (f32[256,1792]{1,0:T(8,128)}, f32[4,64,128]{2,1,0:T(8,128)}) custom-call(bf16[56,8320]{1,0:T(8,128)(2,1)} %get-tuple-element.70.refs_0_, bf16[56,8320]{1,0:T(8,128)(2,1)} %get-tuple-element.71.refs_1_, bf16[56,8320]{1,0:T(8,128)(2,1)} %get-tuple-element.72.refs_2_, bf16[56,8320]{1,0:T(8,128)(2,1)} %copy-done.19, bf16[1792,8192]{1,0:T(8,128)(2,1)} %refs_4_.7), custom_call_target="tpu_custom_call" | custom-call | flops 1 | bytes 1 | tf_op jit(solution)/shard_map/hidden_chunk/pallas_call | solution.py:115
  204.6 7.8 %project.1 = f32[16,32,128]{2,1,0:T(8,128)} custom-call(f32[256,1792]{1,0:T(8,128)} %get-tuple-element.56.refs_0_, f32[256,1792]{1,0:T(8,128)} %get-tuple-element.68.refs_1_, f32[256,1792]{1,0:T(8,128)} %get-tuple-element.69.refs_2_, f32[256,1792]{1,0:T(8,128)} %get-tuple-element.73.refs_3_, bf16[16,56,1792]{2,1,0:T(8,128)(2,1)} %all-to-all-done.refs_4_, ...), custom_call_target="tpu_custom_call" | custom-call | flops 1 | bytes 1 | tf_op jit(solution)/shard_map/project/pallas_call | solution.py:166
  212.8 1.4 collective-permute-done.17
  215.9 7.9 %collective-permute-done.18 = f32[16,32,128]{2,1,0:T(8,128)S(1)} collective-permute-done((f32[16,32,128]{2,1,0:T(8,128)S(1)}, f32[16,32,128]{2,1,0:T(8,128)S(1)}, u32[]{:S(2)}, u32[]{:S(2)}) %collective-permute-start.18) | collective-permute-done | bytes 262176 | tf_op jit(solution)/shard_map/ppermute | solution.py:22
  224.0 7.6 %collective-permute-done.19 = f32[16,32,128]{2,1,0:T(8,128)S(1)} collective-permute-done((f32[16,32,128]{2,1,0:T(8,128)S(1)}, f32[16,32,128]{2,1,0:T(8,128)S(1)}, u32[]{:S(2)}, u32[]{:S(2)}) %collective-permute-start.19) | collective-permute-done | bytes 262176 | tf_op jit(solution)/shard_map/ppermute | solution.py:22
  233.0 1.4 gather_fusion
  234.4 10.6 %collective-permute-done.20 = f32[16,32,128]{2,1,0:T(8,128)S(1)} collective-permute-done((f32[16,32,128]{2,1,0:T(8,128)S(1)}, f32[16,32,128]{2,1,0:T(8,128)S(1)}, u32[]{:S(2)}, u32[]{:S(2)}) %collective-permute-start.20) | collective-permute-done | bytes 262176 | tf_op jit(solution)/shard_map/ppermute | solution.py:22
  246.4 18.9 %finish.1 = f32[64,128]{1,0:T(8,128)} custom-call(f32[16,32,128]{2,1,0:T(8,128)} %copy-done.17, f32[16,64,64]{2,1,0:T(8,128)} %gather_fusion, f32[4,16,256]{2,1,0:T(8,128)} %and_convert_fusion.m, f32[128,4096]{1,0:T(8,128)} %q.1), custom_call_target="tpu_custom_call" | custom-call | tf_op jit(solution)/shard_map/finish/pallas_call | solution.py:264
  (106 shorter events, 16.9 us)
Async XLA Ops:
  4.6 23.9 %collective-permute-start = (bf16[56,8320]{1,0:T(8,128)(2,1)}, bf16[56,8320]{1,0:T(8,128)(2,1)S(1)}, u32[]{:S(2)}, u32[]{:S(2)}) collective-permute-start(bf16[56,8320]{1,0:T(8,128)(2,1)} %concatenate.6.refs_0_), channel_id=1, source_target_pairs={{0,4},{1,5},{2,6},{3,7},{4,0},{5,1},{6,2},{7,3},{8,12},{9,13},{10,... | collective-permute-start | bytes 2795528 | tf_op jit(solution)/shard_map/ppermute | solution.py:26
  7.6 20.9 %collective-permute-start.1 = (bf16[56,8320]{1,0:T(8,128)(2,1)}, bf16[56,8320]{1,0:T(8,128)(2,1)S(1)}, u32[]{:S(2)}, u32[]{:S(2)}) collective-permute-start(bf16[56,8320]{1,0:T(8,128)(2,1)} %concatenate.6.refs_0_), channel_id=1, source_target_pairs={{4,8},{5,9},{6,10},{7,11},{8,4},{9,5},{10,6},{11,7},{20,24},{21,25... | collective-permute-start | bytes 2795528 | tf_op jit(solution)/shard_map/ppermute | solution.py:26
  8.3 22.4 %collective-permute-start.2 = (bf16[56,8320]{1,0:T(8,128)(2,1)}, bf16[56,8320]{1,0:T(8,128)(2,1)S(1)}, u32[]{:S(2)}, u32[]{:S(2)}) collective-permute-start(bf16[56,8320]{1,0:T(8,128)(2,1)} %concatenate.6.refs_0_), channel_id=1, source_target_pairs={{0,2},{1,3},{2,0},{3,1},{4,6},{5,7},{6,4},{7,5},{8,10},{9,11},{10,... | collective-permute-start | bytes 2795528 | tf_op jit(solution)/shard_map/ppermute | solution.py:22
  9.9 20.8 %collective-permute-start.3 = (bf16[56,8320]{1,0:T(8,128)(2,1)}, bf16[56,8320]{1,0:T(8,128)(2,1)}, u32[]{:S(2)}, u32[]{:S(2)}) collective-permute-start(bf16[56,8320]{1,0:T(8,128)(2,1)} %concatenate.6.refs_0_), channel_id=1, source_target_pairs={{0,1},{1,0},{2,3},{3,2},{4,5},{5,4},{6,7},{7,6},{8,9},{9,8},{10,11... | collective-permute-start | bytes 2795528 | tf_op jit(solution)/shard_map/ppermute | solution.py:22
  31.7 4.2 %collective-permute-start.4 = (bf16[56,8320]{1,0:T(8,128)(2,1)}, bf16[56,8320]{1,0:T(8,128)(2,1)S(1)}, u32[]{:S(2)}, u32[]{:S(2)}) collective-permute-start(bf16[56,8320]{1,0:T(8,128)(2,1)} %get-tuple-element.42.refs_2_), channel_id=1, source_target_pairs={{4,8},{5,9},{6,10},{7,11},{8,4},{9,5},{10,6},{11,7},{20,24},{21,25... | collective-permute-start | bytes 2795528 | tf_op jit(solution)/shard_map/ppermute | solution.py:26
  32.4 21.5 %collective-permute-start.6 = (bf16[56,8320]{1,0:T(8,128)(2,1)}, bf16[56,8320]{1,0:T(8,128)(2,1)S(1)}, u32[]{:S(2)}, u32[]{:S(2)}) collective-permute-start(bf16[56,8320]{1,0:T(8,128)(2,1)} %get-tuple-element.42.refs_2_), channel_id=1, source_target_pairs={{0,2},{1,3},{2,0},{3,1},{4,6},{5,7},{6,4},{7,5},{8,10},{9,11},{10,... | collective-permute-start | bytes 2795528 | tf_op jit(solution)/shard_map/ppermute | solution.py:22
  34.0 19.9 %collective-permute-start.7 = (bf16[56,8320]{1,0:T(8,128)(2,1)}, bf16[56,8320]{1,0:T(8,128)(2,1)S(1)}, u32[]{:S(2)}, u32[]{:S(2)}) collective-permute-start(bf16[56,8320]{1,0:T(8,128)(2,1)} %get-tuple-element.42.refs_2_), channel_id=1, source_target_pairs={{0,1},{1,0},{2,3},{3,2},{4,5},{5,4},{6,7},{7,6},{8,9},{9,8},{10,11... | collective-permute-start | bytes 2795528 | tf_op jit(solution)/shard_map/ppermute | solution.py:22
  34.0 28.7 %collective-permute-start.5 = (bf16[56,8320]{1,0:T(8,128)(2,1)}, bf16[56,8320]{1,0:T(8,128)(2,1)S(1)}, u32[]{:S(2)}, u32[]{:S(2)}) collective-permute-start(bf16[56,8320]{1,0:T(8,128)(2,1)} %get-tuple-element.43.refs_3_), channel_id=1, source_target_pairs={{4,0},{5,1},{6,2},{7,3},{8,12},{9,13},{10,14},{11,15},{20,16},{21,... | collective-permute-start | bytes 2795528 | tf_op jit(solution)/shard_map/ppermute | solution.py:26
  35.3 27.4 %collective-permute-start.8 = (bf16[56,8320]{1,0:T(8,128)(2,1)}, bf16[56,8320]{1,0:T(8,128)(2,1)S(1)}, u32[]{:S(2)}, u32[]{:S(2)}) collective-permute-start(bf16[56,8320]{1,0:T(8,128)(2,1)} %get-tuple-element.44.refs_4_), channel_id=1, source_target_pairs={{0,1},{1,0},{2,3},{3,2},{4,5},{5,4},{6,7},{7,6},{8,9},{9,8},{10,11... | collective-permute-start | bytes 2795528 | tf_op jit(solution)/shard_map/ppermute | solution.py:22
  35.9 26.8 %copy-start.14 = (bf16[56,8320]{1,0:T(8,128)(2,1)}, bf16[56,8320]{1,0:T(8,128)(2,1)S(1)}, u32[]{:S(2)}) copy-start(bf16[56,8320]{1,0:T(8,128)(2,1)S(1)} %collective-permute-done.4.refs_0_) | copy-start | bytes 2795524
  53.9 9.7 %copy-start.4 = (bf16[56,8320]{1,0:T(8,128)(2,1)}, bf16[56,8320]{1,0:T(8,128)(2,1)S(1)}, u32[]{:S(2)}) copy-start(bf16[56,8320]{1,0:T(8,128)(2,1)S(1)} %collective-permute-done.6.refs_5_) | copy-start | bytes 2795524
  53.9 9.7 %copy-start.6 = (bf16[56,8320]{1,0:T(8,128)(2,1)}, bf16[56,8320]{1,0:T(8,128)(2,1)S(1)}, u32[]{:S(2)}) copy-start(bf16[56,8320]{1,0:T(8,128)(2,1)S(1)} %collective-permute-done.7.refs_6_) | copy-start | bytes 2795524
  64.6 140.0 %all-to-all-start = ((bf16[16,56,1792]{2,1,0:T(8,128)(2,1)}), bf16[16,56,1792]{2,1,0:T(8,128)(2,1)}, u32[]{:S(2)}, u32[]{:S(2)}) async-start(bf16[16,56,1792]{2,1,0:T(8,128)(2,1)} %get-tuple-element.74), calls=%async_computation | async-start | bytes 6422528 | tf_op jit(solution)/shard_map/all_to_all | solution.py:203
  71.7 48.4 %collective-permute-start.11 = (bf16[56,8320]{1,0:T(8,128)(2,1)}, bf16[56,8320]{1,0:T(8,128)(2,1)S(1)}, u32[]{:S(2)}, u32[]{:S(2)}) collective-permute-start(bf16[56,8320]{1,0:T(8,128)(2,1)} %copies.4.refs_2_), channel_id=1, source_target_pairs={{0,2},{1,3},{2,0},{3,1},{4,6},{5,7},{6,4},{7,5},{8,10},{9,11},{10,... | collective-permute-start | bytes 2795528 | tf_op jit(solution)/shard_map/ppermute | solution.py:22
  73.5 46.6 %collective-permute-start.12 = (bf16[56,8320]{1,0:T(8,128)(2,1)}, bf16[56,8320]{1,0:T(8,128)(2,1)S(1)}, u32[]{:S(2)}, u32[]{:S(2)}) collective-permute-start(bf16[56,8320]{1,0:T(8,128)(2,1)} %copies.4.refs_2_), channel_id=1, source_target_pairs={{0,1},{1,0},{2,3},{3,2},{4,5},{5,4},{6,7},{7,6},{8,9},{9,8},{10,11... | collective-permute-start | bytes 2795528 | tf_op jit(solution)/shard_map/ppermute | solution.py:22
  73.5 46.6 %collective-permute-start.10 = (bf16[56,8320]{1,0:T(8,128)(2,1)S(1)}, bf16[56,8320]{1,0:T(8,128)(2,1)S(1)}, u32[]{:S(2)}, u32[]{:S(2)}) collective-permute-start(bf16[56,8320]{1,0:T(8,128)(2,1)S(1)} %copy-done.5), channel_id=1, source_target_pairs={{0,1},{1,0},{2,3},{3,2},{4,5},{5,4},{6,7},{7,6},{8,9},{9,8},{10,11... | collective-permute-start | bytes 2795528 | tf_op jit(solution)/shard_map/ppermute | solution.py:22
  74.0 69.7 %collective-permute-start.9 = (bf16[56,8320]{1,0:T(8,128)(2,1)}, bf16[56,8320]{1,0:T(8,128)(2,1)S(1)}, u32[]{:S(2)}, u32[]{:S(2)}) collective-permute-start(bf16[56,8320]{1,0:T(8,128)(2,1)} %get-tuple-element.46.refs_1_), channel_id=1, source_target_pairs={{4,0},{5,1},{6,2},{7,3},{8,12},{9,13},{10,14},{11,15},{20,16},{21,... | collective-permute-start | bytes 2795528 | tf_op jit(solution)/shard_map/ppermute | solution.py:26
  120.1 24.6 %copy-start.8 = (bf16[56,8320]{1,0:T(8,128)(2,1)}, bf16[56,8320]{1,0:T(8,128)(2,1)S(1)}, u32[]{:S(2)}) copy-start(bf16[56,8320]{1,0:T(8,128)(2,1)S(1)} %collective-permute-done.11.refs_7_) | copy-start | bytes 2795524
  120.1 24.6 %copy-start.9 = (bf16[56,8320]{1,0:T(8,128)(2,1)}, bf16[56,8320]{1,0:T(8,128)(2,1)S(1)}, u32[]{:S(2)}) copy-start(bf16[56,8320]{1,0:T(8,128)(2,1)S(1)} %collective-permute-done.12.refs_8_) | copy-start | bytes 2795524
  144.7 20.9 %collective-permute-start.15 = (bf16[56,8320]{1,0:T(8,128)(2,1)}, bf16[56,8320]{1,0:T(8,128)(2,1)S(1)}, u32[]{:S(2)}, u32[]{:S(2)}) collective-permute-start(bf16[56,8320]{1,0:T(8,128)(2,1)} %get-tuple-element.66.refs_2_), channel_id=1, source_target_pairs={{0,1},{1,0},{2,3},{3,2},{4,5},{5,4},{6,7},{7,6},{8,9},{9,8},{10,11... | collective-permute-start | bytes 2795528 | tf_op jit(solution)/shard_map/ppermute | solution.py:22
  147.2 35.9 %collective-permute-start.13 = (bf16[56,8320]{1,0:T(8,128)(2,1)}, bf16[56,8320]{1,0:T(8,128)(2,1)S(1)}, u32[]{:S(2)}, u32[]{:S(2)}) collective-permute-start(bf16[56,8320]{1,0:T(8,128)(2,1)} %copies.5.refs_0_), channel_id=1, source_target_pairs={{0,2},{1,3},{2,0},{3,1},{4,6},{5,7},{6,4},{7,5},{8,10},{9,11},{10,... | collective-permute-start | bytes 2795528 | tf_op jit(solution)/shard_map/ppermute | solution.py:22
  148.9 34.2 %collective-permute-start.14 = (bf16[56,8320]{1,0:T(8,128)(2,1)}, bf16[56,8320]{1,0:T(8,128)(2,1)S(1)}, u32[]{:S(2)}, u32[]{:S(2)}) collective-permute-start(bf16[56,8320]{1,0:T(8,128)(2,1)} %copies.5.refs_0_), channel_id=1, source_target_pairs={{0,1},{1,0},{2,3},{3,2},{4,5},{5,4},{6,7},{7,6},{8,9},{9,8},{10,11... | collective-permute-start | bytes 2795528 | tf_op jit(solution)/shard_map/ppermute | solution.py:22
  184.4 2.7 %collective-permute-start.16 = (bf16[56,8320]{1,0:T(8,128)(2,1)}, bf16[56,8320]{1,0:T(8,128)(2,1)S(1)}, u32[]{:S(2)}, u32[]{:S(2)}) collective-permute-start(bf16[56,8320]{1,0:T(8,128)(2,1)} %get-tuple-element.72.refs_2_), channel_id=1, source_target_pairs={{0,1},{1,0},{2,3},{3,2},{4,5},{5,4},{6,7},{7,6},{8,9},{9,8},{10,11... | collective-permute-start | bytes 2795528 | tf_op jit(solution)/shard_map/ppermute | solution.py:22
  204.6 19.3 %copy-start.21 = (f32[4,64,128]{2,1,0:T(8,128)S(1)}, f32[4,64,128]{2,1,0:T(8,128)}, u32[]{:S(2)}) copy-start(f32[4,64,128]{2,1,0:T(8,128)} %get-tuple-element.75) | copy-start | bytes 393220
  204.6 19.3 %copy-start.22 = (f32[4,64,128]{2,1,0:T(8,128)S(1)}, f32[4,64,128]{2,1,0:T(8,128)}, u32[]{:S(2)}) copy-start(f32[4,64,128]{2,1,0:T(8,128)} %get-tuple-element.76) | copy-start | bytes 393220
  212.4 11.6 %copy-start.23 = (f32[4,64,128]{2,1,0:T(8,128)S(1)}, f32[4,64,128]{2,1,0:T(8,128)}, u32[]{:S(2)}) copy-start(f32[4,64,128]{2,1,0:T(8,128)} %get-tuple-element.77) | copy-start | bytes 393220
  212.4 20.4 %copy-start.24 = (f32[4,64,128]{2,1,0:T(8,128)S(1)}, f32[4,64,128]{2,1,0:T(8,128)}, u32[]{:S(2)}) copy-start(f32[4,64,128]{2,1,0:T(8,128)} %get-tuple-element.78) | copy-start | bytes 393220
  212.4 1.8 collective-permute-start.17
  215.2 8.6 %collective-permute-start.18 = (f32[16,32,128]{2,1,0:T(8,128)S(1)}, f32[16,32,128]{2,1,0:T(8,128)S(1)}, u32[]{:S(2)}, u32[]{:S(2)}) collective-permute-start(f32[16,32,128]{2,1,0:T(8,128)S(1)} %add.27), channel_id=1, source_target_pairs={{0,2},{1,3},{2,0},{3,1},{4,6},{5,7},{6,4},{7,5},{8,10},{9,11},{10,... | collective-permute-start | bytes 786440 | tf_op jit(solution)/shard_map/ppermute | solution.py:22
  223.8 7.8 %collective-permute-start.19 = (f32[16,32,128]{2,1,0:T(8,128)S(1)}, f32[16,32,128]{2,1,0:T(8,128)S(1)}, u32[]{:S(2)}, u32[]{:S(2)}) collective-permute-start(f32[16,32,128]{2,1,0:T(8,128)S(1)} %add.28), channel_id=1, source_target_pairs={{0,4},{1,5},{2,6},{3,7},{4,0},{5,1},{6,2},{7,3},{8,12},{9,13},{10,... | collective-permute-start | bytes 786440 | tf_op jit(solution)/shard_map/ppermute | solution.py:22
  231.7 13.4 %collective-permute-start.20 = (f32[16,32,128]{2,1,0:T(8,128)S(1)}, f32[16,32,128]{2,1,0:T(8,128)S(1)}, u32[]{:S(2)}, u32[]{:S(2)}) collective-permute-start(f32[16,32,128]{2,1,0:T(8,128)S(1)} %add.29), channel_id=1, source_target_pairs={{0,8},{1,9},{2,10},{3,11},{4,12},{5,13},{6,14},{7,15},{8,0},{9,1},... | collective-permute-start | bytes 786440 | tf_op jit(solution)/shard_map/ppermute | solution.py:22
  233.0 32.3 %copy-start.1 = (bf16[64,8192]{1,0:T(8,128)(2,1)S(1)}, bf16[64,8192]{1,0:T(8,128)(2,1)}, u32[]{:S(2)}) copy-start(bf16[64,8192]{1,0:T(8,128)(2,1)} %param.12) | copy-start | bytes 3145732
  (16 other events, 23.9 us)

commit v2 on v1

v2 whole, which is shorter than its diff:
```python
import functools

import jax
import jax.numpy as jnp
from jax import lax
from jax.experimental import pallas as pl
from jax.experimental.pallas import tpu as pltpu
from jax.sharding import PartitionSpec as P

AXIS = "dp"
HBM = pl.BlockSpec(memory_space=pl.ANY)
VMEM_LIMIT = 56 * 1024 * 1024


def contract_last(left, right):
    return lax.dot_general(
        left, right, (((1,), (1,)), ((), ())), preferred_element_type=jnp.float32
    )


def swap(block, bit, count):
    return lax.ppermute(block, AXIS, [(i, i ^ bit) for i in range(count)])


def line(block, pairs):
    return lax.ppermute(block, AXIS, [(4 * a + i, 4 * b + i) for a, b in pairs for i in range(4)])


def fence(*arrays):
    def body(*refs):
        pass

    return pl.pallas_call(
        body,
        out_shape=[jax.ShapeDtypeStruct(a.shape, a.dtype) for a in arrays],
        in_specs=[HBM] * len(arrays),
        out_specs=[HBM] * len(arrays),
        input_output_aliases={i: i for i in range(len(arrays))},
        name="fence",
    )(*arrays)


def by_device(gate, inner, count, first):
    rows, width = gate.shape[0], gate.shape[1] // count
    lanes = inner.shape[1]

    def body(g, own, one, two, sem):
        moves = []
        for i in range(count):
            cuts = (
                (pl.ds(i * width, first), one.at[i, :, pl.ds(0, first)]),
                (pl.ds(i * width + first, width - first), two.at[i]),
            )
            for half, (src, dst) in enumerate(cuts):
                moves.append(pltpu.make_async_copy(g.at[:, src], dst, sem.at[half, i]))
        for move in moves:
            move.start()
        for i in range(count):
            one[i, :, first:] = own[...]
        for move in moves:
            move.wait()

    return pl.pallas_call(
        body,
        out_shape=[
            jax.ShapeDtypeStruct((count, rows, first + lanes), gate.dtype),
            jax.ShapeDtypeStruct((count, rows, width - first), gate.dtype),
        ],
        in_specs=[HBM, pl.BlockSpec(memory_space=pltpu.VMEM)],
        out_specs=[pl.BlockSpec(memory_space=pltpu.VMEM)] * 2,
        scratch_shapes=[pltpu.SemaphoreType.DMA((2, count))],
        compiler_params=pltpu.CompilerParams(vmem_limit_bytes=VMEM_LIMIT),
        cost_estimate=pl.CostEstimate(flops=1, bytes_accessed=1, transcendentals=0),
        name="by_device",
    )(gate, inner)


def hidden_chunk(blocks, weight, tile=256):
    rows, depth = blocks[0].shape
    width = weight.shape[0]
    count = len(blocks)

    def body(*refs):
        ins, w, out, stacked = refs[:count], *refs[count:]

        @pl.when(pl.program_id(0) == 0)
        def _():
            for i in range(count):
                stacked[64 * i : 64 * i + rows, :] = ins[i][...]
                if rows < 64:
                    stacked[64 * i + rows : 64 * i + 64, :] = jnp.zeros((64 - rows, depth), stacked.dtype)

        out[...] = contract_last(stacked[...], w[...])

    return pl.pallas_call(
        body,
        grid=(width // tile,),
        out_shape=jax.ShapeDtypeStruct((64 * count, width), jnp.float32),
        in_specs=[pl.BlockSpec((rows, depth), lambda j: (0, 0), pipeline_mode=pl.Buffered(1))] * count
        + [pl.BlockSpec((tile, depth), lambda j: (j, 0))],
        out_specs=pl.BlockSpec((64 * count, tile), lambda j: (0, j)),
        scratch_shapes=[pltpu.VMEM((64 * count, depth), jnp.bfloat16)],
        compiler_params=pltpu.CompilerParams(vmem_limit_bytes=VMEM_LIMIT),
        cost_estimate=pl.CostEstimate(flops=1, bytes_accessed=1, transcendentals=0),
        name="hidden_chunk",
    )(*blocks, weight)


def project(hiddens, gates, proj, start, columns, tile=256):
    count, rows, _ = gates.shape
    heads = proj.shape[0]
    slots = len(hiddens)
    skip = start // tile

    def body(*refs):
        hs, g, p, out, grads = refs[:slots], *refs[slots:]
        step = pl.program_id(0)
        me = lax.axis_index(AXIS)

        @pl.when(step == 0)
        def _():
            grads[...] = jnp.zeros_like(grads)
            out[...] = jnp.zeros_like(out)

        for m in range(slots):
            for r in range(4):
                gate = g[me ^ (4 * m + r)].astype(jnp.float32)
                at = 256 * m + 64 * r
                grads[at : at + rows, :] = (hs[m][64 * r : 64 * r + rows, :] * gate).astype(jnp.bfloat16)
        out[...] += contract_last(grads[...], p[...])

    return pl.pallas_call(
        body,
        grid=(columns // tile,),
        out_shape=jax.ShapeDtypeStruct((256 * slots, heads), jnp.float32),
        in_specs=[pl.BlockSpec((256, tile), lambda j: (0, j + skip))] * slots
        + [
            pl.BlockSpec((count, rows, tile), lambda j: (0, 0, j)),
            pl.BlockSpec((heads, tile), lambda j: (0, j + skip)),
        ],
        out_specs=pl.BlockSpec((256 * slots, heads), lambda j: (0, 0)),
        scratch_shapes=[pltpu.VMEM((256 * slots, tile), jnp.bfloat16)],
        compiler_params=pltpu.CompilerParams(vmem_limit_bytes=VMEM_LIMIT),
        cost_estimate=pl.CostEstimate(flops=1, bytes_accessed=1, transcendentals=0),
        name="project",
    )(*hiddens, gates, proj)


def arrange(one, two, lengths, rows):
    count, heads = one.shape[0] // 64, one.shape[1]

    def body(a, b, spans, kept, given):
        me = lax.axis_index(AXIS)
        even = me % 2 == 0
        for r in range(count):
            block = a[64 * r : 64 * r + 64, :] + b[64 * r : 64 * r + 64, :]
            if r == 0:
                at = lax.broadcasted_iota(jnp.int32, block.shape, 0)
                block = jnp.where(at == rows, spans[...], block)
            low = jnp.concatenate([block[:16], block[16:32]], axis=1)
            high = jnp.concatenate([block[32:48], block[48:]], axis=1)
            kept[me ^ r] = jnp.where(even, low, high)
            given[me ^ r] = jnp.where(even, high, low)

    return pl.pallas_call(
        body, out_shape=[jax.ShapeDtypeStruct((count, 16, 2 * heads), jnp.float32)] * 2, name="arrange"
    )(one, two, lengths)


def partial_projection(rows, gate, inner, weight, proj, lengths):
    first = weight.shape[0] * 3 // 7
    place = lax.axis_index(AXIS) // 4
    edge = (place == 0) | (place == 3)
    pairs = [(0, 1), (1, 0), (2, 3), (3, 2)]
    middle = [(1, 2), (2, 1)]
    ends = [(1, 0), (2, 3)]

    def across(block):
        return swap(block, 2, 16)

    def core(block):
        return swap(block, 1, 16)

    def exchange(block):
        return lax.all_to_all(block, AXIS, split_axis=0, concat_axis=0, tiled=True)

    near, mid, y0, c0 = line(rows, pairs), line(rows, middle), across(rows), core(rows)
    one, two = by_device(gate, inner, 16, first)
    near, mid, y0, c0, one, two = fence(near, mid, y0, c0, one, two)

    mid_far, out_mid, y1 = line(near, middle), line(mid, ends), across(near)
    c1, cy0 = core(near), core(y0)
    h0 = hidden_chunk((rows, c0, y0, cy0), weight)
    mid_far, out_mid, near, mid, y1, c1, h0, one, two = fence(mid_far, out_mid, near, mid, y1, c1, h0, one, two)

    slot2 = jnp.where(edge, out_mid, mid_far)
    out_far, y2 = line(mid_far, ends), across(slot2)
    c2, cy1 = core(slot2), core(y1)
    h1 = hidden_chunk((near, c1, y1, cy1), weight)
    h1, one = fence(h1, one)
    one = exchange(one)
    out_far, mid, slot2, y2, c2, two = fence(out_far, mid, slot2, y2, c2, two)

    slot3 = jnp.where(edge, out_far, mid)
    y3 = across(slot3)
    c3, cy2 = core(slot3), core(y2)
    h2 = hidden_chunk((slot2, c2, y2, cy2), weight)
    slot3, y3, c3, h2, one, two = fence(slot3, y3, c3, h2, one, two)

    cy3 = core(y3)
    two = exchange(two)
    h3 = hidden_chunk((slot3, c3, y3, cy3), weight)
    hiddens = (h0, h1, h2, h3)
    p1 = project(hiddens, one, proj, 0, first)
    p2 = project(hiddens, two, proj, first, weight.shape[0] - first)
    return arrange(p1, p2, lengths, rows.shape[0]), one[:, :, first:]


def eliminate(system, right):
    size = system.shape[0]
    both = jnp.concatenate([system, right], axis=1)
    at = lax.broadcasted_iota(jnp.int32, (size, 1), 0)
    for j in range(0, size, 2):
        one, two = (jnp.broadcast_to(both[:, j + k : j + k + 1], both.shape) for k in range(2))
        a, b, c, d = one[j : j + 1], two[j : j + 1], one[j + 1 : j + 2], two[j + 1 : j + 2]
        inverse = 1.0 / (a * d - b * c)
        first, second = both[j : j + 1], both[j + 1 : j + 2]
        first, second = (d * first - b * second) * inverse, (a * second - c * first) * inverse
        both = both - jnp.where(at == j, a - 1.0, one) * first - jnp.where(at == j + 1, d - 1.0, two) * second
    return both[:, size:]


def halves(block):
    high = block.astype(jnp.bfloat16)
    return high, (block - high.astype(jnp.float32)).astype(jnp.bfloat16)


def product(left, right, dims):
    def one(a, b):
        return lax.dot_general(a, b, (dims, ((), ())), preferred_element_type=jnp.float32)

    return one(left[0], right[0]) + (one(left[0], right[1]) + one(left[1], right[0]))


def finish(kept, given, in_blocks, member, queries):
    count, _, heads = in_blocks.shape
    groups = count // 4
    examples = 4 * count
    wanted = queries.shape[0]

    def body(own, other, i, m, q, scores, left, double, grads):
        even = lax.axis_index(AXIS) % 2 == 0
        double[...] = jnp.zeros_like(double)
        for g in range(groups):
            parts = []
            for r in range(4):
                low = jnp.where(even, own[4 * g + r], other[4 * g + r])
                high = jnp.where(even, other[4 * g + r], own[4 * g + r])
                parts += [low[:, :heads], low[:, heads:], high[:, :heads], high[:, heads:]]
            turned = jnp.concatenate(parts, axis=0).T
            inner = i[4 * g : 4 * g + 4].reshape(256, heads)
            double[:256, :heads] = inner
            double[256:, heads:] = inner
            mask = m[g]
            for p in range(heads // 2):
                left[16 * p : 16 * p + 16, :256] = mask * turned[2 * p : 2 * p + 1, :]
                left[16 * p : 16 * p + 16, 256:] = mask * turned[2 * p + 1 : 2 * p + 2, :]
            made = product(halves(left[...]), halves(double[...]), ((1,), (0,)))
            for p in range(heads // 2):
                grads[16 * g : 16 * g + 16, 128 * p : 128 * p + 128] = made[16 * p : 16 * p + 16, :]
        made = halves(grads[...])
        last = ((1,), (1,))
        against = product(halves(q[...]), made, last).T
        gram = product(made, made, last)
        row = lax.broadcasted_iota(jnp.int32, (examples, examples), 0)
        eye = (row == lax.broadcasted_iota(jnp.int32, (examples, examples), 1)).astype(jnp.float32)
        trace = jnp.sum(gram * eye, axis=(0, 1), keepdims=True)
        damping = 0.1 * trace / (examples * examples)
        scores[...] = eliminate(gram / examples + damping * eye, against)

    return pl.pallas_call(
        body,
        out_shape=jax.ShapeDtypeStruct((examples, wanted), jnp.float32),
        scratch_shapes=[
            pltpu.VMEM((8 * heads, 512), jnp.float32),
            pltpu.VMEM((512, 2 * heads), jnp.float32),
            pltpu.VMEM((examples, heads * heads), jnp.float32),
        ],
        compiler_params=pltpu.CompilerParams(vmem_limit_bytes=VMEM_LIMIT),
        name="finish",
    )(kept, given, in_blocks, member, queries)


def in_place_order(inner, spans, rows):
    count = spans.shape[0]
    heads = inner.shape[2] // 2
    inner = jnp.pad(inner.astype(jnp.float32), ((0, 0), (0, 64 - rows), (0, 0)))
    in_blocks = inner[:, :, :heads] + inner[:, :, heads:]
    stop_at = jnp.cumsum(spans, axis=1)
    position = jnp.arange(64, dtype=jnp.int32)
    inside = (position >= (stop_at - spans)[:, :, None]) & (position < stop_at[:, :, None])
    apart = jnp.eye(4, dtype=bool)[None, :, None, :, None] & inside.reshape(count // 4, 4, 4, 1, 64)
    return in_blocks, apart.astype(jnp.float32).reshape(count // 4, 16, 256)


def per_device(acts, out_grad, gate_factor, down_weight, proj_in, proj_out, lengths, queries):
    rows = acts.shape[0]
    count = gate_factor.shape[1] // down_weight.shape[0]
    heads = proj_in.shape[0]
    own = contract_last(acts, proj_in)
    high = lax.reduce_precision(own, 8, 7)
    low = (own - high).astype(jnp.bfloat16)
    inner = jnp.concatenate([high.astype(jnp.bfloat16), low], axis=1)
    spans = jnp.pad(lengths.astype(jnp.float32), ((0, 0), (0, heads - 4)))
    if count == 16:
        (kept, given), inner = partial_projection(out_grad, gate_factor, inner, down_weight, proj_out, spans)
    else:
        inner = lax.all_gather(inner, AXIS)
        factor = lax.all_to_all(gate_factor, AXIS, split_axis=1, concat_axis=0, tiled=True)
        hidden = contract_last(lax.all_gather(out_grad, AXIS, axis=0, tiled=True), down_weight)
        hidden_grad = (hidden * factor.astype(jnp.float32)).astype(jnp.bfloat16)
        partial = contract_last(hidden_grad, proj_out).reshape(count, rows, heads)
        partial = jnp.pad(partial, ((0, 0), (0, 64 - rows), (0, 0)))
        partial = lax.dynamic_update_slice(partial, spans[None], (lax.axis_index(AXIS), rows, 0))
        low, high = (jnp.concatenate([half[:, :16], half[:, 16:]], axis=2) for half in (partial[:, :32], partial[:, 32:]))
        even = lax.axis_index(AXIS) % 2 == 0
        kept, given = jnp.where(even, low, high), jnp.where(even, high, low)
    kept = kept + swap(given, 1, count)
    bit = 2
    while bit < count:
        kept = kept + swap(kept, bit, count)
        bit *= 2
    given = swap(kept, 1, count)
    high = jnp.where(lax.axis_index(AXIS) % 2 == 0, given, kept)
    at = rows - 32
    spans = high[:, at % 16, heads * (at // 16) : heads * (at // 16) + 4].astype(jnp.int32)
    in_blocks, member = in_place_order(inner, spans, rows)
    return finish(kept, given, in_blocks, member, queries)


def solution(mesh):
    return jax.shard_map(
        per_device,
        mesh=mesh,
        in_specs=(
            P(("groups", "dp"), None),
            P(("groups", "dp"), None),
            P(("groups", "dp"), None),
            P("dp", None),
            P(),
            P(None, "dp"),
            P(("groups", "dp"), None),
            P("dp", None),
        ),
        out_specs=P("groups", "dp"),
        check_vma=False,
    )
```

time: 266 us -> 216 us (0.81)
  waiting for transfers between devices: 124 us -> 68.5 us
  starting transfers between devices: 21.9 us -> 37.1 us
  Pallas kernels: 102 us -> 91.5 us
  local copies, waits for them, and re-layouts: 13.9 us -> 9.54 us
  other arithmetic: 2.14 us -> 6.13 us
    ppermute x16 -> x17, waiting for transfers between devices: 77.6 us -> 36.1 us  [swap(): return lax.ppermute(block, AXIS, [(i, i ^ bit) for i in range(count)])]
    ppermute x5, waiting for transfers between devices: 46 us -> 20.1 us  [line(): lax.ppermute(block, AXIS, [(4 * a + i, 4 * b + i) for a, b in pairs for i...]
    all_to_all x1 -> x2, waiting for transfers between devices: 0.01 us -> 12.3 us  [exchange(): return lax.all_to_all(block, AXIS, split_axis=0, concat_axis=0, tiled=True)]
    ppermute x16 -> x17, starting transfers between devices: 10.4 us -> 20 us  [swap(): return lax.ppermute(block, AXIS, [(i, i ^ bit) for i in range(count)])]
    pallas_call x1, Pallas kernels: 18.9 us -> 9.83 us  [finish(): pl.pallas_call(body, out_shape=jax.ShapeDtypeStruct((examples, wanted), j...]
    all_to_all x1 -> x2, starting transfers between devices: 4.49 us -> 10.1 us  [exchange(): return lax.all_to_all(block, AXIS, split_axis=0, concat_axis=0, tiled=True)]
    unnamed x55 -> x38, local copies, waits for them, and re-layouts: 9.59 us -> 7.4 us
  transfers between devices with their start and end apart: 22 -> 24, of which waited for: 11 -> 11; matrix products, arithmetic and copies ran while one was open for 1% -> 4% of each run, Pallas kernels for 28% -> 35%
where the time goes in v2:
time: 216 us; the launch traced here: 215 us
  Pallas kernels  91.5 us (42%)
  waiting for transfers between devices  68.5 us (32%)
  starting transfers between devices  37.1 us (17%)
  local copies, waits for them, and re-layouts  9.54 us (4%)
  other arithmetic  6.13 us (3%)
    pallas_call x4, Pallas kernels, hidden_chunk(): pl.pallas_call(body, grid=(width // tile,), out_shape=jax.ShapeDtypeStruc...  66 us
    ppermute x17, waiting for transfers between devices, swap(): return lax.ppermute(block, AXIS, [(i, i ^ bit) for i in range(count)])  36.1 us
    ppermute x5, waiting for transfers between devices, line(): lax.ppermute(block, AXIS, [(4 * a + i, 4 * b + i) for a, b in pairs for i...  20.1 us
    ppermute x17, starting transfers between devices, swap(): return lax.ppermute(block, AXIS, [(i, i ^ bit) for i in range(count)])  20 us
    all_to_all x2, waiting for transfers between devices, exchange(): return lax.all_to_all(block, AXIS, split_axis=0, concat_axis=0, tiled=True)  12.3 us
    all_to_all x2, starting transfers between devices, exchange(): return lax.all_to_all(block, AXIS, split_axis=0, concat_axis=0, tiled=True)  10.1 us
    pallas_call x1, Pallas kernels, finish(): pl.pallas_call(body, out_shape=jax.ShapeDtypeStruct((examples, wanted), j...  9.83 us
    pallas_call x2, Pallas kernels, project(): pl.pallas_call(body, grid=(columns // tile,), out_shape=jax.ShapeDtypeStr...  8.9 us
  transfers between devices with their start and end apart: 24, of which 11 were waited for; matrix products, arithmetic and copies ran while one was open for 4% of the time, Pallas kernels for 35%

profile of v2, /device:TPU:0, one launch (start us, length us, event | category | flops | bytes accessed | tf_op | source)
XLA Modules:
  0.0 214.7 jit_solution(2212411890770064626)
XLA Ops:
  0.0 3.0 %collective-permute-start = (bf16[56,8192]{1,0:T(8,128)(2,1)}, bf16[56,8192]{1,0:T(8,128)(2,1)S(1)}, u32[]{:S(2)}, u32[]{:S(2)}) collective-permute-start(bf16[56,8192]{1,0:T(8,128)(2,1)} %refs_0_.1), channel_id=1, source_target_pairs={{0,4},{1,5},{2,6},{3,7},{4,0},{5,1},{6,2},{7,3},{8,12},{9,13},{10,... | collective-permute-start | bytes 2752520 | tf_op jit(solution)/shard_map/ppermute | solution.py:26
  3.7 1.6 collective-permute-start.2
  5.3 1.6 reduce-precision_convert_fusion
  7.6 4.7 %by_device.1 = (bf16[16,56,896]{2,1,0:T(8,128)(2,1)}, bf16[16,56,1024]{2,1,0:T(8,128)(2,1)}) custom-call(bf16[56,28672]{1,0:T(8,128)(2,1)} %g.1, bf16[56,128]{1,0:T(8,128)(2,1)} %pad_maximum_fusion.own), custom_call_target="tpu_custom_call" | custom-call | flops 1 | bytes 1 | tf_op jit(solution)/shard_map/by_device/pallas_call | solution.py:63
  12.3 11.2 %collective-permute-done.refs_0_ = bf16[56,8192]{1,0:T(8,128)(2,1)S(1)} collective-permute-done((bf16[56,8192]{1,0:T(8,128)(2,1)}, bf16[56,8192]{1,0:T(8,128)(2,1)S(1)}, u32[]{:S(2)}, u32[]{:S(2)}) %collective-permute-start) | collective-permute-done | bytes 917536 | tf_op jit(solution)/shard_map/ppermute | solution.py:26
  23.6 2.3 %collective-permute-done.2.refs_2_ = bf16[56,8192]{1,0:T(8,128)(2,1)} collective-permute-done((bf16[56,8192]{1,0:T(8,128)(2,1)}, bf16[56,8192]{1,0:T(8,128)(2,1)}, u32[]{:S(2)}, u32[]{:S(2)}) %collective-permute-start.2) | collective-permute-done | bytes 917536 | tf_op jit(solution)/shard_map/ppermute | solution.py:22
  26.8 1.3 collective-permute-start.5
  28.1 1.6 collective-permute-start.6
  29.9 16.5 %hidden_chunk.4.refs_6_ = f32[256,1792]{1,0:T(8,128)} custom-call(bf16[56,8192]{1,0:T(8,128)(2,1)} %refs_0_.1, bf16[56,8192]{1,0:T(8,128)(2,1)} %get-tuple-element.42.refs_1_, bf16[56,8192]{1,0:T(8,128)(2,1)} %get-tuple-element.43.refs_2_, bf16[56,8192]{1,0:T(8,128)(2,1)} %collective-permute-done.8.refs_3_, bf16[1792,8192]{1,0:T(8,128)(2,1)} %refs_4_.7), custom_call_target="tpu_custom_call" | custom-call | flops 1 | bytes 1 | tf_op jit(solution)/shard_map/hidden_chunk/pallas_call | solution.py:95
  46.3 8.8 %collective-permute-done.5.refs_1_ = bf16[56,8192]{1,0:T(8,128)(2,1)S(1)} collective-permute-done((bf16[56,8192]{1,0:T(8,128)(2,1)}, bf16[56,8192]{1,0:T(8,128)(2,1)S(1)}, u32[]{:S(2)}, u32[]{:S(2)}) %collective-permute-start.5) | collective-permute-done | bytes 917536 | tf_op jit(solution)/shard_map/ppermute | solution.py:26
  56.4 1.3 collective-permute-start.10
  57.7 1.3 broadcast_select_fusion.1.refs_2_
  59.0 1.6 collective-permute-start.11
  61.8 16.5 %hidden_chunk.5.refs_0_ = f32[256,1792]{1,0:T(8,128)} custom-call(bf16[56,8192]{1,0:T(8,128)(2,1)} %get-tuple-element.47.refs_0_, bf16[56,8192]{1,0:T(8,128)(2,1)} %get-tuple-element.48.refs_1_, bf16[56,8192]{1,0:T(8,128)(2,1)} %get-tuple-element.49.refs_2_, bf16[56,8192]{1,0:T(8,128)(2,1)} %copy-done.13, bf16[1792,8192]{1,0:T(8,128)(2,1)} %refs_4_.7), custom_call_target="tpu_custom_call" | custom-call | flops 1 | bytes 1 | tf_op jit(solution)/shard_map/hidden_chunk/pallas_call | solution.py:95
  78.2 5.3 %all-to-all-start = ((bf16[16,56,896]{2,1,0:T(8,128)(2,1)}), bf16[16,56,896]{2,1,0:T(8,128)(2,1)S(1)}, u32[]{:S(2)}, u32[]{:S(2)}) async-start(bf16[16,56,896]{2,1,0:T(8,128)(2,1)} %get-tuple-element.61), calls=%async_computation | async-start | bytes 3211264 | tf_op jit(solution)/shard_map/all_to_all | solution.py:185
  85.4 1.7 collective-permute-start.13
  88.2 16.5 %hidden_chunk.6.refs_3_ = f32[256,1792]{1,0:T(8,128)} custom-call(bf16[56,8192]{1,0:T(8,128)(2,1)} %get-tuple-element.58.refs_0_, bf16[56,8192]{1,0:T(8,128)(2,1)} %get-tuple-element.59.refs_1_, bf16[56,8192]{1,0:T(8,128)(2,1)} %get-tuple-element.60.refs_2_, bf16[56,8192]{1,0:T(8,128)(2,1)} %copy-done.14, bf16[1792,8192]{1,0:T(8,128)(2,1)} %refs_4_.7), custom_call_target="tpu_custom_call" | custom-call | flops 1 | bytes 1 | tf_op jit(solution)/shard_map/hidden_chunk/pallas_call | solution.py:95
  104.7 18.9 %collective-permute-done.13.refs_1_ = bf16[56,8192]{1,0:T(8,128)(2,1)S(1)} collective-permute-done((bf16[56,8192]{1,0:T(8,128)(2,1)S(1)}, bf16[56,8192]{1,0:T(8,128)(2,1)S(1)}, u32[]{:S(2)}, u32[]{:S(2)}) %collective-permute-start.13) | collective-permute-done | bytes 917536 | tf_op jit(solution)/shard_map/ppermute | solution.py:22
  125.7 4.8 %all-to-all-start.1 = ((bf16[16,56,1024]{2,1,0:T(8,128)(2,1)}), bf16[16,56,1024]{2,1,0:T(8,128)(2,1)S(1)}, u32[]{:S(2)}, u32[]{:S(2)}) async-start(bf16[16,56,1024]{2,1,0:T(8,128)(2,1)} %get-tuple-element.68), calls=%async_computation.1 | async-start | bytes 3670016 | tf_op jit(solution)/shard_map/all_to_all | solution.py:185
  131.5 1.6 collective-permute-done.16.refs_3_
  134.0 16.5 %hidden_chunk.7.refs_3_ = f32[256,1792]{1,0:T(8,128)} custom-call(bf16[56,8192]{1,0:T(8,128)(2,1)} %get-tuple-element.64.refs_0_, bf16[56,8192]{1,0:T(8,128)(2,1)} %get-tuple-element.65.refs_1_, bf16[56,8192]{1,0:T(8,128)(2,1)} %get-tuple-element.66.refs_2_, bf16[56,8192]{1,0:T(8,128)(2,1)} %copy-done.15, bf16[1792,8192]{1,0:T(8,128)(2,1)} %refs_4_.7), custom_call_target="tpu_custom_call" | custom-call | flops 1 | bytes 1 | tf_op jit(solution)/shard_map/hidden_chunk/pallas_call | solution.py:95
  150.6 4.2 %project.2.a = f32[1024,64]{1,0:T(8,128)} custom-call(f32[256,1792]{1,0:T(8,128)} %get-tuple-element.46.refs_0_, f32[256,1792]{1,0:T(8,128)} %get-tuple-element.51.refs_1_, f32[256,1792]{1,0:T(8,128)} %get-tuple-element.63.refs_2_, f32[256,1792]{1,0:T(8,128)} %hidden_chunk.7.refs_3_, bf16[16,56,896]{2,1,0:T(8,128)(2,1)} %get-tuple-element.67.refs_4_, ...), custom_call_target="tpu_custom_call" | custom-call | flops 1 | bytes 1 | tf_op jit(solution)/shard_map/project/pallas_call | solution.py:132
  154.7 12.3 %all-to-all-done.1.refs_4_ = bf16[16,56,1024]{2,1,0:T(8,128)(2,1)S(1)} async-done(((bf16[16,56,1024]{2,1,0:T(8,128)(2,1)}), bf16[16,56,1024]{2,1,0:T(8,128)(2,1)S(1)}, u32[]{:S(2)}, u32[]{:S(2)}) %all-to-all-start.1) | async-done | bytes 1835040 | tf_op jit(solution)/shard_map/all_to_all | solution.py:185
  168.3 4.7 %project.3.b = f32[1024,64]{1,0:T(8,128)} custom-call(f32[256,1792]{1,0:T(8,128)} %get-tuple-element.46.refs_0_, f32[256,1792]{1,0:T(8,128)} %get-tuple-element.51.refs_1_, f32[256,1792]{1,0:T(8,128)} %get-tuple-element.63.refs_2_, f32[256,1792]{1,0:T(8,128)} %hidden_chunk.7.refs_3_, bf16[16,56,1024]{2,1,0:T(8,128)(2,1)} %copy-done.7, bf16[64,1792]{1,0:T(8,128)(2,1)} %refs_5_.3), custom_call_target="tpu_custom_call" | custom-call | flops 1 | bytes 1 | tf_op jit(solution)/shard_map/project/pallas_call | solution.py:132
  173.0 2.0 arrange.1
  178.0 3.1 %collective-permute-start.18 = (f32[16,16,128]{2,1,0:T(8,128)S(1)}, f32[16,16,128]{2,1,0:T(8,128)S(1)}, u32[]{:S(2)}, u32[]{:S(2)}) collective-permute-start(f32[16,16,128]{2,1,0:T(8,128)S(1)} %add.24), channel_id=1, source_target_pairs={{0,2},{1,3},{2,0},{3,1},{4,6},{5,7},{6,4},{7,5},{8,10},{9,11},{10,... | collective-permute-start | bytes 393224 | tf_op jit(solution)/shard_map/ppermute | solution.py:22
  181.1 4.0 %collective-permute-done.18 = f32[16,16,128]{2,1,0:T(8,128)S(1)} collective-permute-done((f32[16,16,128]{2,1,0:T(8,128)S(1)}, f32[16,16,128]{2,1,0:T(8,128)S(1)}, u32[]{:S(2)}, u32[]{:S(2)}) %collective-permute-start.18) | collective-permute-done | bytes 131104 | tf_op jit(solution)/shard_map/ppermute | solution.py:22
  185.1 5.1 %collective-permute-start.19 = (f32[16,16,128]{2,1,0:T(8,128)S(1)}, f32[16,16,128]{2,1,0:T(8,128)S(1)}, u32[]{:S(2)}, u32[]{:S(2)}) collective-permute-start(f32[16,16,128]{2,1,0:T(8,128)S(1)} %add.25), channel_id=1, source_target_pairs={{0,4},{1,5},{2,6},{3,7},{4,0},{5,1},{6,2},{7,3},{8,12},{9,13},{10,... | collective-permute-start | bytes 393224 | tf_op jit(solution)/shard_map/ppermute | solution.py:22
  190.2 3.5 %collective-permute-done.19 = f32[16,16,128]{2,1,0:T(8,128)S(1)} collective-permute-done((f32[16,16,128]{2,1,0:T(8,128)S(1)}, f32[16,16,128]{2,1,0:T(8,128)S(1)}, u32[]{:S(2)}, u32[]{:S(2)}) %collective-permute-start.19) | collective-permute-done | bytes 131104 | tf_op jit(solution)/shard_map/ppermute | solution.py:22
  193.7 3.0 %collective-permute-start.20 = (f32[16,16,128]{2,1,0:T(8,128)S(1)}, f32[16,16,128]{2,1,0:T(8,128)S(1)}, u32[]{:S(2)}, u32[]{:S(2)}) collective-permute-start(f32[16,16,128]{2,1,0:T(8,128)S(1)} %add.26), channel_id=1, source_target_pairs={{0,8},{1,9},{2,10},{3,11},{4,12},{5,13},{6,14},{7,15},{8,0},{9,1},... | collective-permute-start | bytes 393224 | tf_op jit(solution)/shard_map/ppermute | solution.py:22
  197.8 4.3 %collective-permute-done.20 = f32[16,16,128]{2,1,0:T(8,128)S(1)} collective-permute-done((f32[16,16,128]{2,1,0:T(8,128)S(1)}, f32[16,16,128]{2,1,0:T(8,128)S(1)}, u32[]{:S(2)}, u32[]{:S(2)}) %collective-permute-start.20) | collective-permute-done | bytes 131104 | tf_op jit(solution)/shard_map/ppermute | solution.py:22
  204.9 9.8 %finish.1 = f32[64,128]{1,0:T(8,128)} custom-call(f32[16,16,128]{2,1,0:T(8,128)} %copy-done.16, f32[16,16,128]{2,1,0:T(8,128)} %copy-done.17, f32[16,64,64]{2,1,0:T(8,128)} %slice_add_fusion.i, f32[4,16,256]{2,1,0:T(8,128)} %and_convert_fusion.m, f32[128,4096]{1,0:T(8,128)} %q.1), custom_call_target="tpu_custom_call" | custom-call | tf_op jit(solution)/shard_map/finish/pallas_call | solution.py:281
  (94 shorter events, 19.7 us)
Async XLA Ops:
  0.0 5.3 %copy-start = (bf16[64,8192]{1,0:T(8,128)(2,1)S(1)}, bf16[64,8192]{1,0:T(8,128)(2,1)}, u32[]{:S(2)}) copy-start(bf16[64,8192]{1,0:T(8,128)(2,1)} %param.12) | copy-start | bytes 3145732
  0.0 23.6 %collective-permute-start = (bf16[56,8192]{1,0:T(8,128)(2,1)}, bf16[56,8192]{1,0:T(8,128)(2,1)S(1)}, u32[]{:S(2)}, u32[]{:S(2)}) collective-permute-start(bf16[56,8192]{1,0:T(8,128)(2,1)} %refs_0_.1), channel_id=1, source_target_pairs={{0,4},{1,5},{2,6},{3,7},{4,0},{5,1},{6,2},{7,3},{8,12},{9,13},{10,... | collective-permute-start | bytes 2752520 | tf_op jit(solution)/shard_map/ppermute | solution.py:26
  3.0 20.6 %collective-permute-start.1 = (bf16[56,8192]{1,0:T(8,128)(2,1)}, bf16[56,8192]{1,0:T(8,128)(2,1)S(1)}, u32[]{:S(2)}, u32[]{:S(2)}) collective-permute-start(bf16[56,8192]{1,0:T(8,128)(2,1)} %refs_0_.1), channel_id=1, source_target_pairs={{4,8},{5,9},{6,10},{7,11},{8,4},{9,5},{10,6},{11,7},{20,24},{21,25... | collective-permute-start | bytes 2752520 | tf_op jit(solution)/shard_map/ppermute | solution.py:26
  3.7 22.2 %collective-permute-start.2 = (bf16[56,8192]{1,0:T(8,128)(2,1)}, bf16[56,8192]{1,0:T(8,128)(2,1)}, u32[]{:S(2)}, u32[]{:S(2)}) collective-permute-start(bf16[56,8192]{1,0:T(8,128)(2,1)} %refs_0_.1), channel_id=1, source_target_pairs={{0,2},{1,3},{2,0},{3,1},{4,6},{5,7},{6,4},{7,5},{8,10},{9,11},{10,... | collective-permute-start | bytes 2752520 | tf_op jit(solution)/shard_map/ppermute | solution.py:22
  5.3 20.6 %collective-permute-start.3 = (bf16[56,8192]{1,0:T(8,128)(2,1)}, bf16[56,8192]{1,0:T(8,128)(2,1)}, u32[]{:S(2)}, u32[]{:S(2)}) collective-permute-start(bf16[56,8192]{1,0:T(8,128)(2,1)} %refs_0_.1), channel_id=1, source_target_pairs={{0,1},{1,0},{2,3},{3,2},{4,5},{5,4},{6,7},{7,6},{8,9},{9,8},{10,11... | collective-permute-start | bytes 2752520 | tf_op jit(solution)/shard_map/ppermute | solution.py:22
  26.0 3.9 %collective-permute-start.8 = (bf16[56,8192]{1,0:T(8,128)(2,1)}, bf16[56,8192]{1,0:T(8,128)(2,1)}, u32[]{:S(2)}, u32[]{:S(2)}) collective-permute-start(bf16[56,8192]{1,0:T(8,128)(2,1)} %get-tuple-element.43.refs_2_), channel_id=1, source_target_pairs={{0,1},{1,0},{2,3},{3,2},{4,5},{5,4},{6,7},{7,6},{8,9},{9,8},{10,11... | collective-permute-start | bytes 2752520 | tf_op jit(solution)/shard_map/ppermute | solution.py:22
  26.0 20.3 %collective-permute-start.4 = (bf16[56,8192]{1,0:T(8,128)(2,1)}, bf16[56,8192]{1,0:T(8,128)(2,1)S(1)}, u32[]{:S(2)}, u32[]{:S(2)}) collective-permute-start(bf16[56,8192]{1,0:T(8,128)(2,1)} %get-tuple-element.40.refs_2_), channel_id=1, source_target_pairs={{4,8},{5,9},{6,10},{7,11},{8,4},{9,5},{10,6},{11,7},{20,24},{21,25... | collective-permute-start | bytes 2752520 | tf_op jit(solution)/shard_map/ppermute | solution.py:26
  26.8 28.4 %collective-permute-start.5 = (bf16[56,8192]{1,0:T(8,128)(2,1)}, bf16[56,8192]{1,0:T(8,128)(2,1)S(1)}, u32[]{:S(2)}, u32[]{:S(2)}) collective-permute-start(bf16[56,8192]{1,0:T(8,128)(2,1)} %get-tuple-element.41.refs_3_), channel_id=1, source_target_pairs={{4,0},{5,1},{6,2},{7,3},{8,12},{9,13},{10,14},{11,15},{20,16},{21,... | collective-permute-start | bytes 2752520 | tf_op jit(solution)/shard_map/ppermute | solution.py:26
  28.1 27.1 %collective-permute-start.6 = (bf16[56,8192]{1,0:T(8,128)(2,1)}, bf16[56,8192]{1,0:T(8,128)(2,1)S(1)}, u32[]{:S(2)}, u32[]{:S(2)}) collective-permute-start(bf16[56,8192]{1,0:T(8,128)(2,1)} %get-tuple-element.40.refs_2_), channel_id=1, source_target_pairs={{0,2},{1,3},{2,0},{3,1},{4,6},{5,7},{6,4},{7,5},{8,10},{9,11},{10,... | collective-permute-start | bytes 2752520 | tf_op jit(solution)/shard_map/ppermute | solution.py:22
  29.6 25.5 %collective-permute-start.7 = (bf16[56,8192]{1,0:T(8,128)(2,1)}, bf16[56,8192]{1,0:T(8,128)(2,1)}, u32[]{:S(2)}, u32[]{:S(2)}) collective-permute-start(bf16[56,8192]{1,0:T(8,128)(2,1)} %get-tuple-element.40.refs_2_), channel_id=1, source_target_pairs={{0,1},{1,0},{2,3},{3,2},{4,5},{5,4},{6,7},{7,6},{8,9},{9,8},{10,11... | collective-permute-start | bytes 2752520 | tf_op jit(solution)/shard_map/ppermute | solution.py:22
  46.3 8.8 %copy-start.8 = (bf16[56,8192]{1,0:T(8,128)(2,1)}, bf16[56,8192]{1,0:T(8,128)(2,1)S(1)}, u32[]{:S(2)}) copy-start(bf16[56,8192]{1,0:T(8,128)(2,1)S(1)} %collective-permute-done.4.refs_0_) | copy-start | bytes 2752516
  56.4 4.4 %collective-permute-start.9 = (bf16[56,8192]{1,0:T(8,128)(2,1)}, bf16[56,8192]{1,0:T(8,128)(2,1)S(1)}, u32[]{:S(2)}, u32[]{:S(2)}) collective-permute-start(bf16[56,8192]{1,0:T(8,128)(2,1)} %get-tuple-element.49.refs_2_), channel_id=1, source_target_pairs={{0,1},{1,0},{2,3},{3,2},{4,5},{5,4},{6,7},{7,6},{8,9},{9,8},{10,11... | collective-permute-start | bytes 2752520 | tf_op jit(solution)/shard_map/ppermute | solution.py:22
  56.4 27.2 %collective-permute-start.10 = (bf16[56,8192]{1,0:T(8,128)(2,1)}, bf16[56,8192]{1,0:T(8,128)(2,1)}, u32[]{:S(2)}, u32[]{:S(2)}) collective-permute-start(bf16[56,8192]{1,0:T(8,128)(2,1)} %get-tuple-element.52), channel_id=1, source_target_pairs={{4,0},{5,1},{6,2},{7,3},{8,12},{9,13},{10,14},{11,15},{20,16},{21,... | collective-permute-start | bytes 2752520 | tf_op jit(solution)/shard_map/ppermute | solution.py:26
  59.0 19.3 %copy-start.4 = (bf16[56,8192]{1,0:T(8,128)(2,1)}, bf16[56,8192]{1,0:T(8,128)(2,1)S(1)}, u32[]{:S(2)}) copy-start(bf16[56,8192]{1,0:T(8,128)(2,1)S(1)} %broadcast_select_fusion.1.refs_2_) | copy-start | bytes 2752516
  59.0 24.6 %collective-permute-start.11 = (bf16[56,8192]{1,0:T(8,128)(2,1)S(1)}, bf16[56,8192]{1,0:T(8,128)(2,1)}, u32[]{:S(2)}, u32[]{:S(2)}) collective-permute-start(bf16[56,8192]{1,0:T(8,128)(2,1)S(1)} %broadcast_select_fusion.1.refs_2_), channel_id=1, source_target_pairs={{0,2},{1,3},{2,0},{3,1},{4,6},{5,7},{6,4},{7,5},{8,10},{9,11},{10,... | collective-permute-start | bytes 2752520 | tf_op jit(solution)/shard_map/ppermute | solution.py:22
  60.6 23.0 %collective-permute-start.12 = (bf16[56,8192]{1,0:T(8,128)(2,1)S(1)}, bf16[56,8192]{1,0:T(8,128)(2,1)}, u32[]{:S(2)}, u32[]{:S(2)}) collective-permute-start(bf16[56,8192]{1,0:T(8,128)(2,1)S(1)} %broadcast_select_fusion.1.refs_2_), channel_id=1, source_target_pairs={{0,1},{1,0},{2,3},{3,2},{4,5},{5,4},{6,7},{7,6},{8,9},{9,8},{10,11... | collective-permute-start | bytes 2752520 | tf_op jit(solution)/shard_map/ppermute | solution.py:22
  78.2 46.3 %all-to-all-start = ((bf16[16,56,896]{2,1,0:T(8,128)(2,1)}), bf16[16,56,896]{2,1,0:T(8,128)(2,1)S(1)}, u32[]{:S(2)}, u32[]{:S(2)}) async-start(bf16[16,56,896]{2,1,0:T(8,128)(2,1)} %get-tuple-element.61), calls=%async_computation | async-start | bytes 3211264 | tf_op jit(solution)/shard_map/all_to_all | solution.py:185
  83.6 3.6 %collective-permute-start.15 = (bf16[56,8192]{1,0:T(8,128)(2,1)}, bf16[56,8192]{1,0:T(8,128)(2,1)S(1)}, u32[]{:S(2)}, u32[]{:S(2)}) collective-permute-start(bf16[56,8192]{1,0:T(8,128)(2,1)} %get-tuple-element.60.refs_2_), channel_id=1, source_target_pairs={{0,1},{1,0},{2,3},{3,2},{4,5},{5,4},{6,7},{7,6},{8,9},{9,8},{10,11... | collective-permute-start | bytes 2752520 | tf_op jit(solution)/shard_map/ppermute | solution.py:22
  85.4 19.3 %copy-start.6 = (bf16[56,8192]{1,0:T(8,128)(2,1)}, bf16[56,8192]{1,0:T(8,128)(2,1)S(1)}, u32[]{:S(2)}) copy-start(bf16[56,8192]{1,0:T(8,128)(2,1)S(1)} %broadcast_select_fusion.refs_0_) | copy-start | bytes 2752516
  85.4 38.2 %collective-permute-start.13 = (bf16[56,8192]{1,0:T(8,128)(2,1)S(1)}, bf16[56,8192]{1,0:T(8,128)(2,1)S(1)}, u32[]{:S(2)}, u32[]{:S(2)}) collective-permute-start(bf16[56,8192]{1,0:T(8,128)(2,1)S(1)} %broadcast_select_fusion.refs_0_), channel_id=1, source_target_pairs={{0,2},{1,3},{2,0},{3,1},{4,6},{5,7},{6,4},{7,5},{8,10},{9,11},{10,... | collective-permute-start | bytes 2752520 | tf_op jit(solution)/shard_map/ppermute | solution.py:22
  87.2 37.4 %collective-permute-start.14 = (bf16[56,8192]{1,0:T(8,128)(2,1)S(1)}, bf16[56,8192]{1,0:T(8,128)(2,1)}, u32[]{:S(2)}, u32[]{:S(2)}) collective-permute-start(bf16[56,8192]{1,0:T(8,128)(2,1)S(1)} %broadcast_select_fusion.refs_0_), channel_id=1, source_target_pairs={{0,1},{1,0},{2,3},{3,2},{4,5},{5,4},{6,7},{7,6},{8,9},{9,8},{10,11... | collective-permute-start | bytes 2752520 | tf_op jit(solution)/shard_map/ppermute | solution.py:22
  125.7 4.8 %copy-start.12 = (bf16[56,8192]{1,0:T(8,128)(2,1)S(1)}, bf16[56,8192]{1,0:T(8,128)(2,1)}, u32[]{:S(2)}) copy-start(bf16[56,8192]{1,0:T(8,128)(2,1)} %get-tuple-element.66.refs_2_) | copy-start | bytes 2752516
  125.7 5.3 %copy-start.18 = (s32[1,4]{1,0:T(1,128)S(1)}, s32[1,4]{1,0:T(1,128)}, u32[]{:S(2)}) copy-start(s32[1,4]{1,0:T(1,128)} %param.14) | copy-start | bytes 52
  125.7 41.3 %all-to-all-start.1 = ((bf16[16,56,1024]{2,1,0:T(8,128)(2,1)}), bf16[16,56,1024]{2,1,0:T(8,128)(2,1)S(1)}, u32[]{:S(2)}, u32[]{:S(2)}) async-start(bf16[16,56,1024]{2,1,0:T(8,128)(2,1)} %get-tuple-element.68), calls=%async_computation.1 | async-start | bytes 3670016 | tf_op jit(solution)/shard_map/all_to_all | solution.py:185
  130.6 2.6 %collective-permute-start.16 = (bf16[56,8192]{1,0:T(8,128)(2,1)S(1)}, bf16[56,8192]{1,0:T(8,128)(2,1)S(1)}, u32[]{:S(2)}, u32[]{:S(2)}) collective-permute-start(bf16[56,8192]{1,0:T(8,128)(2,1)S(1)} %copy-done.12), channel_id=1, source_target_pairs={{0,1},{1,0},{2,3},{3,2},{4,5},{5,4},{6,7},{7,6},{8,9},{9,8},{10,11... | collective-permute-start | bytes 2752520 | tf_op jit(solution)/shard_map/ppermute | solution.py:22
  175.1 2.0 collective-permute-start.17
  178.0 7.1 %collective-permute-start.18 = (f32[16,16,128]{2,1,0:T(8,128)S(1)}, f32[16,16,128]{2,1,0:T(8,128)S(1)}, u32[]{:S(2)}, u32[]{:S(2)}) collective-permute-start(f32[16,16,128]{2,1,0:T(8,128)S(1)} %add.24), channel_id=1, source_target_pairs={{0,2},{1,3},{2,0},{3,1},{4,6},{5,7},{6,4},{7,5},{8,10},{9,11},{10,... | collective-permute-start | bytes 393224 | tf_op jit(solution)/shard_map/ppermute | solution.py:22
  185.1 8.5 %collective-permute-start.19 = (f32[16,16,128]{2,1,0:T(8,128)S(1)}, f32[16,16,128]{2,1,0:T(8,128)S(1)}, u32[]{:S(2)}, u32[]{:S(2)}) collective-permute-start(f32[16,16,128]{2,1,0:T(8,128)S(1)} %add.25), channel_id=1, source_target_pairs={{0,4},{1,5},{2,6},{3,7},{4,0},{5,1},{6,2},{7,3},{8,12},{9,13},{10,... | collective-permute-start | bytes 393224 | tf_op jit(solution)/shard_map/ppermute | solution.py:22
  193.7 8.4 %collective-permute-start.20 = (f32[16,16,128]{2,1,0:T(8,128)S(1)}, f32[16,16,128]{2,1,0:T(8,128)S(1)}, u32[]{:S(2)}, u32[]{:S(2)}) collective-permute-start(f32[16,16,128]{2,1,0:T(8,128)S(1)} %add.26), channel_id=1, source_target_pairs={{0,8},{1,9},{2,10},{3,11},{4,12},{5,13},{6,14},{7,15},{8,0},{9,1},... | collective-permute-start | bytes 393224 | tf_op jit(solution)/shard_map/ppermute | solution.py:22
  202.1 2.8 %copy-start.16 = (f32[16,16,128]{2,1,0:T(8,128)}, f32[16,16,128]{2,1,0:T(8,128)S(1)}, u32[]{:S(2)}) copy-start(f32[16,16,128]{2,1,0:T(8,128)S(1)} %add.27.own) | copy-start | bytes 393220
  202.1 1.4 collective-permute-start.21
  202.2 12.5 %copy-start.1 = (bf16[64,8192]{1,0:T(8,128)(2,1)S(1)}, bf16[64,8192]{1,0:T(8,128)(2,1)}, u32[]{:S(2)}) copy-start(bf16[64,8192]{1,0:T(8,128)(2,1)} %param.12) | copy-start | bytes 3145732
  (11 other events, 14.4 us)

commit v3 on v2

--- a/solution.py
+++ b/solution.py
@@ -40,35 +40,33 @@
     )(*arrays)
 
 
-def by_device(gate, inner, count, first):
+def by_device(gate, inner, count, parts):
     rows, width = gate.shape[0], gate.shape[1] // count
     lanes = inner.shape[1]
 
-    def body(g, own, one, two, sem):
+    def body(g, own, *refs):
+        outs, sem = refs[:-1], refs[-1]
         moves = []
         for i in range(count):
-            cuts = (
-                (pl.ds(i * width, first), one.at[i, :, pl.ds(0, first)]),
-                (pl.ds(i * width + first, width - first), two.at[i]),
-            )
-            for half, (src, dst) in enumerate(cuts):
-                moves.append(pltpu.make_async_copy(g.at[:, src], dst, sem.at[half, i]))
+            start = i * width
+            for k, size in enumerate(parts):
+                src, dst = g.at[:, pl.ds(start, size)], outs[k].at[i, :, pl.ds(0, size)]
+                moves.append(pltpu.make_async_copy(src, dst, sem.at[k, i]))
+                start += size
         for move in moves:
             move.start()
         for i in range(count):
-            one[i, :, first:] = own[...]
+            outs[0][i, :, parts[0] :] = own[...]
         for move in moves:
             move.wait()
 
+    sizes = [parts[0] + lanes, *parts[1:]]
     return pl.pallas_call(
         body,
-        out_shape=[
-            jax.ShapeDtypeStruct((count, rows, first + lanes), gate.dtype),
-            jax.ShapeDtypeStruct((count, rows, width - first), gate.dtype),
-        ],
+        out_shape=[jax.ShapeDtypeStruct((count, rows, size), gate.dtype) for size in sizes],
         in_specs=[HBM, pl.BlockSpec(memory_space=pltpu.VMEM)],
-        out_specs=[pl.BlockSpec(memory_space=pltpu.VMEM)] * 2,
-        scratch_shapes=[pltpu.SemaphoreType.DMA((2, count))],
+        out_specs=[pl.BlockSpec(memory_space=pltpu.VMEM)] * len(parts),
+        scratch_shapes=[pltpu.SemaphoreType.DMA((len(parts), count))],
         compiler_params=pltpu.CompilerParams(vmem_limit_bytes=VMEM_LIMIT),
         cost_estimate=pl.CostEstimate(flops=1, bytes_accessed=1, transcendentals=0),
         name="by_device",
@@ -106,69 +104,76 @@
     )(*blocks, weight)
 
 
-def project(hiddens, gates, proj, start, columns, tile=256):
+def project(hiddens, gates, proj, start, columns, before=None, lengths=None, tile=256):
     count, rows, _ = gates.shape
     heads = proj.shape[0]
     slots = len(hiddens)
     skip = start // tile
+    more = [a for a in (before, lengths) if a is not None]
 
     def body(*refs):
-        hs, g, p, out, grads = refs[:slots], *refs[slots:]
+        hs, g, p = refs[:slots], refs[slots], refs[slots + 1]
+        total, grads = refs[-2:]
+        outs = refs[slots + 2 + len(more) : -2]
         step = pl.program_id(0)
         me = lax.axis_index(AXIS)
 
         @pl.when(step == 0)
         def _():
             grads[...] = jnp.zeros_like(grads)
-            out[...] = jnp.zeros_like(out)
+            total[...] = jnp.zeros_like(total) if before is None else refs[slots + 2][...]
 
         for m in range(slots):
             for r in range(4):
                 gate = g[me ^ (4 * m + r)].astype(jnp.float32)
                 at = 256 * m + 64 * r
                 grads[at : at + rows, :] = (hs[m][64 * r : 64 * r + rows, :] * gate).astype(jnp.bfloat16)
-        out[...] += contract_last(grads[...], p[...])
-
-    return pl.pallas_call(
+        total[...] += contract_last(grads[...], p[...])
+
+        @pl.when(step == pl.num_programs(0) - 1)
+        def _():
+            if lengths is None:
+                outs[0][...] = total[...]
+                return
+            even = me % 2 == 0
+            for r in range(4 * slots):
+                block = total[64 * r : 64 * r + 64]
+                if r == 0:
+                    at = lax.broadcasted_iota(jnp.int32, block.shape, 0)
+                    block = jnp.where(at == rows, refs[slots + 3][...], block)
+                low = jnp.concatenate([block[:16], block[16:32]], axis=1)
+                high = jnp.concatenate([block[32:48], block[48:]], axis=1)
+                outs[0][me ^ r] = jnp.where(even, low, high)
+                outs[1][me ^ r] = jnp.where(even, high, low)
+
+    if lengths is None:
+        shapes = [(256 * slots, heads)]
+    else:
+        shapes = [(count, 16, 2 * heads)] * 2
+    outs = pl.pallas_call(
         body,
         grid=(columns // tile,),
-        out_shape=jax.ShapeDtypeStruct((256 * slots, heads), jnp.float32),
+        out_shape=[jax.ShapeDtypeStruct(shape, jnp.float32) for shape in shapes],
         in_specs=[pl.BlockSpec((256, tile), lambda j: (0, j + skip))] * slots
         + [
             pl.BlockSpec((count, rows, tile), lambda j: (0, 0, j)),
             pl.BlockSpec((heads, tile), lambda j: (0, j + skip)),
+        ]
+        + [pl.BlockSpec(a.shape, lambda j: (0, 0)) for a in more],
+        out_specs=[pl.BlockSpec(shape, lambda j, rank=len(shape): (0,) * rank) for shape in shapes],
+        scratch_shapes=[
+            pltpu.VMEM((256 * slots, heads), jnp.float32),
+            pltpu.VMEM((256 * slots, tile), jnp.bfloat16),
         ],
-        out_specs=pl.BlockSpec((256 * slots, heads), lambda j: (0, 0)),
-        scratch_shapes=[pltpu.VMEM((256 * slots, tile), jnp.bfloat16)],
         compiler_params=pltpu.CompilerParams(vmem_limit_bytes=VMEM_LIMIT),
         cost_estimate=pl.CostEstimate(flops=1, bytes_accessed=1, transcendentals=0),
         name="project",
-    )(*hiddens, gates, proj)
-
-
-def arrange(one, two, lengths, rows):
-    count, heads = one.shape[0] // 64, one.shape[1]
-
-    def body(a, b, spans, kept, given):
-        me = lax.axis_index(AXIS)
-        even = me % 2 == 0
-        for r in range(count):
-            block = a[64 * r : 64 * r + 64, :] + b[64 * r : 64 * r + 64, :]
-            if r == 0:
-                at = lax.broadcasted_iota(jnp.int32, block.shape, 0)
-                block = jnp.where(at == rows, spans[...], block)
-            low = jnp.concatenate([block[:16], block[16:32]], axis=1)
-            high = jnp.concatenate([block[32:48], block[48:]], axis=1)
-            kept[me ^ r] = jnp.where(even, low, high)
-            given[me ^ r] = jnp.where(even, high, low)
-
-    return pl.pallas_call(
-        body, out_shape=[jax.ShapeDtypeStruct((count, 16, 2 * heads), jnp.float32)] * 2, name="arrange"
-    )(one, two, lengths)
+    )(*hiddens, gates, proj, *more)
+    return outs[0] if lengths is None else outs
 
 
 def partial_projection(rows, gate, inner, weight, proj, lengths):
-    first = weight.shape[0] * 3 // 7
+    parts = [weight.shape[0] // 7 * k for k in (3,4)]
     place = lax.axis_index(AXIS) // 4
     edge = (place == 0) | (place == 3)
     pairs = [(0, 1), (1, 0), (2, 3), (3, 2)]
@@ -185,35 +190,37 @@
         return lax.all_to_all(block, AXIS, split_axis=0, concat_axis=0, tiled=True)
 
     near, mid, y0, c0 = line(rows, pairs), line(rows, middle), across(rows), core(rows)
-    one, two = by_device(gate, inner, 16, first)
-    near, mid, y0, c0, one, two = fence(near, mid, y0, c0, one, two)
+    g0, g1 = by_device(gate, inner, 16, parts)
+    near, mid, y0, c0, g0, g1 = fence(near, mid, y0, c0, g0, g1)
 
     mid_far, out_mid, y1 = line(near, middle), line(mid, ends), across(near)
     c1, cy0 = core(near), core(y0)
     h0 = hidden_chunk((rows, c0, y0, cy0), weight)
-    mid_far, out_mid, near, mid, y1, c1, h0, one, two = fence(mid_far, out_mid, near, mid, y1, c1, h0, one, two)
+    mid_far, out_mid, near, mid, y1, c1, h0, g0, g1 = fence(mid_far, out_mid, near, mid, y1, c1, h0, g0, g1)
 
     slot2 = jnp.where(edge, out_mid, mid_far)
     out_far, y2 = line(mid_far, ends), across(slot2)
     c2, cy1 = core(slot2), core(y1)
     h1 = hidden_chunk((near, c1, y1, cy1), weight)
-    h1, one = fence(h1, one)
-    one = exchange(one)
-    out_far, mid, slot2, y2, c2, two = fence(out_far, mid, slot2, y2, c2, two)
+    h1, g0 = fence(h1, g0)
+    g0 = exchange(g0)
+    out_far, mid, slot2, y2, c2, g1 = fence(out_far, mid, slot2, y2, c2, g1)
 
     slot3 = jnp.where(edge, out_far, mid)
     y3 = across(slot3)
     c3, cy2 = core(slot3), core(y2)
     h2 = hidden_chunk((slot2, c2, y2, cy2), weight)
-    slot3, y3, c3, h2, one, two = fence(slot3, y3, c3, h2, one, two)
+    slot3, y3, c3, h2, g0, g1 = fence(slot3, y3, c3, h2, g0, g1)
 
     cy3 = core(y3)
-    two = exchange(two)
+    g1 = exchange(g1)
     h3 = hidden_chunk((slot3, c3, y3, cy3), weight)
     hiddens = (h0, h1, h2, h3)
-    p1 = project(hiddens, one, proj, 0, first)
-    p2 = project(hiddens, two, proj, first, weight.shape[0] - first)
-    return arrange(p1, p2, lengths, rows.shape[0]), one[:, :, first:]
+    sums, start = None, 0
+    for k, gates in enumerate((g0, g1)):
+        sums = project(hiddens, gates, proj, start, parts[k], sums, lengths if k == len(parts) - 1 else None)
+        start += parts[k]
+    return sums, g0[:, :, parts[0] :]
 
 
 def eliminate(system, right):
@@ -242,26 +249,42 @@
     return one(left[0], right[0]) + (one(left[0], right[1]) + one(left[1], right[0]))
 
 
-def finish(kept, given, in_blocks, member, queries):
+def places(spans):
+    row = lax.broadcasted_iota(jnp.int32, (16, 256), 0)
+    start = stop = jnp.zeros((16, 256), jnp.float32)
+    for r, span in enumerate(spans):
+        end = jnp.zeros((1, 1), jnp.float32)
+        for j in range(4):
+            start = jnp.where(row == 4 * r + j, end, start)
+            end = end + span[:, j : j + 1]
+            stop = jnp.where(row == 4 * r + j, end, stop)
+    at = (lax.broadcasted_iota(jnp.int32, (16, 256), 1) - 64 * (row // 4)).astype(jnp.float32)
+    return jnp.where((at >= start) & (at < stop), 1.0, 0.0)
+
+
+def finish(kept, given, in_blocks, queries, rows):
     count, _, heads = in_blocks.shape
     groups = count // 4
     examples = 4 * count
     wanted = queries.shape[0]
 
-    def body(own, other, i, m, q, scores, left, double, grads):
+    at = rows - 32
+
+    def body(own, other, i, q, scores, left, double, grads):
         even = lax.axis_index(AXIS) % 2 == 0
         double[...] = jnp.zeros_like(double)
         for g in range(groups):
-            parts = []
+            parts, spans = [], []
             for r in range(4):
                 low = jnp.where(even, own[4 * g + r], other[4 * g + r])
                 high = jnp.where(even, other[4 * g + r], own[4 * g + r])
                 parts += [low[:, :heads], low[:, heads:], high[:, :heads], high[:, heads:]]
+                spans.append(high[at % 16 : at % 16 + 1, heads * (at // 16) : heads * (at // 16) + 4])
             turned = jnp.concatenate(parts, axis=0).T
             inner = i[4 * g : 4 * g + 4].reshape(256, heads)
             double[:256, :heads] = inner
             double[256:, heads:] = inner
-            mask = m[g]
+            mask = places(spans)
             for p in range(heads // 2):
                 left[16 * p : 16 * p + 16, :256] = mask * turned[2 * p : 2 * p + 1, :]
                 left[16 * p : 16 * p + 16, 256:] = mask * turned[2 * p + 1 : 2 * p + 2, :]
@@ -286,21 +309,9 @@
             pltpu.VMEM((512, 2 * heads), jnp.float32),
             pltpu.VMEM((examples, heads * heads), jnp.float32),
         ],
-        compiler_params=pltpu.CompilerParams(vmem_limit_bytes=VMEM_LIMIT),
+        compiler_params=pltpu.CompilerParams(vmem_limit_bytes=24 * 1024 * 1024),
         name="finish",
-    )(kept, given, in_blocks, member, queries)
-
-
-def in_place_order(inner, spans, rows):
-    count = spans.shape[0]
-    heads = inner.shape[2] // 2
-    inner = jnp.pad(inner.astype(jnp.float32), ((0, 0), (0, 64 - rows), (0, 0)))
-    in_blocks = inner[:, :, :heads] + inner[:, :, heads:]
-    stop_at = jnp.cumsum(spans, axis=1)
-    position = jnp.arange(64, dtype=jnp.int32)
-    inside = (position >= (stop_at - spans)[:, :, None]) & (position < stop_at[:, :, None])
-    apart = jnp.eye(4, dtype=bool)[None, :, None, :, None] & inside.reshape(count // 4, 4, 4, 1, 64)
-    return in_blocks, apart.astype(jnp.float32).reshape(count // 4, 16, 256)
+    )(kept, given, in_blocks, queries)
 
 
 def per_device(acts, out_grad, gate_factor, down_weight, proj_in, proj_out, lengths, queries):
@@ -331,11 +342,8 @@
         kept = kept + swap(kept, bit, count)
         bit *= 2
     given = swap(kept, 1, count)
-    high = jnp.where(lax.axis_index(AXIS) % 2 == 0, given, kept)
-    at = rows - 32
-    spans = high[:, at % 16, heads * (at // 16) : heads * (at // 16) + 4].astype(jnp.int32)
-    in_blocks, member = in_place_order(inner, spans, rows)
-    return finish(kept, given, in_blocks, member, queries)
+    inner = jnp.pad(inner.astype(jnp.float32), ((0, 0), (0, 64 - rows), (0, 0)))
+    return finish(kept, given, inner[:, :, :heads] + inner[:, :, heads:], queries, rows)
 
 
 def solution(mesh):

time: 216 us -> 213 us (0.986)
  Pallas kernels: 91.5 us -> 88.1 us
    ppermute x17, waiting for transfers between devices: 36.1 us -> 40.5 us  [swap(): return lax.ppermute(block, AXIS, [(i, i ^ bit) for i in range(count)])]
    ppermute x5, waiting for transfers between devices: 20.1 us -> 17.7 us  [line(): lax.ppermute(block, AXIS, [(4 * a + i, 4 * b + i) for a, b in pairs for i...]
    pallas_call x4 -> x3, Pallas kernels: 15.7 us -> 14 us  [the longest x2 9.33 us: project(): pl.pallas_call(body, grid=(columns // tile,), out_shape=[jax.ShapeDtypeSt...]
    unnamed x38 -> x36, local copies, waits for them, and re-layouts: 7.4 us -> 7.17 us
  transfers between devices with their start and end apart: 24 -> 24, of which waited for: 11 -> 12; matrix products, arithmetic and copies ran while one was open for 4% -> 3% of each run, Pallas kernels for 35% -> 35%
where the time goes in v3:
time: 213 us; the launch traced here: 212 us
  Pallas kernels  88.1 us (41%)
  waiting for transfers between devices  70.5 us (33%)
  starting transfers between devices  38.1 us (18%)
  local copies, waits for them, and re-layouts  8.65 us (4%)
  other arithmetic  4.46 us (2%)
    pallas_call x4, Pallas kernels, hidden_chunk(): pl.pallas_call(body, grid=(width // tile,), out_shape=jax.ShapeDtypeStruc...  66 us
    ppermute x17, waiting for transfers between devices, swap(): return lax.ppermute(block, AXIS, [(i, i ^ bit) for i in range(count)])  40.5 us
    ppermute x17, starting transfers between devices, swap(): return lax.ppermute(block, AXIS, [(i, i ^ bit) for i in range(count)])  18.9 us
    ppermute x5, waiting for transfers between devices, line(): lax.ppermute(block, AXIS, [(4 * a + i, 4 * b + i) for a, b in pairs for i...  17.7 us
    all_to_all x2, waiting for transfers between devices, exchange(): return lax.all_to_all(block, AXIS, split_axis=0, concat_axis=0, tiled=True)  12.3 us
    all_to_all x2, starting transfers between devices, exchange(): return lax.all_to_all(block, AXIS, split_axis=0, concat_axis=0, tiled=True)  11.3 us
    pallas_call x2, Pallas kernels, project(): pl.pallas_call(body, grid=(columns // tile,), out_shape=[jax.ShapeDtypeSt...  9.33 us
    pallas_call x1, Pallas kernels, finish(): pl.pallas_call(body, out_shape=jax.ShapeDtypeStruct((examples, wanted), j...  8.03 us
  transfers between devices with their start and end apart: 24, of which 12 were waited for; matrix products, arithmetic and copies ran while one was open for 3% of the time, Pallas kernels for 35%

profile of v3, /device:TPU:0, one launch (start us, length us, event | category | flops | bytes accessed | tf_op | source)
XLA Modules:
  0.0 211.6 jit_solution(9813775588368310634)
XLA Ops:
  0.0 3.0 %collective-permute-start = (bf16[56,8192]{1,0:T(8,128)(2,1)}, bf16[56,8192]{1,0:T(8,128)(2,1)S(1)}, u32[]{:S(2)}, u32[]{:S(2)}) collective-permute-start(bf16[56,8192]{1,0:T(8,128)(2,1)} %refs_0_.1), channel_id=1, source_target_pairs={{0,4},{1,5},{2,6},{3,7},{4,0},{5,1},{6,2},{7,3},{8,12},{9,13},{10,... | collective-permute-start | bytes 2752520 | tf_op jit(solution)/shard_map/ppermute | solution.py:26
  3.7 1.6 collective-permute-start.2
  5.3 1.6 reduce-precision_convert_fusion
  7.6 4.7 %by_device.1 = (bf16[16,56,896]{2,1,0:T(8,128)(2,1)}, bf16[16,56,1024]{2,1,0:T(8,128)(2,1)}) custom-call(bf16[56,28672]{1,0:T(8,128)(2,1)} %g.1, bf16[56,128]{1,0:T(8,128)(2,1)} %pad_maximum_fusion.own), custom_call_target="tpu_custom_call" | custom-call | flops 1 | bytes 1 | tf_op jit(solution)/shard_map/by_device/pallas_call | solution.py:64
  12.3 11.2 %collective-permute-done.refs_0_ = bf16[56,8192]{1,0:T(8,128)(2,1)S(1)} collective-permute-done((bf16[56,8192]{1,0:T(8,128)(2,1)}, bf16[56,8192]{1,0:T(8,128)(2,1)S(1)}, u32[]{:S(2)}, u32[]{:S(2)}) %collective-permute-start) | collective-permute-done | bytes 917536 | tf_op jit(solution)/shard_map/ppermute | solution.py:26
  23.6 2.3 %collective-permute-done.2.refs_2_ = bf16[56,8192]{1,0:T(8,128)(2,1)} collective-permute-done((bf16[56,8192]{1,0:T(8,128)(2,1)}, bf16[56,8192]{1,0:T(8,128)(2,1)}, u32[]{:S(2)}, u32[]{:S(2)}) %collective-permute-start.2) | collective-permute-done | bytes 917536 | tf_op jit(solution)/shard_map/ppermute | solution.py:22
  26.0 1.6 collective-permute-start.4
  27.6 1.5 collective-permute-start.6
  29.4 1.3 collective-permute-start.5
  30.7 16.5 %hidden_chunk.4.refs_6_ = f32[256,1792]{1,0:T(8,128)} custom-call(bf16[56,8192]{1,0:T(8,128)(2,1)} %refs_0_.1, bf16[56,8192]{1,0:T(8,128)(2,1)} %get-tuple-element.42.refs_1_, bf16[56,8192]{1,0:T(8,128)(2,1)} %get-tuple-element.43.refs_2_, bf16[56,8192]{1,0:T(8,128)(2,1)} %collective-permute-done.8.refs_3_, bf16[1792,8192]{1,0:T(8,128)(2,1)} %refs_4_.7), custom_call_target="tpu_custom_call" | custom-call | flops 1 | bytes 1 | tf_op jit(solution)/shard_map/hidden_chunk/pallas_call | solution.py:93
  47.2 3.4 %collective-permute-done.6.refs_4_ = bf16[56,8192]{1,0:T(8,128)(2,1)S(1)} collective-permute-done((bf16[56,8192]{1,0:T(8,128)(2,1)}, bf16[56,8192]{1,0:T(8,128)(2,1)S(1)}, u32[]{:S(2)}, u32[]{:S(2)}) %collective-permute-start.6) | collective-permute-done | bytes 917536 | tf_op jit(solution)/shard_map/ppermute | solution.py:22
  50.6 6.4 %collective-permute-done.5.refs_1_ = bf16[56,8192]{1,0:T(8,128)(2,1)S(1)} collective-permute-done((bf16[56,8192]{1,0:T(8,128)(2,1)}, bf16[56,8192]{1,0:T(8,128)(2,1)S(1)}, u32[]{:S(2)}, u32[]{:S(2)}) %collective-permute-start.5) | collective-permute-done | bytes 917536 | tf_op jit(solution)/shard_map/ppermute | solution.py:26
  57.9 1.3 broadcast_select_fusion.1.refs_2_
  60.0 1.3 collective-permute-start.10
  62.2 16.5 %hidden_chunk.5.refs_0_ = f32[256,1792]{1,0:T(8,128)} custom-call(bf16[56,8192]{1,0:T(8,128)(2,1)} %get-tuple-element.47.refs_0_, bf16[56,8192]{1,0:T(8,128)(2,1)} %get-tuple-element.48.refs_1_, bf16[56,8192]{1,0:T(8,128)(2,1)} %get-tuple-element.49.refs_2_, bf16[56,8192]{1,0:T(8,128)(2,1)} %copy-done.14, bf16[1792,8192]{1,0:T(8,128)(2,1)} %refs_4_.7), custom_call_target="tpu_custom_call" | custom-call | flops 1 | bytes 1 | tf_op jit(solution)/shard_map/hidden_chunk/pallas_call | solution.py:93
  78.8 6.5 %all-to-all-start = ((bf16[16,56,896]{2,1,0:T(8,128)(2,1)}), bf16[16,56,896]{2,1,0:T(8,128)(2,1)S(1)}, u32[]{:S(2)}, u32[]{:S(2)}) async-start(bf16[16,56,896]{2,1,0:T(8,128)(2,1)} %get-tuple-element.61), calls=%async_computation | async-start | bytes 3211264 | tf_op jit(solution)/shard_map/all_to_all | solution.py:190
  87.1 1.7 collective-permute-start.13
  89.8 16.5 %hidden_chunk.6.refs_3_ = f32[256,1792]{1,0:T(8,128)} custom-call(bf16[56,8192]{1,0:T(8,128)(2,1)} %get-tuple-element.58.refs_0_, bf16[56,8192]{1,0:T(8,128)(2,1)} %get-tuple-element.59.refs_1_, bf16[56,8192]{1,0:T(8,128)(2,1)} %get-tuple-element.60.refs_2_, bf16[56,8192]{1,0:T(8,128)(2,1)} %copy-done.15, bf16[1792,8192]{1,0:T(8,128)(2,1)} %refs_4_.7), custom_call_target="tpu_custom_call" | custom-call | flops 1 | bytes 1 | tf_op jit(solution)/shard_map/hidden_chunk/pallas_call | solution.py:93
  106.3 18.9 %collective-permute-done.13.refs_1_ = bf16[56,8192]{1,0:T(8,128)(2,1)S(1)} collective-permute-done((bf16[56,8192]{1,0:T(8,128)(2,1)S(1)}, bf16[56,8192]{1,0:T(8,128)(2,1)S(1)}, u32[]{:S(2)}, u32[]{:S(2)}) %collective-permute-start.13) | collective-permute-done | bytes 917536 | tf_op jit(solution)/shard_map/ppermute | solution.py:22
  127.4 4.8 %all-to-all-start.1 = ((bf16[16,56,1024]{2,1,0:T(8,128)(2,1)}), bf16[16,56,1024]{2,1,0:T(8,128)(2,1)S(1)}, u32[]{:S(2)}, u32[]{:S(2)}) async-start(bf16[16,56,1024]{2,1,0:T(8,128)(2,1)} %get-tuple-element.67), calls=%async_computation.1 | async-start | bytes 3670016 | tf_op jit(solution)/shard_map/all_to_all | solution.py:190
  133.2 1.6 collective-permute-done.16.refs_3_
  135.7 16.5 %hidden_chunk.7.refs_3_ = f32[256,1792]{1,0:T(8,128)} custom-call(bf16[56,8192]{1,0:T(8,128)(2,1)} %get-tuple-element.64.refs_0_, bf16[56,8192]{1,0:T(8,128)(2,1)} %get-tuple-element.65.refs_1_, bf16[56,8192]{1,0:T(8,128)(2,1)} %get-tuple-element.66.refs_2_, bf16[56,8192]{1,0:T(8,128)(2,1)} %copy-done.16, bf16[1792,8192]{1,0:T(8,128)(2,1)} %refs_4_.7), custom_call_target="tpu_custom_call" | custom-call | flops 1 | bytes 1 | tf_op jit(solution)/shard_map/hidden_chunk/pallas_call | solution.py:93
  152.2 4.2 %project.2.refs_6_ = f32[1024,64]{1,0:T(8,128)} custom-call(f32[256,1792]{1,0:T(8,128)} %get-tuple-element.46.refs_0_, f32[256,1792]{1,0:T(8,128)} %get-tuple-element.51.refs_1_, f32[256,1792]{1,0:T(8,128)} %get-tuple-element.63.refs_2_, f32[256,1792]{1,0:T(8,128)} %hidden_chunk.7.refs_3_, bf16[16,56,896]{2,1,0:T(8,128)(2,1)} %get-tuple-element.68.refs_4_, ...), custom_call_target="tpu_custom_call" | custom-call | flops 1 | bytes 1 | tf_op jit(solution)/shard_map/project/pallas_call | solution.py:153
  156.4 12.3 %all-to-all-done.1.refs_4_ = bf16[16,56,1024]{2,1,0:T(8,128)(2,1)S(1)} async-done(((bf16[16,56,1024]{2,1,0:T(8,128)(2,1)}), bf16[16,56,1024]{2,1,0:T(8,128)(2,1)S(1)}, u32[]{:S(2)}, u32[]{:S(2)}) %all-to-all-start.1) | async-done | bytes 1835040 | tf_op jit(solution)/shard_map/all_to_all | solution.py:190
  170.0 5.1 %project.3 = (f32[16,16,128]{2,1,0:T(8,128)}, f32[16,16,128]{2,1,0:T(8,128)}) custom-call(f32[256,1792]{1,0:T(8,128)} %get-tuple-element.46.refs_0_, f32[256,1792]{1,0:T(8,128)} %get-tuple-element.51.refs_1_, f32[256,1792]{1,0:T(8,128)} %get-tuple-element.63.refs_2_, f32[256,1792]{1,0:T(8,128)} %hidden_chunk.7.refs_3_, bf16[16,56,1024]{2,1,0:T(8,128)(2,1)} %copy-done.8, ...), custom_call_target="tpu_custom_call" | custom-call | flops 1 | bytes 1 | tf_op jit(solution)/shard_map/project/pallas_call | solution.py:153
  178.0 3.1 %collective-permute-start.18 = (f32[16,16,128]{2,1,0:T(8,128)S(1)}, f32[16,16,128]{2,1,0:T(8,128)S(1)}, u32[]{:S(2)}, u32[]{:S(2)}) collective-permute-start(f32[16,16,128]{2,1,0:T(8,128)S(1)} %add.20), channel_id=1, source_target_pairs={{0,2},{1,3},{2,0},{3,1},{4,6},{5,7},{6,4},{7,5},{8,10},{9,11},{10,... | collective-permute-start | bytes 393224 | tf_op jit(solution)/shard_map/ppermute | solution.py:22
  181.1 4.0 %collective-permute-done.18 = f32[16,16,128]{2,1,0:T(8,128)S(1)} collective-permute-done((f32[16,16,128]{2,1,0:T(8,128)S(1)}, f32[16,16,128]{2,1,0:T(8,128)S(1)}, u32[]{:S(2)}, u32[]{:S(2)}) %collective-permute-start.18) | collective-permute-done | bytes 131104 | tf_op jit(solution)/shard_map/ppermute | solution.py:22
  185.1 5.1 %collective-permute-start.19 = (f32[16,16,128]{2,1,0:T(8,128)S(1)}, f32[16,16,128]{2,1,0:T(8,128)S(1)}, u32[]{:S(2)}, u32[]{:S(2)}) collective-permute-start(f32[16,16,128]{2,1,0:T(8,128)S(1)} %add.21), channel_id=1, source_target_pairs={{0,4},{1,5},{2,6},{3,7},{4,0},{5,1},{6,2},{7,3},{8,12},{9,13},{10,... | collective-permute-start | bytes 393224 | tf_op jit(solution)/shard_map/ppermute | solution.py:22
  190.2 3.5 %collective-permute-done.19 = f32[16,16,128]{2,1,0:T(8,128)S(1)} collective-permute-done((f32[16,16,128]{2,1,0:T(8,128)S(1)}, f32[16,16,128]{2,1,0:T(8,128)S(1)}, u32[]{:S(2)}, u32[]{:S(2)}) %collective-permute-start.19) | collective-permute-done | bytes 131104 | tf_op jit(solution)/shard_map/ppermute | solution.py:22
  193.7 3.0 %collective-permute-start.20 = (f32[16,16,128]{2,1,0:T(8,128)S(1)}, f32[16,16,128]{2,1,0:T(8,128)S(1)}, u32[]{:S(2)}, u32[]{:S(2)}) collective-permute-start(f32[16,16,128]{2,1,0:T(8,128)S(1)} %add.22), channel_id=1, source_target_pairs={{0,8},{1,9},{2,10},{3,11},{4,12},{5,13},{6,14},{7,15},{8,0},{9,1},... | collective-permute-start | bytes 393224 | tf_op jit(solution)/shard_map/ppermute | solution.py:22
  197.7 4.4 %collective-permute-done.20 = f32[16,16,128]{2,1,0:T(8,128)S(1)} collective-permute-done((f32[16,16,128]{2,1,0:T(8,128)S(1)}, f32[16,16,128]{2,1,0:T(8,128)S(1)}, u32[]{:S(2)}, u32[]{:S(2)}) %collective-permute-start.20) | collective-permute-done | bytes 131104 | tf_op jit(solution)/shard_map/ppermute | solution.py:22
  203.5 8.0 %finish.1 = f32[64,128]{1,0:T(8,128)} custom-call(f32[16,16,128]{2,1,0:T(8,128)S(1)} %add.23.own, f32[16,16,128]{2,1,0:T(8,128)S(1)} %collective-permute-done.21.other, f32[16,64,64]{2,1,0:T(8,128)S(1)} %slice_add_fusion.i, f32[128,4096]{1,0:T(8,128)S(1)} %copy-done.2), custom_call_target="tpu_custom_call" | custom-call | tf_op jit(solution)/shard_map/finish/pallas_call | solution.py:304
  (78 shorter events, 17.8 us)
Async XLA Ops:
  0.0 5.3 %copy-start = (bf16[64,8192]{1,0:T(8,128)(2,1)S(1)}, bf16[64,8192]{1,0:T(8,128)(2,1)}, u32[]{:S(2)}) copy-start(bf16[64,8192]{1,0:T(8,128)(2,1)} %param.12) | copy-start | bytes 3145732
  0.0 23.6 %collective-permute-start = (bf16[56,8192]{1,0:T(8,128)(2,1)}, bf16[56,8192]{1,0:T(8,128)(2,1)S(1)}, u32[]{:S(2)}, u32[]{:S(2)}) collective-permute-start(bf16[56,8192]{1,0:T(8,128)(2,1)} %refs_0_.1), channel_id=1, source_target_pairs={{0,4},{1,5},{2,6},{3,7},{4,0},{5,1},{6,2},{7,3},{8,12},{9,13},{10,... | collective-permute-start | bytes 2752520 | tf_op jit(solution)/shard_map/ppermute | solution.py:26
  3.0 20.6 %collective-permute-start.1 = (bf16[56,8192]{1,0:T(8,128)(2,1)}, bf16[56,8192]{1,0:T(8,128)(2,1)S(1)}, u32[]{:S(2)}, u32[]{:S(2)}) collective-permute-start(bf16[56,8192]{1,0:T(8,128)(2,1)} %refs_0_.1), channel_id=1, source_target_pairs={{4,8},{5,9},{6,10},{7,11},{8,4},{9,5},{10,6},{11,7},{20,24},{21,25... | collective-permute-start | bytes 2752520 | tf_op jit(solution)/shard_map/ppermute | solution.py:26
  3.7 22.2 %collective-permute-start.2 = (bf16[56,8192]{1,0:T(8,128)(2,1)}, bf16[56,8192]{1,0:T(8,128)(2,1)}, u32[]{:S(2)}, u32[]{:S(2)}) collective-permute-start(bf16[56,8192]{1,0:T(8,128)(2,1)} %refs_0_.1), channel_id=1, source_target_pairs={{0,2},{1,3},{2,0},{3,1},{4,6},{5,7},{6,4},{7,5},{8,10},{9,11},{10,... | collective-permute-start | bytes 2752520 | tf_op jit(solution)/shard_map/ppermute | solution.py:22
  5.3 20.6 %collective-permute-start.3 = (bf16[56,8192]{1,0:T(8,128)(2,1)}, bf16[56,8192]{1,0:T(8,128)(2,1)}, u32[]{:S(2)}, u32[]{:S(2)}) collective-permute-start(bf16[56,8192]{1,0:T(8,128)(2,1)} %refs_0_.1), channel_id=1, source_target_pairs={{0,1},{1,0},{2,3},{3,2},{4,5},{5,4},{6,7},{7,6},{8,9},{9,8},{10,11... | collective-permute-start | bytes 2752520 | tf_op jit(solution)/shard_map/ppermute | solution.py:22
  26.0 4.7 %collective-permute-start.8 = (bf16[56,8192]{1,0:T(8,128)(2,1)}, bf16[56,8192]{1,0:T(8,128)(2,1)}, u32[]{:S(2)}, u32[]{:S(2)}) collective-permute-start(bf16[56,8192]{1,0:T(8,128)(2,1)} %get-tuple-element.43.refs_2_), channel_id=1, source_target_pairs={{0,1},{1,0},{2,3},{3,2},{4,5},{5,4},{6,7},{7,6},{8,9},{9,8},{10,11... | collective-permute-start | bytes 2752520 | tf_op jit(solution)/shard_map/ppermute | solution.py:22
  26.0 21.1 %collective-permute-start.4 = (bf16[56,8192]{1,0:T(8,128)(2,1)}, bf16[56,8192]{1,0:T(8,128)(2,1)}, u32[]{:S(2)}, u32[]{:S(2)}) collective-permute-start(bf16[56,8192]{1,0:T(8,128)(2,1)} %get-tuple-element.40.refs_2_), channel_id=1, source_target_pairs={{4,8},{5,9},{6,10},{7,11},{8,4},{9,5},{10,6},{11,7},{20,24},{21,25... | collective-permute-start | bytes 2752520 | tf_op jit(solution)/shard_map/ppermute | solution.py:26
  27.6 22.9 %collective-permute-start.6 = (bf16[56,8192]{1,0:T(8,128)(2,1)}, bf16[56,8192]{1,0:T(8,128)(2,1)S(1)}, u32[]{:S(2)}, u32[]{:S(2)}) collective-permute-start(bf16[56,8192]{1,0:T(8,128)(2,1)} %get-tuple-element.40.refs_2_), channel_id=1, source_target_pairs={{0,2},{1,3},{2,0},{3,1},{4,6},{5,7},{6,4},{7,5},{8,10},{9,11},{10,... | collective-permute-start | bytes 2752520 | tf_op jit(solution)/shard_map/ppermute | solution.py:22
  29.1 21.4 %collective-permute-start.7 = (bf16[56,8192]{1,0:T(8,128)(2,1)}, bf16[56,8192]{1,0:T(8,128)(2,1)S(1)}, u32[]{:S(2)}, u32[]{:S(2)}) collective-permute-start(bf16[56,8192]{1,0:T(8,128)(2,1)} %get-tuple-element.40.refs_2_), channel_id=1, source_target_pairs={{0,1},{1,0},{2,3},{3,2},{4,5},{5,4},{6,7},{7,6},{8,9},{9,8},{10,11... | collective-permute-start | bytes 2752520 | tf_op jit(solution)/shard_map/ppermute | solution.py:22
  29.4 27.7 %collective-permute-start.5 = (bf16[56,8192]{1,0:T(8,128)(2,1)}, bf16[56,8192]{1,0:T(8,128)(2,1)S(1)}, u32[]{:S(2)}, u32[]{:S(2)}) collective-permute-start(bf16[56,8192]{1,0:T(8,128)(2,1)} %get-tuple-element.41.refs_3_), channel_id=1, source_target_pairs={{4,0},{5,1},{6,2},{7,3},{8,12},{9,13},{10,14},{11,15},{20,16},{21,... | collective-permute-start | bytes 2752520 | tf_op jit(solution)/shard_map/ppermute | solution.py:26
  50.6 6.4 %copy-start.10 = (bf16[56,8192]{1,0:T(8,128)(2,1)}, bf16[56,8192]{1,0:T(8,128)(2,1)S(1)}, u32[]{:S(2)}) copy-start(bf16[56,8192]{1,0:T(8,128)(2,1)S(1)} %collective-permute-done.6.refs_4_) | copy-start | bytes 2752516
  50.6 6.4 %copy-start.11 = (bf16[56,8192]{1,0:T(8,128)(2,1)}, bf16[56,8192]{1,0:T(8,128)(2,1)S(1)}, u32[]{:S(2)}) copy-start(bf16[56,8192]{1,0:T(8,128)(2,1)S(1)} %collective-permute-done.7.refs_5_) | copy-start | bytes 2752516
  57.9 3.4 %collective-permute-start.9 = (bf16[56,8192]{1,0:T(8,128)(2,1)}, bf16[56,8192]{1,0:T(8,128)(2,1)S(1)}, u32[]{:S(2)}, u32[]{:S(2)}) collective-permute-start(bf16[56,8192]{1,0:T(8,128)(2,1)} %get-tuple-element.49.refs_2_), channel_id=1, source_target_pairs={{0,1},{1,0},{2,3},{3,2},{4,5},{5,4},{6,7},{7,6},{8,9},{9,8},{10,11... | collective-permute-start | bytes 2752520 | tf_op jit(solution)/shard_map/ppermute | solution.py:22
  59.2 19.6 %copy-start.5 = (bf16[56,8192]{1,0:T(8,128)(2,1)}, bf16[56,8192]{1,0:T(8,128)(2,1)S(1)}, u32[]{:S(2)}) copy-start(bf16[56,8192]{1,0:T(8,128)(2,1)S(1)} %broadcast_select_fusion.1.refs_2_) | copy-start | bytes 2752516
  59.2 26.0 %collective-permute-start.11 = (bf16[56,8192]{1,0:T(8,128)(2,1)S(1)}, bf16[56,8192]{1,0:T(8,128)(2,1)}, u32[]{:S(2)}, u32[]{:S(2)}) collective-permute-start(bf16[56,8192]{1,0:T(8,128)(2,1)S(1)} %broadcast_select_fusion.1.refs_2_), channel_id=1, source_target_pairs={{0,2},{1,3},{2,0},{3,1},{4,6},{5,7},{6,4},{7,5},{8,10},{9,11},{10,... | collective-permute-start | bytes 2752520 | tf_op jit(solution)/shard_map/ppermute | solution.py:22
  59.8 25.5 %collective-permute-start.12 = (bf16[56,8192]{1,0:T(8,128)(2,1)S(1)}, bf16[56,8192]{1,0:T(8,128)(2,1)}, u32[]{:S(2)}, u32[]{:S(2)}) collective-permute-start(bf16[56,8192]{1,0:T(8,128)(2,1)S(1)} %broadcast_select_fusion.1.refs_2_), channel_id=1, source_target_pairs={{0,1},{1,0},{2,3},{3,2},{4,5},{5,4},{6,7},{7,6},{8,9},{9,8},{10,11... | collective-permute-start | bytes 2752520 | tf_op jit(solution)/shard_map/ppermute | solution.py:22
  60.0 25.3 %collective-permute-start.10 = (bf16[56,8192]{1,0:T(8,128)(2,1)}, bf16[56,8192]{1,0:T(8,128)(2,1)}, u32[]{:S(2)}, u32[]{:S(2)}) collective-permute-start(bf16[56,8192]{1,0:T(8,128)(2,1)} %get-tuple-element.52), channel_id=1, source_target_pairs={{4,0},{5,1},{6,2},{7,3},{8,12},{9,13},{10,14},{11,15},{20,16},{21,... | collective-permute-start | bytes 2752520 | tf_op jit(solution)/shard_map/ppermute | solution.py:26
  78.8 47.4 %all-to-all-start = ((bf16[16,56,896]{2,1,0:T(8,128)(2,1)}), bf16[16,56,896]{2,1,0:T(8,128)(2,1)S(1)}, u32[]{:S(2)}, u32[]{:S(2)}) async-start(bf16[16,56,896]{2,1,0:T(8,128)(2,1)} %get-tuple-element.61), calls=%async_computation | async-start | bytes 3211264 | tf_op jit(solution)/shard_map/all_to_all | solution.py:190
  85.3 3.6 %collective-permute-start.15 = (bf16[56,8192]{1,0:T(8,128)(2,1)}, bf16[56,8192]{1,0:T(8,128)(2,1)S(1)}, u32[]{:S(2)}, u32[]{:S(2)}) collective-permute-start(bf16[56,8192]{1,0:T(8,128)(2,1)} %get-tuple-element.60.refs_2_), channel_id=1, source_target_pairs={{0,1},{1,0},{2,3},{3,2},{4,5},{5,4},{6,7},{7,6},{8,9},{9,8},{10,11... | collective-permute-start | bytes 2752520 | tf_op jit(solution)/shard_map/ppermute | solution.py:22
  87.0 19.3 %copy-start.7 = (bf16[56,8192]{1,0:T(8,128)(2,1)}, bf16[56,8192]{1,0:T(8,128)(2,1)S(1)}, u32[]{:S(2)}) copy-start(bf16[56,8192]{1,0:T(8,128)(2,1)S(1)} %broadcast_select_fusion.refs_0_) | copy-start | bytes 2752516
  87.1 38.2 %collective-permute-start.13 = (bf16[56,8192]{1,0:T(8,128)(2,1)S(1)}, bf16[56,8192]{1,0:T(8,128)(2,1)S(1)}, u32[]{:S(2)}, u32[]{:S(2)}) collective-permute-start(bf16[56,8192]{1,0:T(8,128)(2,1)S(1)} %broadcast_select_fusion.refs_0_), channel_id=1, source_target_pairs={{0,2},{1,3},{2,0},{3,1},{4,6},{5,7},{6,4},{7,5},{8,10},{9,11},{10,... | collective-permute-start | bytes 2752520 | tf_op jit(solution)/shard_map/ppermute | solution.py:22
  88.8 37.4 %collective-permute-start.14 = (bf16[56,8192]{1,0:T(8,128)(2,1)S(1)}, bf16[56,8192]{1,0:T(8,128)(2,1)}, u32[]{:S(2)}, u32[]{:S(2)}) collective-permute-start(bf16[56,8192]{1,0:T(8,128)(2,1)S(1)} %broadcast_select_fusion.refs_0_), channel_id=1, source_target_pairs={{0,1},{1,0},{2,3},{3,2},{4,5},{5,4},{6,7},{7,6},{8,9},{9,8},{10,11... | collective-permute-start | bytes 2752520 | tf_op jit(solution)/shard_map/ppermute | solution.py:22
  127.4 5.3 %copy-start.17 = (s32[1,4]{1,0:T(1,128)S(1)}, s32[1,4]{1,0:T(1,128)}, u32[]{:S(2)}) copy-start(s32[1,4]{1,0:T(1,128)} %param.14) | copy-start | bytes 52
  127.4 41.3 %all-to-all-start.1 = ((bf16[16,56,1024]{2,1,0:T(8,128)(2,1)}), bf16[16,56,1024]{2,1,0:T(8,128)(2,1)S(1)}, u32[]{:S(2)}, u32[]{:S(2)}) async-start(bf16[16,56,1024]{2,1,0:T(8,128)(2,1)} %get-tuple-element.67), calls=%async_computation.1 | async-start | bytes 3670016 | tf_op jit(solution)/shard_map/all_to_all | solution.py:190
  132.2 2.6 %collective-permute-start.16 = (bf16[56,8192]{1,0:T(8,128)(2,1)S(1)}, bf16[56,8192]{1,0:T(8,128)(2,1)S(1)}, u32[]{:S(2)}, u32[]{:S(2)}) collective-permute-start(bf16[56,8192]{1,0:T(8,128)(2,1)S(1)} %copy-done.13), channel_id=1, source_target_pairs={{0,1},{1,0},{2,3},{3,2},{4,5},{5,4},{6,7},{7,6},{8,9},{9,8},{10,11... | collective-permute-start | bytes 2752520 | tf_op jit(solution)/shard_map/ppermute | solution.py:22
  175.1 2.0 collective-permute-start.17
  178.0 7.1 %collective-permute-start.18 = (f32[16,16,128]{2,1,0:T(8,128)S(1)}, f32[16,16,128]{2,1,0:T(8,128)S(1)}, u32[]{:S(2)}, u32[]{:S(2)}) collective-permute-start(f32[16,16,128]{2,1,0:T(8,128)S(1)} %add.20), channel_id=1, source_target_pairs={{0,2},{1,3},{2,0},{3,1},{4,6},{5,7},{6,4},{7,5},{8,10},{9,11},{10,... | collective-permute-start | bytes 393224 | tf_op jit(solution)/shard_map/ppermute | solution.py:22
  185.1 18.4 %copy-start.2 = (f32[128,4096]{1,0:T(8,128)S(1)}, f32[128,4096]{1,0:T(8,128)}, u32[]{:S(2)}) copy-start(f32[128,4096]{1,0:T(8,128)} %q.1) | copy-start | bytes 6291460
  185.1 8.5 %collective-permute-start.19 = (f32[16,16,128]{2,1,0:T(8,128)S(1)}, f32[16,16,128]{2,1,0:T(8,128)S(1)}, u32[]{:S(2)}, u32[]{:S(2)}) collective-permute-start(f32[16,16,128]{2,1,0:T(8,128)S(1)} %add.21), channel_id=1, source_target_pairs={{0,4},{1,5},{2,6},{3,7},{4,0},{5,1},{6,2},{7,3},{8,12},{9,13},{10,... | collective-permute-start | bytes 393224 | tf_op jit(solution)/shard_map/ppermute | solution.py:22
  193.7 8.4 %collective-permute-start.20 = (f32[16,16,128]{2,1,0:T(8,128)S(1)}, f32[16,16,128]{2,1,0:T(8,128)S(1)}, u32[]{:S(2)}, u32[]{:S(2)}) collective-permute-start(f32[16,16,128]{2,1,0:T(8,128)S(1)} %add.22), channel_id=1, source_target_pairs={{0,8},{1,9},{2,10},{3,11},{4,12},{5,13},{6,14},{7,15},{8,0},{9,1},... | collective-permute-start | bytes 393224 | tf_op jit(solution)/shard_map/ppermute | solution.py:22
  202.1 1.4 collective-permute-start.21
  202.2 9.4 %copy-start.1 = (bf16[64,8192]{1,0:T(8,128)(2,1)S(1)}, bf16[64,8192]{1,0:T(8,128)(2,1)}, u32[]{:S(2)}) copy-start(bf16[64,8192]{1,0:T(8,128)(2,1)} %param.12) | copy-start | bytes 3145732
  (10 other events, 16.7 us)

commit v4 on v3

--- a/solution.py
+++ b/solution.py
@@ -178,7 +178,6 @@
     edge = (place == 0) | (place == 3)
     pairs = [(0, 1), (1, 0), (2, 3), (3, 2)]
     middle = [(1, 2), (2, 1)]
-    ends = [(1, 0), (2, 3)]
 
     def across(block):
         return swap(block, 2, 16)
@@ -193,13 +192,13 @@
     g0, g1 = by_device(gate, inner, 16, parts)
     near, mid, y0, c0, g0, g1 = fence(near, mid, y0, c0, g0, g1)
 
-    mid_far, out_mid, y1 = line(near, middle), line(mid, ends), across(near)
+    mid_far, out_mid, y1 = line(near, middle), line(mid, pairs), across(near)
     c1, cy0 = core(near), core(y0)
     h0 = hidden_chunk((rows, c0, y0, cy0), weight)
     mid_far, out_mid, near, mid, y1, c1, h0, g0, g1 = fence(mid_far, out_mid, near, mid, y1, c1, h0, g0, g1)
 
     slot2 = jnp.where(edge, out_mid, mid_far)
-    out_far, y2 = line(mid_far, ends), across(slot2)
+    out_far, y2 = line(mid_far, pairs), across(slot2)
     c2, cy1 = core(slot2), core(y1)
     h1 = hidden_chunk((near, c1, y1, cy1), weight)
     h1, g0 = fence(h1, g0)

time: 213 us -> 210 us (0.986)
  waiting for transfers between devices: 70.5 us -> 65.3 us
  starting transfers between devices: 38.1 us -> 40.3 us
    ppermute x5, starting transfers between devices: 7.88 us -> 12.2 us  [line(): lax.ppermute(block, AXIS, [(4 * a + i, 4 * b + i) for a, b in pairs for i...]
    ppermute x17, waiting for transfers between devices: 40.5 us -> 37.1 us  [swap(): return lax.ppermute(block, AXIS, [(i, i ^ bit) for i in range(count)])]
  transfers between devices with their start and end apart: 24 -> 24, of which waited for: 12 -> 11; matrix products, arithmetic and copies ran while one was open for 3% -> 3% of each run, Pallas kernels for 35% -> 36%
where the time goes in v4:
time: 210 us; the launch traced here: 209 us
  Pallas kernels  88.1 us (42%)
  waiting for transfers between devices  65.3 us (31%)
  starting transfers between devices  40.3 us (19%)
  local copies, waits for them, and re-layouts  8.65 us (4%)
  other arithmetic  4.46 us (2%)
    pallas_call x4, Pallas kernels, hidden_chunk(): pl.pallas_call(body, grid=(width // tile,), out_shape=jax.ShapeDtypeStruc...  66 us
    ppermute x17, waiting for transfers between devices, swap(): return lax.ppermute(block, AXIS, [(i, i ^ bit) for i in range(count)])  37.1 us
    ppermute x17, starting transfers between devices, swap(): return lax.ppermute(block, AXIS, [(i, i ^ bit) for i in range(count)])  18.9 us
    ppermute x5, waiting for transfers between devices, line(): lax.ppermute(block, AXIS, [(4 * a + i, 4 * b + i) for a, b in pairs for i...  16 us
    all_to_all x2, waiting for transfers between devices, exchange(): return lax.all_to_all(block, AXIS, split_axis=0, concat_axis=0, tiled=True)  12.3 us
    ppermute x5, starting transfers between devices, line(): lax.ppermute(block, AXIS, [(4 * a + i, 4 * b + i) for a, b in pairs for i...  12.2 us
    pallas_call x2, Pallas kernels, project(): pl.pallas_call(body, grid=(columns // tile,), out_shape=[jax.ShapeDtypeSt...  9.33 us
    all_to_all x2, starting transfers between devices, exchange(): return lax.all_to_all(block, AXIS, split_axis=0, concat_axis=0, tiled=True)  9.14 us
  transfers between devices with their start and end apart: 24, of which 11 were waited for; matrix products, arithmetic and copies ran while one was open for 3% of the time, Pallas kernels for 36%

profile of v4, /device:TPU:0, one launch (start us, length us, event | category | flops | bytes accessed | tf_op | source)
XLA Modules:
  0.0 208.7 jit_solution(3655739308368428641)
XLA Ops:
  0.0 3.0 %collective-permute-start = (bf16[56,8192]{1,0:T(8,128)(2,1)}, bf16[56,8192]{1,0:T(8,128)(2,1)S(1)}, u32[]{:S(2)}, u32[]{:S(2)}) collective-permute-start(bf16[56,8192]{1,0:T(8,128)(2,1)} %refs_0_.1), channel_id=1, source_target_pairs={{0,4},{1,5},{2,6},{3,7},{4,0},{5,1},{6,2},{7,3},{8,12},{9,13},{10,... | collective-permute-start | bytes 2752520 | tf_op jit(solution)/shard_map/ppermute | solution.py:26
  3.7 1.6 collective-permute-start.2
  5.3 1.6 reduce-precision_convert_fusion
  7.6 4.7 %by_device.1 = (bf16[16,56,896]{2,1,0:T(8,128)(2,1)}, bf16[16,56,1024]{2,1,0:T(8,128)(2,1)}) custom-call(bf16[56,28672]{1,0:T(8,128)(2,1)} %g.1, bf16[56,128]{1,0:T(8,128)(2,1)} %pad_maximum_fusion.own), custom_call_target="tpu_custom_call" | custom-call | flops 1 | bytes 1 | tf_op jit(solution)/shard_map/by_device/pallas_call | solution.py:64
  12.3 11.2 %collective-permute-done.refs_0_ = bf16[56,8192]{1,0:T(8,128)(2,1)S(1)} collective-permute-done((bf16[56,8192]{1,0:T(8,128)(2,1)}, bf16[56,8192]{1,0:T(8,128)(2,1)S(1)}, u32[]{:S(2)}, u32[]{:S(2)}) %collective-permute-start) | collective-permute-done | bytes 917536 | tf_op jit(solution)/shard_map/ppermute | solution.py:26
  23.6 2.3 %collective-permute-done.2.refs_2_ = bf16[56,8192]{1,0:T(8,128)(2,1)} collective-permute-done((bf16[56,8192]{1,0:T(8,128)(2,1)}, bf16[56,8192]{1,0:T(8,128)(2,1)}, u32[]{:S(2)}, u32[]{:S(2)}) %collective-permute-start.2) | collective-permute-done | bytes 917536 | tf_op jit(solution)/shard_map/ppermute | solution.py:22
  26.0 1.6 collective-permute-start.4
  27.6 1.5 collective-permute-start.6
  29.4 5.2 %collective-permute-start.5 = (bf16[56,8192]{1,0:T(8,128)(2,1)}, bf16[56,8192]{1,0:T(8,128)(2,1)S(1)}, u32[]{:S(2)}, u32[]{:S(2)}) collective-permute-start(bf16[56,8192]{1,0:T(8,128)(2,1)} %get-tuple-element.41.refs_3_), channel_id=1, source_target_pairs={{0,4},{1,5},{2,6},{3,7},{4,0},{5,1},{6,2},{7,3},{8,12},{9,13},{10,... | collective-permute-start | bytes 2752520 | tf_op jit(solution)/shard_map/ppermute | solution.py:26
  34.5 16.5 %hidden_chunk.4.refs_6_ = f32[256,1792]{1,0:T(8,128)} custom-call(bf16[56,8192]{1,0:T(8,128)(2,1)} %refs_0_.1, bf16[56,8192]{1,0:T(8,128)(2,1)} %get-tuple-element.42.refs_1_, bf16[56,8192]{1,0:T(8,128)(2,1)} %get-tuple-element.43.refs_2_, bf16[56,8192]{1,0:T(8,128)(2,1)} %collective-permute-done.8.refs_3_, bf16[1792,8192]{1,0:T(8,128)(2,1)} %refs_4_.7), custom_call_target="tpu_custom_call" | custom-call | flops 1 | bytes 1 | tf_op jit(solution)/shard_map/hidden_chunk/pallas_call | solution.py:93
  51.0 4.7 %collective-permute-done.5.refs_1_ = bf16[56,8192]{1,0:T(8,128)(2,1)S(1)} collective-permute-done((bf16[56,8192]{1,0:T(8,128)(2,1)}, bf16[56,8192]{1,0:T(8,128)(2,1)S(1)}, u32[]{:S(2)}, u32[]{:S(2)}) %collective-permute-start.5) | collective-permute-done | bytes 917536 | tf_op jit(solution)/shard_map/ppermute | solution.py:26
  56.7 1.3 broadcast_select_fusion.1.refs_2_
  58.8 1.7 collective-permute-start.10
  61.4 16.5 %hidden_chunk.5.refs_0_ = f32[256,1792]{1,0:T(8,128)} custom-call(bf16[56,8192]{1,0:T(8,128)(2,1)} %get-tuple-element.47.refs_0_, bf16[56,8192]{1,0:T(8,128)(2,1)} %get-tuple-element.48.refs_1_, bf16[56,8192]{1,0:T(8,128)(2,1)} %get-tuple-element.49.refs_2_, bf16[56,8192]{1,0:T(8,128)(2,1)} %copy-done.14, bf16[1792,8192]{1,0:T(8,128)(2,1)} %refs_4_.7), custom_call_target="tpu_custom_call" | custom-call | flops 1 | bytes 1 | tf_op jit(solution)/shard_map/hidden_chunk/pallas_call | solution.py:93
  78.0 4.4 %all-to-all-start = ((bf16[16,56,896]{2,1,0:T(8,128)(2,1)}), bf16[16,56,896]{2,1,0:T(8,128)(2,1)S(1)}, u32[]{:S(2)}, u32[]{:S(2)}) async-start(bf16[16,56,896]{2,1,0:T(8,128)(2,1)} %get-tuple-element.61), calls=%async_computation | async-start | bytes 3211264 | tf_op jit(solution)/shard_map/all_to_all | solution.py:189
  82.8 1.3 broadcast_select_fusion.refs_0_
  84.1 1.7 collective-permute-start.13
  86.9 16.5 %hidden_chunk.6.refs_3_ = f32[256,1792]{1,0:T(8,128)} custom-call(bf16[56,8192]{1,0:T(8,128)(2,1)} %get-tuple-element.58.refs_0_, bf16[56,8192]{1,0:T(8,128)(2,1)} %get-tuple-element.59.refs_1_, bf16[56,8192]{1,0:T(8,128)(2,1)} %get-tuple-element.60.refs_2_, bf16[56,8192]{1,0:T(8,128)(2,1)} %copy-done.15, bf16[1792,8192]{1,0:T(8,128)(2,1)} %refs_4_.7), custom_call_target="tpu_custom_call" | custom-call | flops 1 | bytes 1 | tf_op jit(solution)/shard_map/hidden_chunk/pallas_call | solution.py:93
  103.4 18.9 %collective-permute-done.13.refs_1_ = bf16[56,8192]{1,0:T(8,128)(2,1)S(1)} collective-permute-done((bf16[56,8192]{1,0:T(8,128)(2,1)S(1)}, bf16[56,8192]{1,0:T(8,128)(2,1)S(1)}, u32[]{:S(2)}, u32[]{:S(2)}) %collective-permute-start.13) | collective-permute-done | bytes 917536 | tf_op jit(solution)/shard_map/ppermute | solution.py:22
  124.5 4.8 %all-to-all-start.1 = ((bf16[16,56,1024]{2,1,0:T(8,128)(2,1)}), bf16[16,56,1024]{2,1,0:T(8,128)(2,1)S(1)}, u32[]{:S(2)}, u32[]{:S(2)}) async-start(bf16[16,56,1024]{2,1,0:T(8,128)(2,1)} %get-tuple-element.67), calls=%async_computation.1 | async-start | bytes 3670016 | tf_op jit(solution)/shard_map/all_to_all | solution.py:189
  130.3 1.6 collective-permute-done.16.refs_3_
  132.8 16.5 %hidden_chunk.7.refs_3_ = f32[256,1792]{1,0:T(8,128)} custom-call(bf16[56,8192]{1,0:T(8,128)(2,1)} %get-tuple-element.64.refs_0_, bf16[56,8192]{1,0:T(8,128)(2,1)} %get-tuple-element.65.refs_1_, bf16[56,8192]{1,0:T(8,128)(2,1)} %get-tuple-element.66.refs_2_, bf16[56,8192]{1,0:T(8,128)(2,1)} %copy-done.16, bf16[1792,8192]{1,0:T(8,128)(2,1)} %refs_4_.7), custom_call_target="tpu_custom_call" | custom-call | flops 1 | bytes 1 | tf_op jit(solution)/shard_map/hidden_chunk/pallas_call | solution.py:93
  149.3 4.2 %project.2.refs_6_ = f32[1024,64]{1,0:T(8,128)} custom-call(f32[256,1792]{1,0:T(8,128)} %get-tuple-element.46.refs_0_, f32[256,1792]{1,0:T(8,128)} %get-tuple-element.51.refs_1_, f32[256,1792]{1,0:T(8,128)} %get-tuple-element.63.refs_2_, f32[256,1792]{1,0:T(8,128)} %hidden_chunk.7.refs_3_, bf16[16,56,896]{2,1,0:T(8,128)(2,1)} %get-tuple-element.68.refs_4_, ...), custom_call_target="tpu_custom_call" | custom-call | flops 1 | bytes 1 | tf_op jit(solution)/shard_map/project/pallas_call | solution.py:153
  153.5 12.3 %all-to-all-done.1.refs_4_ = bf16[16,56,1024]{2,1,0:T(8,128)(2,1)S(1)} async-done(((bf16[16,56,1024]{2,1,0:T(8,128)(2,1)}), bf16[16,56,1024]{2,1,0:T(8,128)(2,1)S(1)}, u32[]{:S(2)}, u32[]{:S(2)}) %all-to-all-start.1) | async-done | bytes 1835040 | tf_op jit(solution)/shard_map/all_to_all | solution.py:189
  167.1 5.1 %project.3 = (f32[16,16,128]{2,1,0:T(8,128)}, f32[16,16,128]{2,1,0:T(8,128)}) custom-call(f32[256,1792]{1,0:T(8,128)} %get-tuple-element.46.refs_0_, f32[256,1792]{1,0:T(8,128)} %get-tuple-element.51.refs_1_, f32[256,1792]{1,0:T(8,128)} %get-tuple-element.63.refs_2_, f32[256,1792]{1,0:T(8,128)} %hidden_chunk.7.refs_3_, bf16[16,56,1024]{2,1,0:T(8,128)(2,1)} %copy-done.8, ...), custom_call_target="tpu_custom_call" | custom-call | flops 1 | bytes 1 | tf_op jit(solution)/shard_map/project/pallas_call | solution.py:153
  175.1 3.1 %collective-permute-start.18 = (f32[16,16,128]{2,1,0:T(8,128)S(1)}, f32[16,16,128]{2,1,0:T(8,128)S(1)}, u32[]{:S(2)}, u32[]{:S(2)}) collective-permute-start(f32[16,16,128]{2,1,0:T(8,128)S(1)} %add.20), channel_id=1, source_target_pairs={{0,2},{1,3},{2,0},{3,1},{4,6},{5,7},{6,4},{7,5},{8,10},{9,11},{10,... | collective-permute-start | bytes 393224 | tf_op jit(solution)/shard_map/ppermute | solution.py:22
  178.2 4.0 %collective-permute-done.18 = f32[16,16,128]{2,1,0:T(8,128)S(1)} collective-permute-done((f32[16,16,128]{2,1,0:T(8,128)S(1)}, f32[16,16,128]{2,1,0:T(8,128)S(1)}, u32[]{:S(2)}, u32[]{:S(2)}) %collective-permute-start.18) | collective-permute-done | bytes 131104 | tf_op jit(solution)/shard_map/ppermute | solution.py:22
  182.2 5.1 %collective-permute-start.19 = (f32[16,16,128]{2,1,0:T(8,128)S(1)}, f32[16,16,128]{2,1,0:T(8,128)S(1)}, u32[]{:S(2)}, u32[]{:S(2)}) collective-permute-start(f32[16,16,128]{2,1,0:T(8,128)S(1)} %add.21), channel_id=1, source_target_pairs={{0,4},{1,5},{2,6},{3,7},{4,0},{5,1},{6,2},{7,3},{8,12},{9,13},{10,... | collective-permute-start | bytes 393224 | tf_op jit(solution)/shard_map/ppermute | solution.py:22
  187.3 3.5 %collective-permute-done.19 = f32[16,16,128]{2,1,0:T(8,128)S(1)} collective-permute-done((f32[16,16,128]{2,1,0:T(8,128)S(1)}, f32[16,16,128]{2,1,0:T(8,128)S(1)}, u32[]{:S(2)}, u32[]{:S(2)}) %collective-permute-start.19) | collective-permute-done | bytes 131104 | tf_op jit(solution)/shard_map/ppermute | solution.py:22
  190.8 3.0 %collective-permute-start.20 = (f32[16,16,128]{2,1,0:T(8,128)S(1)}, f32[16,16,128]{2,1,0:T(8,128)S(1)}, u32[]{:S(2)}, u32[]{:S(2)}) collective-permute-start(f32[16,16,128]{2,1,0:T(8,128)S(1)} %add.22), channel_id=1, source_target_pairs={{0,8},{1,9},{2,10},{3,11},{4,12},{5,13},{6,14},{7,15},{8,0},{9,1},... | collective-permute-start | bytes 393224 | tf_op jit(solution)/shard_map/ppermute | solution.py:22
  194.8 4.4 %collective-permute-done.20 = f32[16,16,128]{2,1,0:T(8,128)S(1)} collective-permute-done((f32[16,16,128]{2,1,0:T(8,128)S(1)}, f32[16,16,128]{2,1,0:T(8,128)S(1)}, u32[]{:S(2)}, u32[]{:S(2)}) %collective-permute-start.20) | collective-permute-done | bytes 131104 | tf_op jit(solution)/shard_map/ppermute | solution.py:22
  200.6 8.0 %finish.1 = f32[64,128]{1,0:T(8,128)} custom-call(f32[16,16,128]{2,1,0:T(8,128)S(1)} %add.23.own, f32[16,16,128]{2,1,0:T(8,128)S(1)} %collective-permute-done.21.other, f32[16,64,64]{2,1,0:T(8,128)S(1)} %slice_add_fusion.i, f32[128,4096]{1,0:T(8,128)S(1)} %copy-done.2), custom_call_target="tpu_custom_call" | custom-call | tf_op jit(solution)/shard_map/finish/pallas_call | solution.py:303
  (78 shorter events, 16.6 us)
Async XLA Ops:
  0.0 5.3 %copy-start = (bf16[64,8192]{1,0:T(8,128)(2,1)S(1)}, bf16[64,8192]{1,0:T(8,128)(2,1)}, u32[]{:S(2)}) copy-start(bf16[64,8192]{1,0:T(8,128)(2,1)} %param.12) | copy-start | bytes 3145732
  0.0 23.6 %collective-permute-start = (bf16[56,8192]{1,0:T(8,128)(2,1)}, bf16[56,8192]{1,0:T(8,128)(2,1)S(1)}, u32[]{:S(2)}, u32[]{:S(2)}) collective-permute-start(bf16[56,8192]{1,0:T(8,128)(2,1)} %refs_0_.1), channel_id=1, source_target_pairs={{0,4},{1,5},{2,6},{3,7},{4,0},{5,1},{6,2},{7,3},{8,12},{9,13},{10,... | collective-permute-start | bytes 2752520 | tf_op jit(solution)/shard_map/ppermute | solution.py:26
  3.0 20.6 %collective-permute-start.1 = (bf16[56,8192]{1,0:T(8,128)(2,1)}, bf16[56,8192]{1,0:T(8,128)(2,1)S(1)}, u32[]{:S(2)}, u32[]{:S(2)}) collective-permute-start(bf16[56,8192]{1,0:T(8,128)(2,1)} %refs_0_.1), channel_id=1, source_target_pairs={{4,8},{5,9},{6,10},{7,11},{8,4},{9,5},{10,6},{11,7},{20,24},{21,25... | collective-permute-start | bytes 2752520 | tf_op jit(solution)/shard_map/ppermute | solution.py:26
  3.7 22.2 %collective-permute-start.2 = (bf16[56,8192]{1,0:T(8,128)(2,1)}, bf16[56,8192]{1,0:T(8,128)(2,1)}, u32[]{:S(2)}, u32[]{:S(2)}) collective-permute-start(bf16[56,8192]{1,0:T(8,128)(2,1)} %refs_0_.1), channel_id=1, source_target_pairs={{0,2},{1,3},{2,0},{3,1},{4,6},{5,7},{6,4},{7,5},{8,10},{9,11},{10,... | collective-permute-start | bytes 2752520 | tf_op jit(solution)/shard_map/ppermute | solution.py:22
  5.3 20.6 %collective-permute-start.3 = (bf16[56,8192]{1,0:T(8,128)(2,1)}, bf16[56,8192]{1,0:T(8,128)(2,1)}, u32[]{:S(2)}, u32[]{:S(2)}) collective-permute-start(bf16[56,8192]{1,0:T(8,128)(2,1)} %refs_0_.1), channel_id=1, source_target_pairs={{0,1},{1,0},{2,3},{3,2},{4,5},{5,4},{6,7},{7,6},{8,9},{9,8},{10,11... | collective-permute-start | bytes 2752520 | tf_op jit(solution)/shard_map/ppermute | solution.py:22
  26.0 8.6 %collective-permute-start.8 = (bf16[56,8192]{1,0:T(8,128)(2,1)}, bf16[56,8192]{1,0:T(8,128)(2,1)}, u32[]{:S(2)}, u32[]{:S(2)}) collective-permute-start(bf16[56,8192]{1,0:T(8,128)(2,1)} %get-tuple-element.43.refs_2_), channel_id=1, source_target_pairs={{0,1},{1,0},{2,3},{3,2},{4,5},{5,4},{6,7},{7,6},{8,9},{9,8},{10,11... | collective-permute-start | bytes 2752520 | tf_op jit(solution)/shard_map/ppermute | solution.py:22
  26.0 25.0 %collective-permute-start.4 = (bf16[56,8192]{1,0:T(8,128)(2,1)}, bf16[56,8192]{1,0:T(8,128)(2,1)}, u32[]{:S(2)}, u32[]{:S(2)}) collective-permute-start(bf16[56,8192]{1,0:T(8,128)(2,1)} %get-tuple-element.40.refs_2_), channel_id=1, source_target_pairs={{4,8},{5,9},{6,10},{7,11},{8,4},{9,5},{10,6},{11,7},{20,24},{21,25... | collective-permute-start | bytes 2752520 | tf_op jit(solution)/shard_map/ppermute | solution.py:26
  27.6 23.4 %collective-permute-start.6 = (bf16[56,8192]{1,0:T(8,128)(2,1)}, bf16[56,8192]{1,0:T(8,128)(2,1)S(1)}, u32[]{:S(2)}, u32[]{:S(2)}) collective-permute-start(bf16[56,8192]{1,0:T(8,128)(2,1)} %get-tuple-element.40.refs_2_), channel_id=1, source_target_pairs={{0,2},{1,3},{2,0},{3,1},{4,6},{5,7},{6,4},{7,5},{8,10},{9,11},{10,... | collective-permute-start | bytes 2752520 | tf_op jit(solution)/shard_map/ppermute | solution.py:22
  29.1 21.9 %collective-permute-start.7 = (bf16[56,8192]{1,0:T(8,128)(2,1)}, bf16[56,8192]{1,0:T(8,128)(2,1)S(1)}, u32[]{:S(2)}, u32[]{:S(2)}) collective-permute-start(bf16[56,8192]{1,0:T(8,128)(2,1)} %get-tuple-element.40.refs_2_), channel_id=1, source_target_pairs={{0,1},{1,0},{2,3},{3,2},{4,5},{5,4},{6,7},{7,6},{8,9},{9,8},{10,11... | collective-permute-start | bytes 2752520 | tf_op jit(solution)/shard_map/ppermute | solution.py:22
  29.4 26.4 %collective-permute-start.5 = (bf16[56,8192]{1,0:T(8,128)(2,1)}, bf16[56,8192]{1,0:T(8,128)(2,1)S(1)}, u32[]{:S(2)}, u32[]{:S(2)}) collective-permute-start(bf16[56,8192]{1,0:T(8,128)(2,1)} %get-tuple-element.41.refs_3_), channel_id=1, source_target_pairs={{0,4},{1,5},{2,6},{3,7},{4,0},{5,1},{6,2},{7,3},{8,12},{9,13},{10,... | collective-permute-start | bytes 2752520 | tf_op jit(solution)/shard_map/ppermute | solution.py:26
  51.0 4.7 %copy-start.10 = (bf16[56,8192]{1,0:T(8,128)(2,1)}, bf16[56,8192]{1,0:T(8,128)(2,1)S(1)}, u32[]{:S(2)}) copy-start(bf16[56,8192]{1,0:T(8,128)(2,1)S(1)} %collective-permute-done.6.refs_4_) | copy-start | bytes 2752516
  56.7 3.8 %collective-permute-start.9 = (bf16[56,8192]{1,0:T(8,128)(2,1)}, bf16[56,8192]{1,0:T(8,128)(2,1)S(1)}, u32[]{:S(2)}, u32[]{:S(2)}) collective-permute-start(bf16[56,8192]{1,0:T(8,128)(2,1)} %get-tuple-element.49.refs_2_), channel_id=1, source_target_pairs={{0,1},{1,0},{2,3},{3,2},{4,5},{5,4},{6,7},{7,6},{8,9},{9,8},{10,11... | collective-permute-start | bytes 2752520 | tf_op jit(solution)/shard_map/ppermute | solution.py:22
  57.9 20.0 %copy-start.5 = (bf16[56,8192]{1,0:T(8,128)(2,1)}, bf16[56,8192]{1,0:T(8,128)(2,1)S(1)}, u32[]{:S(2)}) copy-start(bf16[56,8192]{1,0:T(8,128)(2,1)S(1)} %broadcast_select_fusion.1.refs_2_) | copy-start | bytes 2752516
  58.0 24.4 %collective-permute-start.11 = (bf16[56,8192]{1,0:T(8,128)(2,1)S(1)}, bf16[56,8192]{1,0:T(8,128)(2,1)}, u32[]{:S(2)}, u32[]{:S(2)}) collective-permute-start(bf16[56,8192]{1,0:T(8,128)(2,1)S(1)} %broadcast_select_fusion.1.refs_2_), channel_id=1, source_target_pairs={{0,2},{1,3},{2,0},{3,1},{4,6},{5,7},{6,4},{7,5},{8,10},{9,11},{10,... | collective-permute-start | bytes 2752520 | tf_op jit(solution)/shard_map/ppermute | solution.py:22
  58.5 23.8 %collective-permute-start.12 = (bf16[56,8192]{1,0:T(8,128)(2,1)S(1)}, bf16[56,8192]{1,0:T(8,128)(2,1)}, u32[]{:S(2)}, u32[]{:S(2)}) collective-permute-start(bf16[56,8192]{1,0:T(8,128)(2,1)S(1)} %broadcast_select_fusion.1.refs_2_), channel_id=1, source_target_pairs={{0,1},{1,0},{2,3},{3,2},{4,5},{5,4},{6,7},{7,6},{8,9},{9,8},{10,11... | collective-permute-start | bytes 2752520 | tf_op jit(solution)/shard_map/ppermute | solution.py:22
  58.8 23.6 %collective-permute-start.10 = (bf16[56,8192]{1,0:T(8,128)(2,1)}, bf16[56,8192]{1,0:T(8,128)(2,1)}, u32[]{:S(2)}, u32[]{:S(2)}) collective-permute-start(bf16[56,8192]{1,0:T(8,128)(2,1)} %get-tuple-element.52), channel_id=1, source_target_pairs={{0,4},{1,5},{2,6},{3,7},{4,0},{5,1},{6,2},{7,3},{8,12},{9,13},{10,... | collective-permute-start | bytes 2752520 | tf_op jit(solution)/shard_map/ppermute | solution.py:26
  78.0 45.3 %all-to-all-start = ((bf16[16,56,896]{2,1,0:T(8,128)(2,1)}), bf16[16,56,896]{2,1,0:T(8,128)(2,1)S(1)}, u32[]{:S(2)}, u32[]{:S(2)}) async-start(bf16[16,56,896]{2,1,0:T(8,128)(2,1)} %get-tuple-element.61), calls=%async_computation | async-start | bytes 3211264 | tf_op jit(solution)/shard_map/all_to_all | solution.py:189
  82.4 3.6 %collective-permute-start.15 = (bf16[56,8192]{1,0:T(8,128)(2,1)}, bf16[56,8192]{1,0:T(8,128)(2,1)S(1)}, u32[]{:S(2)}, u32[]{:S(2)}) collective-permute-start(bf16[56,8192]{1,0:T(8,128)(2,1)} %get-tuple-element.60.refs_2_), channel_id=1, source_target_pairs={{0,1},{1,0},{2,3},{3,2},{4,5},{5,4},{6,7},{7,6},{8,9},{9,8},{10,11... | collective-permute-start | bytes 2752520 | tf_op jit(solution)/shard_map/ppermute | solution.py:22
  84.1 19.3 %copy-start.7 = (bf16[56,8192]{1,0:T(8,128)(2,1)}, bf16[56,8192]{1,0:T(8,128)(2,1)S(1)}, u32[]{:S(2)}) copy-start(bf16[56,8192]{1,0:T(8,128)(2,1)S(1)} %broadcast_select_fusion.refs_0_) | copy-start | bytes 2752516
  84.1 38.2 %collective-permute-start.13 = (bf16[56,8192]{1,0:T(8,128)(2,1)S(1)}, bf16[56,8192]{1,0:T(8,128)(2,1)S(1)}, u32[]{:S(2)}, u32[]{:S(2)}) collective-permute-start(bf16[56,8192]{1,0:T(8,128)(2,1)S(1)} %broadcast_select_fusion.refs_0_), channel_id=1, source_target_pairs={{0,2},{1,3},{2,0},{3,1},{4,6},{5,7},{6,4},{7,5},{8,10},{9,11},{10,... | collective-permute-start | bytes 2752520 | tf_op jit(solution)/shard_map/ppermute | solution.py:22
  85.9 37.4 %collective-permute-start.14 = (bf16[56,8192]{1,0:T(8,128)(2,1)S(1)}, bf16[56,8192]{1,0:T(8,128)(2,1)}, u32[]{:S(2)}, u32[]{:S(2)}) collective-permute-start(bf16[56,8192]{1,0:T(8,128)(2,1)S(1)} %broadcast_select_fusion.refs_0_), channel_id=1, source_target_pairs={{0,1},{1,0},{2,3},{3,2},{4,5},{5,4},{6,7},{7,6},{8,9},{9,8},{10,11... | collective-permute-start | bytes 2752520 | tf_op jit(solution)/shard_map/ppermute | solution.py:22
  124.5 4.8 %copy-start.13 = (bf16[56,8192]{1,0:T(8,128)(2,1)S(1)}, bf16[56,8192]{1,0:T(8,128)(2,1)}, u32[]{:S(2)}) copy-start(bf16[56,8192]{1,0:T(8,128)(2,1)} %get-tuple-element.66.refs_2_) | copy-start | bytes 2752516
  124.5 5.3 %copy-start.17 = (s32[1,4]{1,0:T(1,128)S(1)}, s32[1,4]{1,0:T(1,128)}, u32[]{:S(2)}) copy-start(s32[1,4]{1,0:T(1,128)} %param.14) | copy-start | bytes 52
  124.5 41.3 %all-to-all-start.1 = ((bf16[16,56,1024]{2,1,0:T(8,128)(2,1)}), bf16[16,56,1024]{2,1,0:T(8,128)(2,1)S(1)}, u32[]{:S(2)}, u32[]{:S(2)}) async-start(bf16[16,56,1024]{2,1,0:T(8,128)(2,1)} %get-tuple-element.67), calls=%async_computation.1 | async-start | bytes 3670016 | tf_op jit(solution)/shard_map/all_to_all | solution.py:189
  129.3 2.6 %collective-permute-start.16 = (bf16[56,8192]{1,0:T(8,128)(2,1)S(1)}, bf16[56,8192]{1,0:T(8,128)(2,1)S(1)}, u32[]{:S(2)}, u32[]{:S(2)}) collective-permute-start(bf16[56,8192]{1,0:T(8,128)(2,1)S(1)} %copy-done.13), channel_id=1, source_target_pairs={{0,1},{1,0},{2,3},{3,2},{4,5},{5,4},{6,7},{7,6},{8,9},{9,8},{10,11... | collective-permute-start | bytes 2752520 | tf_op jit(solution)/shard_map/ppermute | solution.py:22
  172.2 2.0 collective-permute-start.17
  175.1 7.1 %collective-permute-start.18 = (f32[16,16,128]{2,1,0:T(8,128)S(1)}, f32[16,16,128]{2,1,0:T(8,128)S(1)}, u32[]{:S(2)}, u32[]{:S(2)}) collective-permute-start(f32[16,16,128]{2,1,0:T(8,128)S(1)} %add.20), channel_id=1, source_target_pairs={{0,2},{1,3},{2,0},{3,1},{4,6},{5,7},{6,4},{7,5},{8,10},{9,11},{10,... | collective-permute-start | bytes 393224 | tf_op jit(solution)/shard_map/ppermute | solution.py:22
  182.2 18.4 %copy-start.2 = (f32[128,4096]{1,0:T(8,128)S(1)}, f32[128,4096]{1,0:T(8,128)}, u32[]{:S(2)}) copy-start(f32[128,4096]{1,0:T(8,128)} %q.1) | copy-start | bytes 6291460
  182.2 8.5 %collective-permute-start.19 = (f32[16,16,128]{2,1,0:T(8,128)S(1)}, f32[16,16,128]{2,1,0:T(8,128)S(1)}, u32[]{:S(2)}, u32[]{:S(2)}) collective-permute-start(f32[16,16,128]{2,1,0:T(8,128)S(1)} %add.21), channel_id=1, source_target_pairs={{0,4},{1,5},{2,6},{3,7},{4,0},{5,1},{6,2},{7,3},{8,12},{9,13},{10,... | collective-permute-start | bytes 393224 | tf_op jit(solution)/shard_map/ppermute | solution.py:22
  190.8 8.4 %collective-permute-start.20 = (f32[16,16,128]{2,1,0:T(8,128)S(1)}, f32[16,16,128]{2,1,0:T(8,128)S(1)}, u32[]{:S(2)}, u32[]{:S(2)}) collective-permute-start(f32[16,16,128]{2,1,0:T(8,128)S(1)} %add.22), channel_id=1, source_target_pairs={{0,8},{1,9},{2,10},{3,11},{4,12},{5,13},{6,14},{7,15},{8,0},{9,1},... | collective-permute-start | bytes 393224 | tf_op jit(solution)/shard_map/ppermute | solution.py:22
  199.2 1.4 collective-permute-start.21
  199.3 9.4 %copy-start.1 = (bf16[64,8192]{1,0:T(8,128)(2,1)S(1)}, bf16[64,8192]{1,0:T(8,128)(2,1)}, u32[]{:S(2)}) copy-start(bf16[64,8192]{1,0:T(8,128)(2,1)} %param.12) | copy-start | bytes 3145732
  (10 other events, 16.6 us)

commit v5 on v4

--- a/solution.py
+++ b/solution.py
@@ -73,9 +73,10 @@
     )(gate, inner)
 
 
-def hidden_chunk(blocks, weight, tile=256):
+def hidden_chunk(blocks, weight, start=0, columns=None, tile=256):
     rows, depth = blocks[0].shape
-    width = weight.shape[0]
+    width = columns or weight.shape[0]
+    skip = start // tile
     count = len(blocks)
 
     def body(*refs):
@@ -95,7 +96,7 @@
         grid=(width // tile,),
         out_shape=jax.ShapeDtypeStruct((64 * count, width), jnp.float32),
         in_specs=[pl.BlockSpec((rows, depth), lambda j: (0, 0), pipeline_mode=pl.Buffered(1))] * count
-        + [pl.BlockSpec((tile, depth), lambda j: (j, 0))],
+        + [pl.BlockSpec((tile, depth), lambda j: (j + skip, 0))],
         out_specs=pl.BlockSpec((64 * count, tile), lambda j: (0, j)),
         scratch_shapes=[pltpu.VMEM((64 * count, depth), jnp.bfloat16)],
         compiler_params=pltpu.CompilerParams(vmem_limit_bytes=VMEM_LIMIT),
@@ -154,7 +155,9 @@
         body,
         grid=(columns // tile,),
         out_shape=[jax.ShapeDtypeStruct(shape, jnp.float32) for shape in shapes],
-        in_specs=[pl.BlockSpec((256, tile), lambda j: (0, j + skip))] * slots
+        in_specs=[
+            pl.BlockSpec((256, tile), lambda j, at=skip if h.shape[1] > columns else 0: (0, j + at)) for h in hiddens
+        ]
         + [
             pl.BlockSpec((count, rows, tile), lambda j: (0, 0, j)),
             pl.BlockSpec((heads, tile), lambda j: (0, j + skip)),
@@ -200,24 +203,24 @@
     slot2 = jnp.where(edge, out_mid, mid_far)
     out_far, y2 = line(mid_far, pairs), across(slot2)
     c2, cy1 = core(slot2), core(y1)
-    h1 = hidden_chunk((near, c1, y1, cy1), weight)
-    h1, g0 = fence(h1, g0)
+    h1 = [hidden_chunk((near, c1, y1, cy1), weight, 0, parts[0])]
+    h1[0], y1, g0 = fence(h1[0], y1, g0)
     g0 = exchange(g0)
-    out_far, mid, slot2, y2, c2, g1 = fence(out_far, mid, slot2, y2, c2, g1)
+    h1.append(hidden_chunk((near, c1, y1, cy1), weight, parts[0], parts[1]))
+    out_far, mid, slot2, y2, c2, h1[1], g1 = fence(out_far, mid, slot2, y2, c2, h1[1], g1)
 
     slot3 = jnp.where(edge, out_far, mid)
     y3 = across(slot3)
     c3, cy2 = core(slot3), core(y2)
     h2 = hidden_chunk((slot2, c2, y2, cy2), weight)
-    slot3, y3, c3, h2, g0, g1 = fence(slot3, y3, c3, h2, g0, g1)
+    slot3, y3, c3, h2, g1 = fence(slot3, y3, c3, h2, g1)
 
     cy3 = core(y3)
     g1 = exchange(g1)
     h3 = hidden_chunk((slot3, c3, y3, cy3), weight)
-    hiddens = (h0, h1, h2, h3)
     sums, start = None, 0
     for k, gates in enumerate((g0, g1)):
-        sums = project(hiddens, gates, proj, start, parts[k], sums, lengths if k == len(parts) - 1 else None)
+        sums = project((h0, h1[k], h2, h3), gates, proj, start, parts[k], sums, lengths if k == len(parts) - 1 else None)
         start += parts[k]
     return sums, g0[:, :, parts[0] :]
 

time: 210 us -> 208 us (level)
  Pallas kernels: 88.1 us -> 91.6 us
  starting transfers between devices: 40.3 us -> 38.1 us
    ppermute x17, waiting for transfers between devices: 37.1 us -> 30.9 us  [swap(): return lax.ppermute(block, AXIS, [(i, i ^ bit) for i in range(count)])]
    ppermute x5, waiting for transfers between devices: 16 us -> 20.8 us  [line(): lax.ppermute(block, AXIS, [(4 * a + i, 4 * b + i) for a, b in pairs for i...]
    pallas_call x4 -> x5, Pallas kernels: 66 us -> 69.5 us  [hidden_chunk(): pl.pallas_call(body, grid=(width // tile,), out_shape=jax.ShapeDtypeStruc...]
  transfers between devices with their start and end apart: 24 -> 24, of which waited for: 11 -> 13; matrix products, arithmetic and copies ran while one was open for 3% -> 3% of each run, Pallas kernels for 36% -> 38%
where the time goes in v5:
time: 208 us; the launch traced here: 207 us
  Pallas kernels  91.6 us (44%)
  waiting for transfers between devices  63.8 us (31%)
  starting transfers between devices  38.1 us (18%)
  local copies, waits for them, and re-layouts  7.29 us (4%)
  other arithmetic  4.46 us (2%)
    pallas_call x5, Pallas kernels, hidden_chunk(): pl.pallas_call(body, grid=(width // tile,), out_shape=jax.ShapeDtypeStruc...  69.5 us
    ppermute x17, waiting for transfers between devices, swap(): return lax.ppermute(block, AXIS, [(i, i ^ bit) for i in range(count)])  30.9 us
    ppermute x5, waiting for transfers between devices, line(): lax.ppermute(block, AXIS, [(4 * a + i, 4 * b + i) for a, b in pairs for i...  20.8 us
    ppermute x17, starting transfers between devices, swap(): return lax.ppermute(block, AXIS, [(i, i ^ bit) for i in range(count)])  16.9 us
    ppermute x5, starting transfers between devices, line(): lax.ppermute(block, AXIS, [(4 * a + i, 4 * b + i) for a, b in pairs for i...  12.2 us
    all_to_all x2, waiting for transfers between devices, exchange(): return lax.all_to_all(block, AXIS, split_axis=0, concat_axis=0, tiled=True)  12.1 us
    pallas_call x2, Pallas kernels, project(): pl.pallas_call(body, grid=(columns // tile,), out_shape=[jax.ShapeDtypeSt...  9.38 us
    all_to_all x2, starting transfers between devices, exchange(): return lax.all_to_all(block, AXIS, split_axis=0, concat_axis=0, tiled=True)  8.96 us
  transfers between devices with their start and end apart: 24, of which 13 were waited for; matrix products, arithmetic and copies ran while one was open for 3% of the time, Pallas kernels for 38%

profile of v5, /device:TPU:0, one launch (start us, length us, event | category | flops | bytes accessed | tf_op | source)
XLA Modules:
  0.0 207.1 jit_solution(7861529443222376434)
XLA Ops:
  0.0 3.0 %collective-permute-start = (bf16[56,8192]{1,0:T(8,128)(2,1)}, bf16[56,8192]{1,0:T(8,128)(2,1)S(1)}, u32[]{:S(2)}, u32[]{:S(2)}) collective-permute-start(bf16[56,8192]{1,0:T(8,128)(2,1)} %refs_0_.1), channel_id=1, source_target_pairs={{0,4},{1,5},{2,6},{3,7},{4,0},{5,1},{6,2},{7,3},{8,12},{9,13},{10,... | collective-permute-start | bytes 2752520 | tf_op jit(solution)/shard_map/ppermute | solution.py:26
  3.7 1.6 collective-permute-start.2
  5.3 1.6 reduce-precision_convert_fusion
  7.6 4.7 %by_device.1 = (bf16[16,56,896]{2,1,0:T(8,128)(2,1)}, bf16[16,56,1024]{2,1,0:T(8,128)(2,1)}) custom-call(bf16[56,28672]{1,0:T(8,128)(2,1)} %g.1, bf16[56,128]{1,0:T(8,128)(2,1)} %pad_maximum_fusion.own), custom_call_target="tpu_custom_call" | custom-call | flops 1 | bytes 1 | tf_op jit(solution)/shard_map/by_device/pallas_call | solution.py:64
  12.4 11.2 %collective-permute-done.refs_0_ = bf16[56,8192]{1,0:T(8,128)(2,1)S(1)} collective-permute-done((bf16[56,8192]{1,0:T(8,128)(2,1)}, bf16[56,8192]{1,0:T(8,128)(2,1)S(1)}, u32[]{:S(2)}, u32[]{:S(2)}) %collective-permute-start) | collective-permute-done | bytes 917536 | tf_op jit(solution)/shard_map/ppermute | solution.py:26
  23.6 2.3 %collective-permute-done.2.refs_2_ = bf16[56,8192]{1,0:T(8,128)(2,1)} collective-permute-done((bf16[56,8192]{1,0:T(8,128)(2,1)}, bf16[56,8192]{1,0:T(8,128)(2,1)}, u32[]{:S(2)}, u32[]{:S(2)}) %collective-permute-start.2) | collective-permute-done | bytes 917536 | tf_op jit(solution)/shard_map/ppermute | solution.py:22
  26.0 1.6 collective-permute-start.4
  27.6 1.5 collective-permute-start.6
  29.4 5.2 %collective-permute-start.5 = (bf16[56,8192]{1,0:T(8,128)(2,1)}, bf16[56,8192]{1,0:T(8,128)(2,1)S(1)}, u32[]{:S(2)}, u32[]{:S(2)}) collective-permute-start(bf16[56,8192]{1,0:T(8,128)(2,1)} %get-tuple-element.42.refs_3_), channel_id=1, source_target_pairs={{0,4},{1,5},{2,6},{3,7},{4,0},{5,1},{6,2},{7,3},{8,12},{9,13},{10,... | collective-permute-start | bytes 2752520 | tf_op jit(solution)/shard_map/ppermute | solution.py:26
  34.5 16.5 %hidden_chunk.5.refs_6_ = f32[256,1792]{1,0:T(8,128)} custom-call(bf16[56,8192]{1,0:T(8,128)(2,1)} %refs_0_.1, bf16[56,8192]{1,0:T(8,128)(2,1)} %get-tuple-element.43.refs_1_, bf16[56,8192]{1,0:T(8,128)(2,1)} %get-tuple-element.44.refs_2_, bf16[56,8192]{1,0:T(8,128)(2,1)} %collective-permute-done.8.refs_3_, bf16[1792,8192]{1,0:T(8,128)(2,1)} %refs_4_.9), custom_call_target="tpu_custom_call" | custom-call | flops 1 | bytes 1 | tf_op jit(solution)/shard_map/hidden_chunk/pallas_call | solution.py:94
  51.1 4.7 %collective-permute-done.5.refs_1_ = bf16[56,8192]{1,0:T(8,128)(2,1)S(1)} collective-permute-done((bf16[56,8192]{1,0:T(8,128)(2,1)}, bf16[56,8192]{1,0:T(8,128)(2,1)S(1)}, u32[]{:S(2)}, u32[]{:S(2)}) %collective-permute-start.5) | collective-permute-done | bytes 917536 | tf_op jit(solution)/shard_map/ppermute | solution.py:26
  58.8 1.7 collective-permute-start.9
  61.4 9.2 %hidden_chunk.6.refs_0_ = f32[256,768]{1,0:T(8,128)} custom-call(bf16[56,8192]{1,0:T(8,128)(2,1)} %get-tuple-element.51.refs_0_, bf16[56,8192]{1,0:T(8,128)(2,1)} %get-tuple-element.52.refs_1_, bf16[56,8192]{1,0:T(8,128)(2,1)} %get-tuple-element.53.refs_2_.refs_1_, bf16[56,8192]{1,0:T(8,128)(2,1)} %copy-done.14, bf16[1792,8192]{1,0:T(8,128)(2,1)} %refs_4_.9), custom_call_target="tpu_custom_call" | custom-call | flops 1 | bytes 1 | tf_op jit(solution)/shard_map/hidden_chunk/pallas_call | solution.py:94
  70.6 4.4 %all-to-all-start.1 = ((bf16[16,56,896]{2,1,0:T(8,128)(2,1)}), bf16[16,56,896]{2,1,0:T(8,128)(2,1)S(1)}, u32[]{:S(2)}, u32[]{:S(2)}) async-start(bf16[16,56,896]{2,1,0:T(8,128)(2,1)} %get-tuple-element.70), calls=%async_computation.1 | async-start | bytes 3211264 | tf_op jit(solution)/shard_map/all_to_all | solution.py:192
  75.0 10.7 %hidden_chunk.7.refs_5_ = f32[256,1024]{1,0:T(8,128)} custom-call(bf16[56,8192]{1,0:T(8,128)(2,1)} %get-tuple-element.51.refs_0_, bf16[56,8192]{1,0:T(8,128)(2,1)} %get-tuple-element.52.refs_1_, bf16[56,8192]{1,0:T(8,128)(2,1)} %get-tuple-element.55.refs_2_, bf16[56,8192]{1,0:T(8,128)(2,1)} %copy-done.14, bf16[1792,8192]{1,0:T(8,128)(2,1)} %refs_4_.9), custom_call_target="tpu_custom_call" | custom-call | flops 1 | bytes 1 | tf_op jit(solution)/shard_map/hidden_chunk/pallas_call | solution.py:94
  85.7 4.9 %collective-permute-done.9.refs_0_ = bf16[56,8192]{1,0:T(8,128)(2,1)} collective-permute-done((bf16[56,8192]{1,0:T(8,128)(2,1)}, bf16[56,8192]{1,0:T(8,128)(2,1)}, u32[]{:S(2)}, u32[]{:S(2)}) %collective-permute-start.9) | collective-permute-done | bytes 917536 | tf_op jit(solution)/shard_map/ppermute | solution.py:26
  90.6 1.3 broadcast_select_fusion.refs_0_
  94.2 16.5 %hidden_chunk.8.refs_3_ = f32[256,1792]{1,0:T(8,128)} custom-call(bf16[56,8192]{1,0:T(8,128)(2,1)} %get-tuple-element.60.refs_0_, bf16[56,8192]{1,0:T(8,128)(2,1)} %get-tuple-element.61.refs_1_, bf16[56,8192]{1,0:T(8,128)(2,1)} %get-tuple-element.62.refs_2_, bf16[56,8192]{1,0:T(8,128)(2,1)} %copy-done.15, bf16[1792,8192]{1,0:T(8,128)(2,1)} %refs_4_.9), custom_call_target="tpu_custom_call" | custom-call | flops 1 | bytes 1 | tf_op jit(solution)/shard_map/hidden_chunk/pallas_call | solution.py:94
  110.8 10.7 %collective-permute-done.13.refs_1_ = bf16[56,8192]{1,0:T(8,128)(2,1)S(1)} collective-permute-done((bf16[56,8192]{1,0:T(8,128)(2,1)S(1)}, bf16[56,8192]{1,0:T(8,128)(2,1)S(1)}, u32[]{:S(2)}, u32[]{:S(2)}) %collective-permute-start.13) | collective-permute-done | bytes 917536 | tf_op jit(solution)/shard_map/ppermute | solution.py:22
  124.5 4.6 %all-to-all-start = ((bf16[16,56,1024]{2,1,0:T(8,128)(2,1)}), bf16[16,56,1024]{2,1,0:T(8,128)(2,1)}, u32[]{:S(2)}, u32[]{:S(2)}) async-start(bf16[16,56,1024]{2,1,0:T(8,128)(2,1)} %get-tuple-element.68), calls=%async_computation | async-start | bytes 3670016 | tf_op jit(solution)/shard_map/all_to_all | solution.py:192
  129.8 1.9 collective-permute-done.16.refs_3_
  132.6 16.5 %hidden_chunk.9.refs_3_ = f32[256,1792]{1,0:T(8,128)} custom-call(bf16[56,8192]{1,0:T(8,128)(2,1)} %get-tuple-element.65.refs_0_, bf16[56,8192]{1,0:T(8,128)(2,1)} %get-tuple-element.66.refs_1_, bf16[56,8192]{1,0:T(8,128)(2,1)} %get-tuple-element.67.refs_2_, bf16[56,8192]{1,0:T(8,128)(2,1)} %copy-done.16, bf16[1792,8192]{1,0:T(8,128)(2,1)} %refs_4_.9), custom_call_target="tpu_custom_call" | custom-call | flops 1 | bytes 1 | tf_op jit(solution)/shard_map/hidden_chunk/pallas_call | solution.py:94
  149.1 4.2 %project.2.refs_6_ = f32[1024,64]{1,0:T(8,128)} custom-call(f32[256,1792]{1,0:T(8,128)} %get-tuple-element.47.refs_0_, f32[256,768]{1,0:T(8,128)} %get-tuple-element.69.refs_1_, f32[256,1792]{1,0:T(8,128)} %get-tuple-element.64.refs_2_, f32[256,1792]{1,0:T(8,128)} %hidden_chunk.9.refs_3_, bf16[16,56,896]{2,1,0:T(8,128)(2,1)} %copy-done.9, ...), custom_call_target="tpu_custom_call" | custom-call | flops 1 | bytes 1 | tf_op jit(solution)/shard_map/project/pallas_call | solution.py:154
  153.3 12.1 %all-to-all-done.refs_4_ = bf16[16,56,1024]{2,1,0:T(8,128)(2,1)} async-done(((bf16[16,56,1024]{2,1,0:T(8,128)(2,1)}), bf16[16,56,1024]{2,1,0:T(8,128)(2,1)}, u32[]{:S(2)}, u32[]{:S(2)}) %all-to-all-start) | async-done | bytes 1835040 | tf_op jit(solution)/shard_map/all_to_all | solution.py:192
  165.5 5.2 %project.3 = (f32[16,16,128]{2,1,0:T(8,128)}, f32[16,16,128]{2,1,0:T(8,128)}) custom-call(f32[256,1792]{1,0:T(8,128)} %get-tuple-element.47.refs_0_, f32[256,1024]{1,0:T(8,128)} %get-tuple-element.57.refs_1_, f32[256,1792]{1,0:T(8,128)} %get-tuple-element.64.refs_2_, f32[256,1792]{1,0:T(8,128)} %hidden_chunk.9.refs_3_, ...), custom_call_target="tpu_custom_call" | custom-call | flops 1 | bytes 1 | tf_op jit(solution)/shard_map/project/pallas_call | solution.py:154
  173.5 3.1 %collective-permute-start.18 = (f32[16,16,128]{2,1,0:T(8,128)S(1)}, f32[16,16,128]{2,1,0:T(8,128)S(1)}, u32[]{:S(2)}, u32[]{:S(2)}) collective-permute-start(f32[16,16,128]{2,1,0:T(8,128)S(1)} %add.20), channel_id=1, source_target_pairs={{0,2},{1,3},{2,0},{3,1},{4,6},{5,7},{6,4},{7,5},{8,10},{9,11},{10,... | collective-permute-start | bytes 393224 | tf_op jit(solution)/shard_map/ppermute | solution.py:22
  176.6 4.0 %collective-permute-done.18 = f32[16,16,128]{2,1,0:T(8,128)S(1)} collective-permute-done((f32[16,16,128]{2,1,0:T(8,128)S(1)}, f32[16,16,128]{2,1,0:T(8,128)S(1)}, u32[]{:S(2)}, u32[]{:S(2)}) %collective-permute-start.18) | collective-permute-done | bytes 131104 | tf_op jit(solution)/shard_map/ppermute | solution.py:22
  180.7 5.1 %collective-permute-start.19 = (f32[16,16,128]{2,1,0:T(8,128)S(1)}, f32[16,16,128]{2,1,0:T(8,128)S(1)}, u32[]{:S(2)}, u32[]{:S(2)}) collective-permute-start(f32[16,16,128]{2,1,0:T(8,128)S(1)} %add.21), channel_id=1, source_target_pairs={{0,4},{1,5},{2,6},{3,7},{4,0},{5,1},{6,2},{7,3},{8,12},{9,13},{10,... | collective-permute-start | bytes 393224 | tf_op jit(solution)/shard_map/ppermute | solution.py:22
  185.7 3.5 %collective-permute-done.19 = f32[16,16,128]{2,1,0:T(8,128)S(1)} collective-permute-done((f32[16,16,128]{2,1,0:T(8,128)S(1)}, f32[16,16,128]{2,1,0:T(8,128)S(1)}, u32[]{:S(2)}, u32[]{:S(2)}) %collective-permute-start.19) | collective-permute-done | bytes 131104 | tf_op jit(solution)/shard_map/ppermute | solution.py:22
  189.2 3.0 %collective-permute-start.20 = (f32[16,16,128]{2,1,0:T(8,128)S(1)}, f32[16,16,128]{2,1,0:T(8,128)S(1)}, u32[]{:S(2)}, u32[]{:S(2)}) collective-permute-start(f32[16,16,128]{2,1,0:T(8,128)S(1)} %add.22), channel_id=1, source_target_pairs={{0,8},{1,9},{2,10},{3,11},{4,12},{5,13},{6,14},{7,15},{8,0},{9,1},... | collective-permute-start | bytes 393224 | tf_op jit(solution)/shard_map/ppermute | solution.py:22
  192.2 5.4 %collective-permute-done.20 = f32[16,16,128]{2,1,0:T(8,128)S(1)} collective-permute-done((f32[16,16,128]{2,1,0:T(8,128)S(1)}, f32[16,16,128]{2,1,0:T(8,128)S(1)}, u32[]{:S(2)}, u32[]{:S(2)}) %collective-permute-start.20) | collective-permute-done | bytes 131104 | tf_op jit(solution)/shard_map/ppermute | solution.py:22
  199.1 8.0 %finish.1 = f32[64,128]{1,0:T(8,128)} custom-call(f32[16,16,128]{2,1,0:T(8,128)S(1)} %add.23.own, f32[16,16,128]{2,1,0:T(8,128)S(1)} %collective-permute-done.21.other, f32[16,64,64]{2,1,0:T(8,128)S(1)} %slice_add_fusion.i, f32[128,4096]{1,0:T(8,128)S(1)} %copy-done.2), custom_call_target="tpu_custom_call" | custom-call | tf_op jit(solution)/shard_map/finish/pallas_call | solution.py:306
  (80 shorter events, 17.0 us)
Async XLA Ops:
  0.0 5.3 %copy-start = (bf16[64,8192]{1,0:T(8,128)(2,1)S(1)}, bf16[64,8192]{1,0:T(8,128)(2,1)}, u32[]{:S(2)}) copy-start(bf16[64,8192]{1,0:T(8,128)(2,1)} %param.12) | copy-start | bytes 3145732
  0.0 23.6 %collective-permute-start = (bf16[56,8192]{1,0:T(8,128)(2,1)}, bf16[56,8192]{1,0:T(8,128)(2,1)S(1)}, u32[]{:S(2)}, u32[]{:S(2)}) collective-permute-start(bf16[56,8192]{1,0:T(8,128)(2,1)} %refs_0_.1), channel_id=1, source_target_pairs={{0,4},{1,5},{2,6},{3,7},{4,0},{5,1},{6,2},{7,3},{8,12},{9,13},{10,... | collective-permute-start | bytes 2752520 | tf_op jit(solution)/shard_map/ppermute | solution.py:26
  3.0 20.6 %collective-permute-start.1 = (bf16[56,8192]{1,0:T(8,128)(2,1)}, bf16[56,8192]{1,0:T(8,128)(2,1)S(1)}, u32[]{:S(2)}, u32[]{:S(2)}) collective-permute-start(bf16[56,8192]{1,0:T(8,128)(2,1)} %refs_0_.1), channel_id=1, source_target_pairs={{4,8},{5,9},{6,10},{7,11},{8,4},{9,5},{10,6},{11,7},{20,24},{21,25... | collective-permute-start | bytes 2752520 | tf_op jit(solution)/shard_map/ppermute | solution.py:26
  3.7 22.2 %collective-permute-start.2 = (bf16[56,8192]{1,0:T(8,128)(2,1)}, bf16[56,8192]{1,0:T(8,128)(2,1)}, u32[]{:S(2)}, u32[]{:S(2)}) collective-permute-start(bf16[56,8192]{1,0:T(8,128)(2,1)} %refs_0_.1), channel_id=1, source_target_pairs={{0,2},{1,3},{2,0},{3,1},{4,6},{5,7},{6,4},{7,5},{8,10},{9,11},{10,... | collective-permute-start | bytes 2752520 | tf_op jit(solution)/shard_map/ppermute | solution.py:22
  5.3 20.6 %collective-permute-start.3 = (bf16[56,8192]{1,0:T(8,128)(2,1)}, bf16[56,8192]{1,0:T(8,128)(2,1)}, u32[]{:S(2)}, u32[]{:S(2)}) collective-permute-start(bf16[56,8192]{1,0:T(8,128)(2,1)} %refs_0_.1), channel_id=1, source_target_pairs={{0,1},{1,0},{2,3},{3,2},{4,5},{5,4},{6,7},{7,6},{8,9},{9,8},{10,11... | collective-permute-start | bytes 2752520 | tf_op jit(solution)/shard_map/ppermute | solution.py:22
  26.0 8.6 %collective-permute-start.8 = (bf16[56,8192]{1,0:T(8,128)(2,1)}, bf16[56,8192]{1,0:T(8,128)(2,1)}, u32[]{:S(2)}, u32[]{:S(2)}) collective-permute-start(bf16[56,8192]{1,0:T(8,128)(2,1)} %get-tuple-element.44.refs_2_), channel_id=1, source_target_pairs={{0,1},{1,0},{2,3},{3,2},{4,5},{5,4},{6,7},{7,6},{8,9},{9,8},{10,11... | collective-permute-start | bytes 2752520 | tf_op jit(solution)/shard_map/ppermute | solution.py:22
  26.0 25.0 %collective-permute-start.4 = (bf16[56,8192]{1,0:T(8,128)(2,1)}, bf16[56,8192]{1,0:T(8,128)(2,1)}, u32[]{:S(2)}, u32[]{:S(2)}) collective-permute-start(bf16[56,8192]{1,0:T(8,128)(2,1)} %get-tuple-element.41.refs_2_), channel_id=1, source_target_pairs={{4,8},{5,9},{6,10},{7,11},{8,4},{9,5},{10,6},{11,7},{20,24},{21,25... | collective-permute-start | bytes 2752520 | tf_op jit(solution)/shard_map/ppermute | solution.py:26
  27.6 23.4 %collective-permute-start.6 = (bf16[56,8192]{1,0:T(8,128)(2,1)}, bf16[56,8192]{1,0:T(8,128)(2,1)S(1)}, u32[]{:S(2)}, u32[]{:S(2)}) collective-permute-start(bf16[56,8192]{1,0:T(8,128)(2,1)} %get-tuple-element.41.refs_2_), channel_id=1, source_target_pairs={{0,2},{1,3},{2,0},{3,1},{4,6},{5,7},{6,4},{7,5},{8,10},{9,11},{10,... | collective-permute-start | bytes 2752520 | tf_op jit(solution)/shard_map/ppermute | solution.py:22
  29.2 21.9 %collective-permute-start.7 = (bf16[56,8192]{1,0:T(8,128)(2,1)}, bf16[56,8192]{1,0:T(8,128)(2,1)S(1)}, u32[]{:S(2)}, u32[]{:S(2)}) collective-permute-start(bf16[56,8192]{1,0:T(8,128)(2,1)} %get-tuple-element.41.refs_2_), channel_id=1, source_target_pairs={{0,1},{1,0},{2,3},{3,2},{4,5},{5,4},{6,7},{7,6},{8,9},{9,8},{10,11... | collective-permute-start | bytes 2752520 | tf_op jit(solution)/shard_map/ppermute | solution.py:22
  29.4 26.4 %collective-permute-start.5 = (bf16[56,8192]{1,0:T(8,128)(2,1)}, bf16[56,8192]{1,0:T(8,128)(2,1)S(1)}, u32[]{:S(2)}, u32[]{:S(2)}) collective-permute-start(bf16[56,8192]{1,0:T(8,128)(2,1)} %get-tuple-element.42.refs_3_), channel_id=1, source_target_pairs={{0,4},{1,5},{2,6},{3,7},{4,0},{5,1},{6,2},{7,3},{8,12},{9,13},{10,... | collective-permute-start | bytes 2752520 | tf_op jit(solution)/shard_map/ppermute | solution.py:26
  56.7 3.8 %collective-permute-start.12 = (bf16[56,8192]{1,0:T(8,128)(2,1)}, bf16[56,8192]{1,0:T(8,128)(2,1)S(1)}, u32[]{:S(2)}, u32[]{:S(2)}) collective-permute-start(bf16[56,8192]{1,0:T(8,128)(2,1)} %get-tuple-element.53.refs_2_.refs_1_), channel_id=1, source_target_pairs={{0,1},{1,0},{2,3},{3,2},{4,5},{5,4},{6,7},{7,6},{8,9},{9,8},{10,11... | collective-permute-start | bytes 2752520 | tf_op jit(solution)/shard_map/ppermute | solution.py:22
  58.0 12.7 %copy-start.6 = (bf16[56,8192]{1,0:T(8,128)(2,1)}, bf16[56,8192]{1,0:T(8,128)(2,1)S(1)}, u32[]{:S(2)}) copy-start(bf16[56,8192]{1,0:T(8,128)(2,1)S(1)} %broadcast_select_fusion.1.refs_2_) | copy-start | bytes 2752516
  58.0 27.8 %collective-permute-start.10 = (bf16[56,8192]{1,0:T(8,128)(2,1)S(1)}, bf16[56,8192]{1,0:T(8,128)(2,1)}, u32[]{:S(2)}, u32[]{:S(2)}) collective-permute-start(bf16[56,8192]{1,0:T(8,128)(2,1)S(1)} %broadcast_select_fusion.1.refs_2_), channel_id=1, source_target_pairs={{0,2},{1,3},{2,0},{3,1},{4,6},{5,7},{6,4},{7,5},{8,10},{9,11},{10,... | collective-permute-start | bytes 2752520 | tf_op jit(solution)/shard_map/ppermute | solution.py:22
  58.5 27.2 %collective-permute-start.11 = (bf16[56,8192]{1,0:T(8,128)(2,1)S(1)}, bf16[56,8192]{1,0:T(8,128)(2,1)}, u32[]{:S(2)}, u32[]{:S(2)}) collective-permute-start(bf16[56,8192]{1,0:T(8,128)(2,1)S(1)} %broadcast_select_fusion.1.refs_2_), channel_id=1, source_target_pairs={{0,1},{1,0},{2,3},{3,2},{4,5},{5,4},{6,7},{7,6},{8,9},{9,8},{10,11... | collective-permute-start | bytes 2752520 | tf_op jit(solution)/shard_map/ppermute | solution.py:22
  58.8 31.9 %collective-permute-start.9 = (bf16[56,8192]{1,0:T(8,128)(2,1)}, bf16[56,8192]{1,0:T(8,128)(2,1)}, u32[]{:S(2)}, u32[]{:S(2)}) collective-permute-start(bf16[56,8192]{1,0:T(8,128)(2,1)} %get-tuple-element.48), channel_id=1, source_target_pairs={{0,4},{1,5},{2,6},{3,7},{4,0},{5,1},{6,2},{7,3},{8,12},{9,13},{10,... | collective-permute-start | bytes 2752520 | tf_op jit(solution)/shard_map/ppermute | solution.py:26
  70.6 52.7 %all-to-all-start.1 = ((bf16[16,56,896]{2,1,0:T(8,128)(2,1)}), bf16[16,56,896]{2,1,0:T(8,128)(2,1)S(1)}, u32[]{:S(2)}, u32[]{:S(2)}) async-start(bf16[16,56,896]{2,1,0:T(8,128)(2,1)} %get-tuple-element.70), calls=%async_computation.1 | async-start | bytes 3211264 | tf_op jit(solution)/shard_map/all_to_all | solution.py:192
  90.6 2.7 %collective-permute-start.15 = (bf16[56,8192]{1,0:T(8,128)(2,1)}, bf16[56,8192]{1,0:T(8,128)(2,1)S(1)}, u32[]{:S(2)}, u32[]{:S(2)}) collective-permute-start(bf16[56,8192]{1,0:T(8,128)(2,1)} %get-tuple-element.62.refs_2_), channel_id=1, source_target_pairs={{0,1},{1,0},{2,3},{3,2},{4,5},{5,4},{6,7},{7,6},{8,9},{9,8},{10,11... | collective-permute-start | bytes 2752520 | tf_op jit(solution)/shard_map/ppermute | solution.py:22
  91.9 18.9 %copy-start.7 = (bf16[56,8192]{1,0:T(8,128)(2,1)}, bf16[56,8192]{1,0:T(8,128)(2,1)S(1)}, u32[]{:S(2)}) copy-start(bf16[56,8192]{1,0:T(8,128)(2,1)S(1)} %broadcast_select_fusion.refs_0_) | copy-start | bytes 2752516
  91.9 29.6 %collective-permute-start.13 = (bf16[56,8192]{1,0:T(8,128)(2,1)S(1)}, bf16[56,8192]{1,0:T(8,128)(2,1)S(1)}, u32[]{:S(2)}, u32[]{:S(2)}) collective-permute-start(bf16[56,8192]{1,0:T(8,128)(2,1)S(1)} %broadcast_select_fusion.refs_0_), channel_id=1, source_target_pairs={{0,2},{1,3},{2,0},{3,1},{4,6},{5,7},{6,4},{7,5},{8,10},{9,11},{10,... | collective-permute-start | bytes 2752520 | tf_op jit(solution)/shard_map/ppermute | solution.py:22
  92.0 29.5 %collective-permute-start.14 = (bf16[56,8192]{1,0:T(8,128)(2,1)S(1)}, bf16[56,8192]{1,0:T(8,128)(2,1)S(1)}, u32[]{:S(2)}, u32[]{:S(2)}) collective-permute-start(bf16[56,8192]{1,0:T(8,128)(2,1)S(1)} %broadcast_select_fusion.refs_0_), channel_id=1, source_target_pairs={{0,1},{1,0},{2,3},{3,2},{4,5},{5,4},{6,7},{7,6},{8,9},{9,8},{10,11... | collective-permute-start | bytes 2752520 | tf_op jit(solution)/shard_map/ppermute | solution.py:22
  123.4 5.8 %copy-start.11 = (bf16[56,8192]{1,0:T(8,128)(2,1)S(1)}, bf16[56,8192]{1,0:T(8,128)(2,1)}, u32[]{:S(2)}) copy-start(bf16[56,8192]{1,0:T(8,128)(2,1)} %get-tuple-element.67.refs_2_) | copy-start | bytes 2752516
  123.4 5.9 %copy-start.17 = (s32[1,4]{1,0:T(1,128)S(1)}, s32[1,4]{1,0:T(1,128)}, u32[]{:S(2)}) copy-start(s32[1,4]{1,0:T(1,128)} %param.14) | copy-start | bytes 52
  124.5 41.0 %all-to-all-start = ((bf16[16,56,1024]{2,1,0:T(8,128)(2,1)}), bf16[16,56,1024]{2,1,0:T(8,128)(2,1)}, u32[]{:S(2)}, u32[]{:S(2)}) async-start(bf16[16,56,1024]{2,1,0:T(8,128)(2,1)} %get-tuple-element.68), calls=%async_computation | async-start | bytes 3670016 | tf_op jit(solution)/shard_map/all_to_all | solution.py:192
  129.1 2.5 %collective-permute-start.16 = (bf16[56,8192]{1,0:T(8,128)(2,1)S(1)}, bf16[56,8192]{1,0:T(8,128)(2,1)S(1)}, u32[]{:S(2)}, u32[]{:S(2)}) collective-permute-start(bf16[56,8192]{1,0:T(8,128)(2,1)S(1)} %copy-done.11), channel_id=1, source_target_pairs={{0,1},{1,0},{2,3},{3,2},{4,5},{5,4},{6,7},{7,6},{8,9},{9,8},{10,11... | collective-permute-start | bytes 2752520 | tf_op jit(solution)/shard_map/ppermute | solution.py:22
  165.5 26.7 %slice-start = ((bf16[16,56,896]{2,1,0:T(8,128)(2,1)}), bf16[16,56,128]{2,1,0:T(8,128)(2,1)S(1)}, s32[]{:S(2)}) async-start(bf16[16,56,896]{2,1,0:T(8,128)(2,1)} %copy-done.9), calls=%async_computation.2 | async-start | bytes 458752 | tf_op jit(solution)/shard_map/slice | solution.py:225
  170.6 2.0 collective-permute-start.17
  173.5 7.1 %collective-permute-start.18 = (f32[16,16,128]{2,1,0:T(8,128)S(1)}, f32[16,16,128]{2,1,0:T(8,128)S(1)}, u32[]{:S(2)}, u32[]{:S(2)}) collective-permute-start(f32[16,16,128]{2,1,0:T(8,128)S(1)} %add.20), channel_id=1, source_target_pairs={{0,2},{1,3},{2,0},{3,1},{4,6},{5,7},{6,4},{7,5},{8,10},{9,11},{10,... | collective-permute-start | bytes 393224 | tf_op jit(solution)/shard_map/ppermute | solution.py:22
  180.7 18.4 %copy-start.2 = (f32[128,4096]{1,0:T(8,128)S(1)}, f32[128,4096]{1,0:T(8,128)}, u32[]{:S(2)}) copy-start(f32[128,4096]{1,0:T(8,128)} %q.1) | copy-start | bytes 6291460
  180.7 8.5 %collective-permute-start.19 = (f32[16,16,128]{2,1,0:T(8,128)S(1)}, f32[16,16,128]{2,1,0:T(8,128)S(1)}, u32[]{:S(2)}, u32[]{:S(2)}) collective-permute-start(f32[16,16,128]{2,1,0:T(8,128)S(1)} %add.21), channel_id=1, source_target_pairs={{0,4},{1,5},{2,6},{3,7},{4,0},{5,1},{6,2},{7,3},{8,12},{9,13},{10,... | collective-permute-start | bytes 393224 | tf_op jit(solution)/shard_map/ppermute | solution.py:22
  189.2 8.4 %collective-permute-start.20 = (f32[16,16,128]{2,1,0:T(8,128)S(1)}, f32[16,16,128]{2,1,0:T(8,128)S(1)}, u32[]{:S(2)}, u32[]{:S(2)}) collective-permute-start(f32[16,16,128]{2,1,0:T(8,128)S(1)} %add.22), channel_id=1, source_target_pairs={{0,8},{1,9},{2,10},{3,11},{4,12},{5,13},{6,14},{7,15},{8,0},{9,1},... | collective-permute-start | bytes 393224 | tf_op jit(solution)/shard_map/ppermute | solution.py:22
  197.7 1.4 collective-permute-start.21
  197.7 9.4 %copy-start.1 = (bf16[64,8192]{1,0:T(8,128)(2,1)S(1)}, bf16[64,8192]{1,0:T(8,128)(2,1)}, u32[]{:S(2)}) copy-start(bf16[64,8192]{1,0:T(8,128)(2,1)} %param.12) | copy-start | bytes 3145732
  (11 other events, 20.9 us)
